TPU v7x, 512 devices: a whole 4x4x16 slice. The times are simulated.
512 devices in a mesh: ctx: 64 (over x_hi, z, core), tp: 8 (over y, x_lo).
Axes of the slice: x: 4 (x_hi: 2, x_lo: 2; x = x_hi * 2 + x_lo), y: 4, z: 16, core: 2. Of those that a mesh axis runs over, the one named last changes fastest.
Arguments:
- queries: bfloat16 [14336, 5120], P('ctx', 'tp'), may hold values from -8 to 8
- keys: bfloat16 [14336, 1024], P('ctx', 'tp'), may hold values from -8 to 8
- values: bfloat16 [14336, 1024], P('ctx', 'tp'), may hold values from -6 to 6
- doc_lengths: int32 [16], replicated, may hold values from 1 to 7168, 14336 in all
- out_weight: bfloat16 [40, 128, 5120], P('tp', 'ctx'), may hold values from -0.83984375 to 0.83984375
Outputs:
- attended: float32 [14336, 5120], P('ctx', 'tp')
- projected: float32 [14336, 5120], P('ctx', 'tp')
Inputs may be any that keep to these rules, and one draw needn't show every extreme that they name: `doc_lengths`: the 16 lengths sum to 14336; the longest document has exactly 7168 positions.
All inputs are finite; a program needn't handle non-finite values.
Results may differ from a plain program's by a relative error of at most 0.017.
Values may be sent and summed in bfloat16 or wider, within the bound.
No kernel may reach another device: no remote copies, remote signals or barrier semaphores. Data moves between devices by JAX's collectives and lax.ppermute only.
A program may use at most 64 MiB of HBM per device.

v0:
```python
import functools
import math

import jax
import jax.numpy as jnp
from jax import lax
from jax.experimental import pallas as pl
from jax.experimental.pallas import tpu as pltpu
from jax.sharding import Mesh, PartitionSpec as P

HD = 128
XH, NZ, NC, NY, NX = 2, 16, 2, 4, 2
ROWS = 224
QROWS = NC * ROWS
HEADS = 5
WIDE = HEADS * HD
STATE = WIDE + 16
DEEP = 2 * HD
FLOOR = -1e29
MASKED = -1e30
NEG = (((1,), (1,)), ((), ()))
VMEM = 40 * 1024 * 1024
F32 = jnp.float32
BF16 = jnp.bfloat16


def attend_kernel(visits, first, here_ref, len_ref, q_ref, *refs):
    held, starts, state = refs[-2], refs[-1], refs[-3]
    if first:
        state[:WIDE] = jnp.zeros((WIDE, QROWS), F32)
        state[WIDE : WIDE + 8] = jnp.full((8, QROWS), FLOOR, F32)
        state[WIDE + 8 :] = jnp.zeros((8, QROWS), F32)
    else:
        state[...] = refs[-4][...]
    z, core, xh = here_ref[0], here_ref[1], here_ref[2]
    q_start = (xh * NZ + z) * QROWS
    q_last = q_start + QROWS - 1
    q_pos = q_start + lax.broadcasted_iota(jnp.int32, (1, QROWS), 1)
    doc_start = jnp.zeros((1, QROWS), jnp.int32)
    low, high, end = jnp.int32(0), jnp.int32(0), jnp.int32(0)
    for i in range(len_ref.shape[0]):
        end = end + len_ref[i]
        doc_start = jnp.where(q_pos >= end, end, doc_start)
        low = jnp.where(q_start >= end, end, low)
        high = jnp.where(q_last >= end, end, high)
    scale = math.log2(math.e) / math.sqrt(HD)

    def visit(slot, k_start, partial):
        keys = held[slot, :ROWS]
        values = held[slot, ROWS:].T
        if partial:
            k_pos = k_start + lax.broadcasted_iota(jnp.int32, (ROWS, QROWS), 0)
            allowed = (k_pos >= doc_start) & (k_pos <= q_pos)
        for h in range(HEADS):
            rows = slice(h * HD, (h + 1) * HD)
            scores = scale * lax.dot_general(keys, q_ref[:, rows], NEG, preferred_element_type=F32)
            if partial:
                scores = jnp.where(allowed, scores, MASKED)
            old = state[WIDE + h : WIDE + h + 1]
            new = jnp.maximum(old, jnp.max(scores, axis=0, keepdims=True))
            fix = jnp.exp2(old - new)
            weights = jnp.exp2(scores - new)
            state[WIDE + h : WIDE + h + 1] = new
            total = slice(WIDE + 8 + h, WIDE + 9 + h)
            state[total] = state[total] * fix + jnp.sum(weights, axis=0, keepdims=True)
            mixed = jnp.dot(values, weights.astype(BF16), preferred_element_type=F32)
            state[rows] = state[rows] * fix + mixed

    count = jnp.int32(0)
    for operand, block, offset, other in visits:
        plane = xh ^ 1 if other else xh
        k_start = (plane * NZ + ((z + NZ - offset) & (NZ - 1))) * QROWS + core * ROWS
        needed = (k_start + ROWS > low) & (k_start <= q_last)

        @pl.when(needed)
        def _():
            held[count] = refs[operand][block * QROWS : (block + 1) * QROWS]
            starts[count] = k_start

        count = count + needed.astype(jnp.int32)

    @pl.loop(0, count)
    def _(slot):
        k_start = starts[slot]
        whole = (k_start >= high) & (k_start + ROWS <= q_start + 1)
        pl.when(whole)(functools.partial(visit, slot, k_start, False))
        pl.when(jnp.logical_not(whole))(functools.partial(visit, slot, k_start, True))


def attend(here, lengths, q, visits, operands, state):
    smem = pl.BlockSpec(memory_space=pltpu.SMEM)
    vmem = pl.BlockSpec(memory_space=pltpu.VMEM)
    specs = [smem, smem, vmem] + [vmem] * len(operands)
    aliases = {}
    if state is not None:
        aliases = {len(specs): 0}
        operands = operands + [state]
        specs = specs + [vmem]
    pairs = (len(visits) + 1) // 2 * QROWS * ROWS * HEADS
    return pl.pallas_call(
        functools.partial(attend_kernel, visits, state is None),
        out_shape=jax.ShapeDtypeStruct((STATE, QROWS), F32),
        in_specs=specs,
        out_specs=vmem,
        scratch_shapes=[
            pltpu.VMEM((len(visits), QROWS, HD), BF16),
            pltpu.SMEM((len(visits),), jnp.int32),
        ],
        input_output_aliases=aliases,
        cost_estimate=pl.CostEstimate(
            flops=pairs * HD * 8, bytes_accessed=STATE * QROWS * 8, transcendentals=pairs
        ),
        compiler_params=pltpu.CompilerParams(vmem_limit_bytes=VMEM),
    )(here, lengths, q, *operands)


def merge_kernel(here_ref, mine_ref, other_ref, out_ref, a_ref, full):
    for h in range(HEADS):
        rows = slice(h * HD, (h + 1) * HD)
        top = slice(WIDE + h, WIDE + h + 1)
        total = slice(WIDE + 8 + h, WIDE + 9 + h)
        m = jnp.maximum(mine_ref[top], other_ref[top])
        mine, other = jnp.exp2(mine_ref[top] - m), jnp.exp2(other_ref[top] - m)
        den = mine * mine_ref[total] + other * other_ref[total]
        mixed = (mine_ref[rows] * mine + other_ref[rows] * other) / den
        full[:, rows] = mixed.T
    own = full[pl.ds(pl.multiple_of(here_ref[1] * ROWS, ROWS), ROWS)]
    out_ref[...] = own
    a_ref[...] = own.astype(BF16)


def merge(here, mine, other):
    vmem = pl.BlockSpec(memory_space=pltpu.VMEM)
    return pl.pallas_call(
        merge_kernel,
        out_shape=(
            jax.ShapeDtypeStruct((ROWS, WIDE), F32),
            jax.ShapeDtypeStruct((ROWS, WIDE), BF16),
        ),
        in_specs=[pl.BlockSpec(memory_space=pltpu.SMEM), vmem, vmem],
        out_specs=(vmem, vmem),
        scratch_shapes=[pltpu.VMEM((QROWS, WIDE), F32)],
        cost_estimate=pl.CostEstimate(
            flops=QROWS * WIDE * 100, bytes_accessed=STATE * QROWS * 12, transcendentals=QROWS * 16
        ),
        compiler_params=pltpu.CompilerParams(vmem_limit_bytes=VMEM),
    )(here, mine, other)


def project_kernel(first, here_ref, near_ref, far_ref, own_ref, other_ref, *refs):
    core, xh, xl = here_ref[2], here_ref[3], here_ref[4]
    k = lax.broadcasted_iota(jnp.int32, (DEEP, DEEP), 0)
    g = lax.broadcasted_iota(jnp.int32, (DEEP, DEEP), 1)
    source_core = core ^ (g >> 7)
    row = g & (HD - 1)
    d = (xh ^ ((row >> 1) & 1)) * (NZ * 4) + (row >> 3) * 4 + source_core * 2 + (row & 1)
    source_x = xl ^ (k >> 7)
    match = ((k & (HD - 1)) == d) & (((row >> 2) & 1) == source_x)
    perm = jnp.where(match, 1.0, 0.0).astype(BF16)
    total = jnp.zeros((ROWS, WIDE), F32) if first else refs[0][...]
    for h in range(HEADS):
        heads = slice(h * HD, (h + 1) * HD)
        columns = slice(h * WIDE, (h + 1) * WIDE)
        both = jnp.concatenate([near_ref[:, heads], far_ref[:, heads]], axis=1)
        moved = jnp.dot(both, perm, preferred_element_type=F32).astype(BF16)
        weight = jnp.concatenate([own_ref[:, columns], other_ref[:, columns]], axis=0)
        total += jnp.dot(moved, weight, preferred_element_type=F32)
    refs[-1][...] = total


def project(where, near, far, weights, total):
    block = pl.BlockSpec((ROWS, WIDE), lambda i, w: (0, 0))
    weight = pl.BlockSpec((HD, HEADS * WIDE), lambda i, w: (0, w[0]))
    totals = [] if total is None else [total]
    return pl.pallas_call(
        functools.partial(project_kernel, total is None),
        grid_spec=pltpu.PrefetchScalarGridSpec(
            num_scalar_prefetch=1,
            grid=(1,),
            in_specs=[block, block, weight, weight] + [block] * len(totals),
            out_specs=block,
        ),
        out_shape=jax.ShapeDtypeStruct((ROWS, WIDE), F32),
        cost_estimate=pl.CostEstimate(
            flops=2 * ROWS * DEEP * HEADS * (WIDE + DEEP),
            bytes_accessed=DEEP * HEADS * WIDE * 2,
            transcendentals=0,
        ),
        compiler_params=pltpu.CompilerParams(vmem_limit_bytes=VMEM),
    )(where, near, far, *weights, *totals)


def swap(value, axis):
    return lax.ppermute(value, axis, [(0, 1), (1, 0)])


def ring(value, steps):
    return lax.ppermute(value, "z", [(i, (i + steps) % NZ) for i in range(NZ)])


def hop(block, dy, dx):
    perm = [
        (sy * NX + sx, (sy + dy) % NY * NX + (sx ^ dx)) for sy in range(NY) for sx in range(NX)
    ]
    return lax.ppermute(block, "tp", perm)


def split_kernel(after_ref, weight_ref, out_ref):
    for j in range(NY * NX):
        for h in range(HEADS):
            out_ref[j, :, h * WIDE : (h + 1) * WIDE] = weight_ref[h, :, j * WIDE : (j + 1) * WIDE]


def stack_kernel(mine_ref, other_ref, out_ref):
    for e in range(NX):
        for rel, ref in enumerate((mine_ref, other_ref)):
            row = e * 4 + rel * 2
            for y in range(NY):
                lanes = slice(y * HEADS * WIDE, (y + 1) * HEADS * WIDE)
                out_ref[row : row + 2, lanes] = ref[y * NX + e]


def pass_kernel(across_ref, below_ref, weight_ref, out_ref):
    pass


def gather_weight(out_weight, after):
    whole = pl.BlockSpec(memory_space=pl.ANY)
    vmem = pl.BlockSpec(memory_space=pltpu.VMEM)
    split = pl.pallas_call(
        split_kernel,
        out_shape=jax.ShapeDtypeStruct((NY * NX, 2, HEADS * WIDE), BF16),
        in_specs=[whole, vmem],
        out_specs=vmem,
    )(after, out_weight)
    split = lax.all_to_all(split, "tp", 0, 0)
    rows = pl.pallas_call(
        stack_kernel,
        out_shape=jax.ShapeDtypeStruct((8, NY * HEADS * WIDE), BF16),
        in_specs=[vmem, vmem],
        out_specs=vmem,
    )(split, swap(split, "xh"))
    return lax.all_gather(rows, "z", axis=0, tiled=True)


def exchange_weight(own, across, below):
    whole = pl.BlockSpec(memory_space=pl.ANY)
    hbm = pl.BlockSpec(memory_space=pltpu.HBM)
    own = pl.pallas_call(
        pass_kernel,
        out_shape=jax.ShapeDtypeStruct(own.shape, own.dtype),
        in_specs=[whole, whole, hbm],
        out_specs=hbm,
        input_output_aliases={2: 0},
    )(across, below, own)
    return own, swap(own, "core")


def body(queries, keys, values, doc_lengths, out_weight):
    xh, z, core, tp = (lax.axis_index(name) for name in ("xh", "z", "core", "tp"))
    y, xl = tp // NX, tp % NX
    here = jnp.stack([z, core, xh, xl]).astype(jnp.int32)
    own = jnp.concatenate([keys, values], axis=0)
    pair = jnp.concatenate([own, swap(own, "xh")], axis=0)
    weight = gather_weight(out_weight, pair)
    other_q = swap(queries, "core")
    q = jnp.where(core == 0, jnp.concatenate([queries, other_q]), jnp.concatenate([other_q, queries]))
    up, down = {0: pair}, {0: pair}
    for s in range(1, NZ // 2):
        up[s] = ring(up[s - 1], 1)
        down[s] = ring(down[s - 1], -1)
    far = NZ // 2
    last_up = ring(up[far - 1][:QROWS], 1)
    last_down = ring(down[far - 1][QROWS:], -1)

    state = attend(here, doc_lengths, q, [(0, 0, 0, False), (0, 1, 0, True)], [pair], None)
    for steps in ((1,), (2, 3), (4, 5), (6,), (7,)):
        visits, operands = [], []
        for s in steps:
            for offset, block in ((s, up[s]), (-s, down[s])):
                visits += [(len(operands), 0, offset, False), (len(operands), 1, offset, True)]
                operands.append(block)
        state = attend(here, doc_lengths, q, visits, operands, state)
    visits = [(0, 0, far, False), (1, 0, far, True)]
    state = attend(here, doc_lengths, q, visits, [last_up, last_down], state)
    attended, a = merge(here, state, swap(state, "core"))

    across = hop(a, 0, 1)
    below, above = hop(a, 1, 0), hop(a, -1, 0)
    weights = exchange_weight(weight, across, below)
    two = hop(below, 1, 0)
    across_below, across_above = hop(across, 1, 0), hop(across, -1, 0)
    across_two = hop(across_above, -1, 0)
    projected = None
    for dy, near, far in (
        (0, a, across),
        (-1, below, across_below),
        (1, above, across_above),
        (2, two, across_two),
    ):
        where = jnp.stack([(y + dy + NY) % NY, z, core, xh, xl]).astype(jnp.int32)
        projected = project(where, near, far, weights, projected)
    return (attended, projected)


def solution(mesh):
    fine = Mesh(mesh.devices.reshape(XH, NZ, NC, NY * NX), ("xh", "z", "core", "tp"))
    ctx = ("xh", "z", "core")
    in_specs = (P(ctx, "tp"), P(ctx, "tp"), P(ctx, "tp"), P(), P("tp", ctx, None))
    out_specs = (P(ctx, "tp"), P(ctx, "tp"))
    return jax.shard_map(body, mesh=fine, in_specs=in_specs, out_specs=out_specs, check_vma=False)
```

profile of v0, /device:TPU:6, one launch (start us, length us, event | category | flops | bytes accessed | tf_op | source)
XLA Modules:
  0.0 228.9 jit_solution(7028274222534665727)
XLA Ops:
  8.1 3.3 %collective-permute-start.1 = (bf16[448,128]{1,0:T(8,128)(2,1)S(1)}, bf16[448,128]{1,0:T(8,128)(2,1)S(1)}, u32[]{:S(2)}, u32[]{:S(2)}) collective-permute-start(bf16[448,128]{1,0:T(8,128)(2,1)S(1)} %pad_maximum_fusion), channel_id=1, source_target_pairs={{0,256},{256,0},{1,257},{257,1},{2,258},{258,2},{3,259},{259,3},{4... | collective-permute-start | bytes 344072 | tf_op jit(solution)/shard_map/ppermute | solution.py:194
  13.1 3.3 %collective-permute-done.1 = bf16[448,128]{1,0:T(8,128)(2,1)S(1)} collective-permute-done((bf16[448,128]{1,0:T(8,128)(2,1)S(1)}, bf16[448,128]{1,0:T(8,128)(2,1)S(1)}, u32[]{:S(2)}, u32[]{:S(2)}) %collective-permute-start.1) | collective-permute-done | bytes 114720 | tf_op jit(solution)/shard_map/ppermute | solution.py:194
  18.7 11.8 %all_to_all.5.mine_ref = bf16[8,2,3200]{2,1,0:T(2,128)(2,1)S(1)} all-to-all(bf16[8,2,3200]{2,1,0:T(2,128)(2,1)} %shard_map.76), channel_id=1, replica_groups=mesh['xh'=2,'z'=16,'core'=2,'tp'=8] {'tp'}, dimensions={0} | all-to-all | bytes 204800 | tf_op jit(solution)/shard_map/all_to_all | solution.py:236
  30.4 6.0 %collective-permute-start.24 = (bf16[8,2,3200]{2,1,0:T(2,128)(2,1)S(1)}, bf16[8,2,3200]{2,1,0:T(2,128)(2,1)S(1)}, u32[]{:S(2)}, u32[]{:S(2)}) collective-permute-start(bf16[8,2,3200]{2,1,0:T(2,128)(2,1)S(1)} %all_to_all.5.mine_ref), channel_id=1, source_target_pairs={{0,256},{256,0},{1,257},{257,1},{2,258},{258,2},{3,259},{259,3},{4... | collective-permute-start | bytes 307208 | tf_op jit(solution)/shard_map/ppermute | solution.py:194
  41.5 10.4 %collective-permute-start.10 = (bf16[896,128]{1,0:T(8,128)(2,1)}, bf16[896,128]{1,0:T(8,128)(2,1)S(1)}, u32[]{:S(2)}, u32[]{:S(2)}) collective-permute-start(bf16[896,128]{1,0:T(8,128)(2,1)} %copy-done.1), channel_id=1, source_target_pairs={{0,240},{16,0},{32,16},{48,32},{64,48},{80,64},{96,80},{112,96},{1... | collective-permute-start | bytes 688136 | tf_op jit(solution)/shard_map/ppermute | solution.py:198
  55.7 5.5 %collective-permute-start.11 = (bf16[896,128]{1,0:T(8,128)(2,1)S(1)}, bf16[896,128]{1,0:T(8,128)(2,1)S(1)}, u32[]{:S(2)}, u32[]{:S(2)}) collective-permute-start(bf16[896,128]{1,0:T(8,128)(2,1)S(1)} %collective-permute-done.10.refs_1_), channel_id=1, source_target_pairs={{0,240},{16,0},{32,16},{48,32},{64,48},{80,64},{96,80},{112,96},{1... | collective-permute-start | bytes 688136 | tf_op jit(solution)/shard_map/ppermute | solution.py:198
  63.1 5.6 %collective-permute-done.11.refs_1_ = bf16[896,128]{1,0:T(8,128)(2,1)S(1)} collective-permute-done((bf16[896,128]{1,0:T(8,128)(2,1)S(1)}, bf16[896,128]{1,0:T(8,128)(2,1)S(1)}, u32[]{:S(2)}, u32[]{:S(2)}) %collective-permute-start.11) | collective-permute-done | bytes 229408 | tf_op jit(solution)/shard_map/ppermute | solution.py:198
  70.7 5.7 %collective-permute-done.3.refs_0_ = bf16[896,128]{1,0:T(8,128)(2,1)S(1)} collective-permute-done((bf16[896,128]{1,0:T(8,128)(2,1)S(1)}, bf16[896,128]{1,0:T(8,128)(2,1)S(1)}, u32[]{:S(2)}, u32[]{:S(2)}) %collective-permute-start.3) | collective-permute-done | bytes 229408 | tf_op jit(solution)/shard_map/ppermute | solution.py:198
  78.2 4.9 %collective-permute-done.12.refs_3_ = bf16[896,128]{1,0:T(8,128)(2,1)S(1)} collective-permute-done((bf16[896,128]{1,0:T(8,128)(2,1)S(1)}, bf16[896,128]{1,0:T(8,128)(2,1)S(1)}, u32[]{:S(2)}, u32[]{:S(2)}) %collective-permute-start.12) | collective-permute-done | bytes 229408 | tf_op jit(solution)/shard_map/ppermute | solution.py:198
  85.1 5.3 %collective-permute-done.4.refs_2_ = bf16[896,128]{1,0:T(8,128)(2,1)S(1)} collective-permute-done((bf16[896,128]{1,0:T(8,128)(2,1)S(1)}, bf16[896,128]{1,0:T(8,128)(2,1)S(1)}, u32[]{:S(2)}, u32[]{:S(2)}) %collective-permute-start.4) | collective-permute-done | bytes 229408 | tf_op jit(solution)/shard_map/ppermute | solution.py:198
  94.6 4.7 %collective-permute-start.14 = (bf16[896,128]{1,0:T(8,128)(2,1)S(1)}, bf16[896,128]{1,0:T(8,128)(2,1)S(1)}, u32[]{:S(2)}, u32[]{:S(2)}) collective-permute-start(bf16[896,128]{1,0:T(8,128)(2,1)S(1)} %collective-permute-done.13.refs_1_), channel_id=1, source_target_pairs={{0,240},{16,0},{32,16},{48,32},{64,48},{80,64},{96,80},{112,96},{1... | collective-permute-start | bytes 688136 | tf_op jit(solution)/shard_map/ppermute | solution.py:198
  104.0 5.5 %collective-permute-done.14.refs_3_ = bf16[896,128]{1,0:T(8,128)(2,1)S(1)} collective-permute-done((bf16[896,128]{1,0:T(8,128)(2,1)S(1)}, bf16[896,128]{1,0:T(8,128)(2,1)S(1)}, u32[]{:S(2)}, u32[]{:S(2)}) %collective-permute-start.14) | collective-permute-done | bytes 229408 | tf_op jit(solution)/shard_map/ppermute | solution.py:198
  109.6 5.5 %collective-permute-start.15 = (bf16[896,128]{1,0:T(8,128)(2,1)S(1)}, bf16[896,128]{1,0:T(8,128)(2,1)S(1)}, u32[]{:S(2)}, u32[]{:S(2)}) collective-permute-start(bf16[896,128]{1,0:T(8,128)(2,1)S(1)} %collective-permute-done.14.refs_3_), channel_id=1, source_target_pairs={{0,240},{16,0},{32,16},{48,32},{64,48},{80,64},{96,80},{112,96},{1... | collective-permute-start | bytes 688136 | tf_op jit(solution)/shard_map/ppermute | solution.py:198
  123.6 5.6 %collective-permute-start.16 = (bf16[896,128]{1,0:T(8,128)(2,1)S(1)}, bf16[896,128]{1,0:T(8,128)(2,1)S(1)}, u32[]{:S(2)}, u32[]{:S(2)}) collective-permute-start(bf16[896,128]{1,0:T(8,128)(2,1)S(1)} %collective-permute-done.15.refs_1_), channel_id=1, source_target_pairs={{0,240},{16,0},{32,16},{48,32},{64,48},{80,64},{96,80},{112,96},{1... | collective-permute-start | bytes 688136 | tf_op jit(solution)/shard_map/ppermute | solution.py:198
  131.2 8.3 %shard_map.70.refs_4_ = f32[656,448]{1,0:T(8,128)S(1)} custom-call(s32[4]{0:T(128)S(1)} %pad_add_fusion.here_ref, s32[16]{0:T(128)S(1)} %copy-done.9, bf16[448,640]{1,0:T(8,128)(2,1)S(1)} %maximum_select_fusion.q_ref, bf16[896,128]{1,0:T(8,128)(2,1)S(1)} %collective-permute-done.3.refs_0_, ...), custom_call_target="tpu_custom_call", output_to_operand_aliasing={{}: (7, {})} | custom-call | flops 2055208960 | bytes 2351104 | tf_op jit(solution)/shard_map/pallas_call | solution.py:100
  139.4 8.5 %shard_map.71.refs_2_ = f32[656,448]{1,0:T(8,128)S(1)} custom-call(s32[4]{0:T(128)S(1)} %pad_add_fusion.here_ref, s32[16]{0:T(128)S(1)} %copy-done.9, bf16[448,640]{1,0:T(8,128)(2,1)S(1)} %maximum_select_fusion.q_ref, bf16[896,128]{1,0:T(8,128)(2,1)S(1)} %collective-permute-done.5.refs_0_, ...), custom_call_target="tpu_custom_call", output_to_operand_aliasing={{}: (7, {})} | custom-call | flops 2055208960 | bytes 2351104 | tf_op jit(solution)/shard_map/pallas_call | solution.py:100
  149.9 3.9 %collective-permute-start.9 = (bf16[448,128]{1,0:T(8,128)(2,1)S(1)}, bf16[448,128]{1,0:T(8,128)(2,1)S(1)}, u32[]{:S(2)}, u32[]{:S(2)}) collective-permute-start(bf16[448,128]{1,0:T(8,128)(2,1)S(1)} %slice.8), channel_id=1, source_target_pairs={{0,16},{16,32},{32,48},{48,64},{64,80},{80,96},{96,112},{112,128},... | collective-permute-start | bytes 344072 | tf_op jit(solution)/shard_map/ppermute | solution.py:198
  153.8 4.5 %shard_map.72.refs_2_ = f32[656,448]{1,0:T(8,128)S(1)} custom-call(s32[4]{0:T(128)S(1)} %pad_add_fusion.here_ref, s32[16]{0:T(128)S(1)} %copy-done.9, bf16[448,640]{1,0:T(8,128)(2,1)S(1)} %maximum_select_fusion.q_ref, bf16[896,128]{1,0:T(8,128)(2,1)S(1)} %collective-permute-done.7.refs_0_, ...), custom_call_target="tpu_custom_call", output_to_operand_aliasing={{}: (5, {})} | custom-call | flops 1027604480 | bytes 2351104 | tf_op jit(solution)/shard_map/pallas_call | solution.py:100
  158.3 4.5 %shard_map.73.refs_2_ = f32[656,448]{1,0:T(8,128)S(1)} custom-call(s32[4]{0:T(128)S(1)} %pad_add_fusion.here_ref, s32[16]{0:T(128)S(1)} %copy-done.9, bf16[448,640]{1,0:T(8,128)(2,1)S(1)} %maximum_select_fusion.q_ref, bf16[896,128]{1,0:T(8,128)(2,1)S(1)} %collective-permute-done.8.refs_0_, ...), custom_call_target="tpu_custom_call", output_to_operand_aliasing={{}: (5, {})} | custom-call | flops 1027604480 | bytes 2351104 | tf_op jit(solution)/shard_map/pallas_call | solution.py:100
  176.7 7.8 %collective-permute-done.19.below_ref.near_ref = bf16[224,640]{1,0:T(8,128)(2,1)S(1)} collective-permute-done((bf16[224,640]{1,0:T(8,128)(2,1)S(1)}, bf16[224,640]{1,0:T(8,128)(2,1)S(1)}, u32[]{:S(2)}, u32[]{:S(2)}) %collective-permute-start.19) | collective-permute-done | bytes 286752 | tf_op jit(solution)/shard_map/ppermute | solution.py:205
  187.8 4.9 %collective-permute-start.22 = (bf16[224,640]{1,0:T(8,128)(2,1)}, bf16[224,640]{1,0:T(8,128)(2,1)}, u32[]{:S(2)}, u32[]{:S(2)}) collective-permute-start(bf16[224,640]{1,0:T(8,128)(2,1)} %copy-done.5), channel_id=1, source_target_pairs={{0,6},{1,7},{2,0},{3,1},{4,2},{5,3},{6,4},{7,5},{8,14},{9,15},{10,... | collective-permute-start | bytes 860168 | tf_op jit(solution)/shard_map/ppermute | solution.py:205
  194.6 5.1 %collective-permute-start.26 = (bf16[224,640]{1,0:T(8,128)(2,1)}, bf16[224,640]{1,0:T(8,128)(2,1)}, u32[]{:S(2)}, u32[]{:S(2)}) collective-permute-start(bf16[224,640]{1,0:T(8,128)(2,1)} %copy-done.7), channel_id=1, source_target_pairs={{0,6},{1,7},{2,0},{3,1},{4,2},{5,3},{6,4},{7,5},{8,14},{9,15},{10,... | collective-permute-start | bytes 860168 | tf_op jit(solution)/shard_map/ppermute | solution.py:205
  201.7 5.1 %collective-permute-start.23 = (bf16[224,640]{1,0:T(8,128)(2,1)}, bf16[224,640]{1,0:T(8,128)(2,1)}, u32[]{:S(2)}, u32[]{:S(2)}) collective-permute-start(bf16[224,640]{1,0:T(8,128)(2,1)} %collective-permute-done.22.far_ref), channel_id=1, source_target_pairs={{0,6},{1,7},{2,0},{3,1},{4,2},{5,3},{6,4},{7,5},{8,14},{9,15},{10,... | collective-permute-start | bytes 860168 | tf_op jit(solution)/shard_map/ppermute | solution.py:205
  218.4 3.6 %shard_map.82 = f32[224,640]{1,0:T(8,128)} custom-call(s32[5]{0:T(128)S(1)} %stack.61.here_ref, bf16[224,640]{1,0:T(8,128)(2,1)} %collective-permute-done.20.near_ref, bf16[224,640]{1,0:T(8,128)(2,1)} %collective-permute-done.23.far_ref, bf16[128,12800]{1,0:T(8,128)(2,1)S(1)} %copy-done, bf16[128,12800]{1,0:T(8,128)(2,1)S(1)} %collective-permute-done.25.other_ref, ...), custom_call_target="tpu_custom_call" | custom-call | flops 513802240 | bytes 1638400 | tf_op jit(solution)/shard_map/pallas_call | solution.py:175
  (89 shorter events, 75.1 us)
Async XLA Ops:
  7.2 178.0 %all-gather.2.cloned.1.call-start = ((), (), s32[]{:S(2)}) async-start(), calls=%async_computation.1 | async-start | bytes 3481600 | tf_op jit(solution)/shard_map/all_gather | solution.py:243
  41.5 14.2 %collective-permute-start.10 = (bf16[896,128]{1,0:T(8,128)(2,1)}, bf16[896,128]{1,0:T(8,128)(2,1)S(1)}, u32[]{:S(2)}, u32[]{:S(2)}) collective-permute-start(bf16[896,128]{1,0:T(8,128)(2,1)} %copy-done.1), channel_id=1, source_target_pairs={{0,240},{16,0},{32,16},{48,32},{64,48},{80,64},{96,80},{112,96},{1... | collective-permute-start | bytes 688136 | tf_op jit(solution)/shard_map/ppermute | solution.py:198
  55.7 13.0 %collective-permute-start.11 = (bf16[896,128]{1,0:T(8,128)(2,1)S(1)}, bf16[896,128]{1,0:T(8,128)(2,1)S(1)}, u32[]{:S(2)}, u32[]{:S(2)}) collective-permute-start(bf16[896,128]{1,0:T(8,128)(2,1)S(1)} %collective-permute-done.10.refs_1_), channel_id=1, source_target_pairs={{0,240},{16,0},{32,16},{48,32},{64,48},{80,64},{96,80},{112,96},{1... | collective-permute-start | bytes 688136 | tf_op jit(solution)/shard_map/ppermute | solution.py:198
  61.2 15.1 %collective-permute-start.3 = (bf16[896,128]{1,0:T(8,128)(2,1)S(1)}, bf16[896,128]{1,0:T(8,128)(2,1)S(1)}, u32[]{:S(2)}, u32[]{:S(2)}) collective-permute-start(bf16[896,128]{1,0:T(8,128)(2,1)S(1)} %collective-permute-done.2.refs_0_), channel_id=1, source_target_pairs={{0,16},{16,32},{32,48},{48,64},{64,80},{80,96},{96,112},{112,128},... | collective-permute-start | bytes 688136 | tf_op jit(solution)/shard_map/ppermute | solution.py:198
  68.7 14.4 %collective-permute-start.12 = (bf16[896,128]{1,0:T(8,128)(2,1)S(1)}, bf16[896,128]{1,0:T(8,128)(2,1)S(1)}, u32[]{:S(2)}, u32[]{:S(2)}) collective-permute-start(bf16[896,128]{1,0:T(8,128)(2,1)S(1)} %collective-permute-done.11.refs_1_), channel_id=1, source_target_pairs={{0,240},{16,0},{32,16},{48,32},{64,48},{80,64},{96,80},{112,96},{1... | collective-permute-start | bytes 688136 | tf_op jit(solution)/shard_map/ppermute | solution.py:198
  76.3 14.0 %collective-permute-start.4 = (bf16[896,128]{1,0:T(8,128)(2,1)S(1)}, bf16[896,128]{1,0:T(8,128)(2,1)S(1)}, u32[]{:S(2)}, u32[]{:S(2)}) collective-permute-start(bf16[896,128]{1,0:T(8,128)(2,1)S(1)} %collective-permute-done.3.refs_0_), channel_id=1, source_target_pairs={{0,16},{16,32},{32,48},{48,64},{64,80},{80,96},{96,112},{112,128},... | collective-permute-start | bytes 688136 | tf_op jit(solution)/shard_map/ppermute | solution.py:198
  83.1 11.5 %collective-permute-start.13 = (bf16[896,128]{1,0:T(8,128)(2,1)S(1)}, bf16[896,128]{1,0:T(8,128)(2,1)S(1)}, u32[]{:S(2)}, u32[]{:S(2)}) collective-permute-start(bf16[896,128]{1,0:T(8,128)(2,1)S(1)} %collective-permute-done.12.refs_3_), channel_id=1, source_target_pairs={{0,240},{16,0},{32,16},{48,32},{64,48},{80,64},{96,80},{112,96},{1... | collective-permute-start | bytes 688136 | tf_op jit(solution)/shard_map/ppermute | solution.py:198
  90.3 11.5 %collective-permute-start.5 = (bf16[896,128]{1,0:T(8,128)(2,1)S(1)}, bf16[896,128]{1,0:T(8,128)(2,1)S(1)}, u32[]{:S(2)}, u32[]{:S(2)}) collective-permute-start(bf16[896,128]{1,0:T(8,128)(2,1)S(1)} %collective-permute-done.4.refs_2_), channel_id=1, source_target_pairs={{0,16},{16,32},{32,48},{48,64},{64,80},{80,96},{96,112},{112,128},... | collective-permute-start | bytes 688136 | tf_op jit(solution)/shard_map/ppermute | solution.py:198
  92.7 24.4 %collective-permute-start = (bf16[224,640]{1,0:T(8,128)(2,1)S(1)}, bf16[224,640]{1,0:T(8,128)(2,1)S(1)}, u32[]{:S(2)}, u32[]{:S(2)}) collective-permute-start(bf16[224,640]{1,0:T(8,128)(2,1)S(1)} %copy-done.11), channel_id=1, source_target_pairs={{0,8},{8,0},{1,9},{9,1},{2,10},{10,2},{3,11},{11,3},{4,12},{12,4},... | collective-permute-start | bytes 860168 | tf_op jit(solution)/shard_map/ppermute | solution.py:194
  94.6 14.9 %collective-permute-start.14 = (bf16[896,128]{1,0:T(8,128)(2,1)S(1)}, bf16[896,128]{1,0:T(8,128)(2,1)S(1)}, u32[]{:S(2)}, u32[]{:S(2)}) collective-permute-start(bf16[896,128]{1,0:T(8,128)(2,1)S(1)} %collective-permute-done.13.refs_1_), channel_id=1, source_target_pairs={{0,240},{16,0},{32,16},{48,32},{64,48},{80,64},{96,80},{112,96},{1... | collective-permute-start | bytes 688136 | tf_op jit(solution)/shard_map/ppermute | solution.py:198
  101.9 13.2 %collective-permute-start.6 = (bf16[896,128]{1,0:T(8,128)(2,1)S(1)}, bf16[896,128]{1,0:T(8,128)(2,1)S(1)}, u32[]{:S(2)}, u32[]{:S(2)}) collective-permute-start(bf16[896,128]{1,0:T(8,128)(2,1)S(1)} %collective-permute-done.5.refs_0_), channel_id=1, source_target_pairs={{0,16},{16,32},{32,48},{48,64},{64,80},{80,96},{96,112},{112,128},... | collective-permute-start | bytes 688136 | tf_op jit(solution)/shard_map/ppermute | solution.py:198
  109.6 14.1 %collective-permute-start.15 = (bf16[896,128]{1,0:T(8,128)(2,1)S(1)}, bf16[896,128]{1,0:T(8,128)(2,1)S(1)}, u32[]{:S(2)}, u32[]{:S(2)}) collective-permute-start(bf16[896,128]{1,0:T(8,128)(2,1)S(1)} %collective-permute-done.14.refs_3_), channel_id=1, source_target_pairs={{0,240},{16,0},{32,16},{48,32},{64,48},{80,64},{96,80},{112,96},{1... | collective-permute-start | bytes 688136 | tf_op jit(solution)/shard_map/ppermute | solution.py:198
  115.1 14.1 %collective-permute-start.7 = (bf16[896,128]{1,0:T(8,128)(2,1)S(1)}, bf16[896,128]{1,0:T(8,128)(2,1)S(1)}, u32[]{:S(2)}, u32[]{:S(2)}) collective-permute-start(bf16[896,128]{1,0:T(8,128)(2,1)S(1)} %collective-permute-done.6.refs_2_), channel_id=1, source_target_pairs={{0,16},{16,32},{32,48},{48,64},{64,80},{80,96},{96,112},{112,128},... | collective-permute-start | bytes 688136 | tf_op jit(solution)/shard_map/ppermute | solution.py:198
  123.6 24.3 %collective-permute-start.16 = (bf16[896,128]{1,0:T(8,128)(2,1)S(1)}, bf16[896,128]{1,0:T(8,128)(2,1)S(1)}, u32[]{:S(2)}, u32[]{:S(2)}) collective-permute-start(bf16[896,128]{1,0:T(8,128)(2,1)S(1)} %collective-permute-done.15.refs_1_), channel_id=1, source_target_pairs={{0,240},{16,0},{32,16},{48,32},{64,48},{80,64},{96,80},{112,96},{1... | collective-permute-start | bytes 688136 | tf_op jit(solution)/shard_map/ppermute | solution.py:198
  129.2 20.6 %collective-permute-start.8 = (bf16[896,128]{1,0:T(8,128)(2,1)S(1)}, bf16[896,128]{1,0:T(8,128)(2,1)S(1)}, u32[]{:S(2)}, u32[]{:S(2)}) collective-permute-start(bf16[896,128]{1,0:T(8,128)(2,1)S(1)} %collective-permute-done.7.refs_0_), channel_id=1, source_target_pairs={{0,16},{16,32},{32,48},{48,64},{64,80},{80,96},{96,112},{112,128},... | collective-permute-start | bytes 688136 | tf_op jit(solution)/shard_map/ppermute | solution.py:198
  147.9 14.9 %collective-permute-start.17 = (bf16[448,128]{1,0:T(8,128)(2,1)S(1)}, bf16[448,128]{1,0:T(8,128)(2,1)S(1)}, u32[]{:S(2)}, u32[]{:S(2)}) collective-permute-start(bf16[448,128]{1,0:T(8,128)(2,1)S(1)} %slice.9), channel_id=1, source_target_pairs={{0,240},{16,0},{32,16},{48,32},{64,48},{80,64},{96,80},{112,96},{1... | collective-permute-start | bytes 344072 | tf_op jit(solution)/shard_map/ppermute | solution.py:198
  149.9 13.0 %collective-permute-start.9 = (bf16[448,128]{1,0:T(8,128)(2,1)S(1)}, bf16[448,128]{1,0:T(8,128)(2,1)S(1)}, u32[]{:S(2)}, u32[]{:S(2)}) collective-permute-start(bf16[448,128]{1,0:T(8,128)(2,1)S(1)} %slice.8), channel_id=1, source_target_pairs={{0,16},{16,32},{32,48},{48,64},{64,80},{80,96},{96,112},{112,128},... | collective-permute-start | bytes 344072 | tf_op jit(solution)/shard_map/ppermute | solution.py:198
  172.5 12.0 %collective-permute-start.19 = (bf16[224,640]{1,0:T(8,128)(2,1)S(1)}, bf16[224,640]{1,0:T(8,128)(2,1)S(1)}, u32[]{:S(2)}, u32[]{:S(2)}) collective-permute-start(bf16[224,640]{1,0:T(8,128)(2,1)S(1)} %get-tuple-element.5.near_ref), channel_id=1, source_target_pairs={{0,2},{1,3},{2,4},{3,5},{4,6},{5,7},{6,0},{7,1},{8,10},{9,11},{10,... | collective-permute-start | bytes 860168 | tf_op jit(solution)/shard_map/ppermute | solution.py:205
  185.9 21.3 %collective-permute-start.25 = (bf16[128,12800]{1,0:T(8,128)(2,1)}, bf16[128,12800]{1,0:T(8,128)(2,1)S(1)}, u32[]{:S(2)}, u32[]{:S(2)}) collective-permute-start(bf16[128,12800]{1,0:T(8,128)(2,1)} %shard_map.78.own_ref), channel_id=1, source_target_pairs={{0,8},{8,0},{1,9},{9,1},{2,10},{10,2},{3,11},{11,3},{4,12},{12,4},... | collective-permute-start | bytes 9830408 | tf_op jit(solution)/shard_map/ppermute | solution.py:194
  187.8 13.9 %collective-permute-start.22 = (bf16[224,640]{1,0:T(8,128)(2,1)}, bf16[224,640]{1,0:T(8,128)(2,1)}, u32[]{:S(2)}, u32[]{:S(2)}) collective-permute-start(bf16[224,640]{1,0:T(8,128)(2,1)} %copy-done.5), channel_id=1, source_target_pairs={{0,6},{1,7},{2,0},{3,1},{4,2},{5,3},{6,4},{7,5},{8,14},{9,15},{10,... | collective-permute-start | bytes 860168 | tf_op jit(solution)/shard_map/ppermute | solution.py:205
  192.7 20.1 %collective-permute-start.27 = (bf16[224,640]{1,0:T(8,128)(2,1)}, bf16[224,640]{1,0:T(8,128)(2,1)}, u32[]{:S(2)}, u32[]{:S(2)}) collective-permute-start(bf16[224,640]{1,0:T(8,128)(2,1)} %copy-done.5), channel_id=1, source_target_pairs={{0,2},{1,3},{2,4},{3,5},{4,6},{5,7},{6,0},{7,1},{8,10},{9,11},{10,... | collective-permute-start | bytes 860168 | tf_op jit(solution)/shard_map/ppermute | solution.py:205
  194.6 21.0 %collective-permute-start.26 = (bf16[224,640]{1,0:T(8,128)(2,1)}, bf16[224,640]{1,0:T(8,128)(2,1)}, u32[]{:S(2)}, u32[]{:S(2)}) collective-permute-start(bf16[224,640]{1,0:T(8,128)(2,1)} %copy-done.7), channel_id=1, source_target_pairs={{0,6},{1,7},{2,0},{3,1},{4,2},{5,3},{6,4},{7,5},{8,14},{9,15},{10,... | collective-permute-start | bytes 860168 | tf_op jit(solution)/shard_map/ppermute | solution.py:205
  199.8 18.7 %collective-permute-start.20 = (bf16[224,640]{1,0:T(8,128)(2,1)}, bf16[224,640]{1,0:T(8,128)(2,1)}, u32[]{:S(2)}, u32[]{:S(2)}) collective-permute-start(bf16[224,640]{1,0:T(8,128)(2,1)} %copy-done.3), channel_id=1, source_target_pairs={{0,2},{1,3},{2,4},{3,5},{4,6},{5,7},{6,0},{7,1},{8,10},{9,11},{10,... | collective-permute-start | bytes 860168 | tf_op jit(solution)/shard_map/ppermute | solution.py:205
  201.7 16.7 %collective-permute-start.23 = (bf16[224,640]{1,0:T(8,128)(2,1)}, bf16[224,640]{1,0:T(8,128)(2,1)}, u32[]{:S(2)}, u32[]{:S(2)}) collective-permute-start(bf16[224,640]{1,0:T(8,128)(2,1)} %collective-permute-done.22.far_ref), channel_id=1, source_target_pairs={{0,6},{1,7},{2,0},{3,1},{4,2},{5,3},{6,4},{7,5},{8,14},{9,15},{10,... | collective-permute-start | bytes 860168 | tf_op jit(solution)/shard_map/ppermute | solution.py:205
  (18 other events, 359.4 us)
Sparse Core Ops, SparseCore 0:
  41.6 85.3 all-gather.1
where the time goes:
time: 230 us; the launch traced here: 229 us
  starting transfers between devices  93.6 us (41%)
  waiting for transfers between devices  50.1 us (22%)
  Pallas kernels  49.8 us (22%)
  between operations  14.6 us (6%)
  blocking collectives  11.8 us (5%)
  local copies, waits for them, and re-layouts  7.93 us (3%)
    ppermute x16, starting transfers between devices, ring(): return lax.ppermute(value, 'z', [(i, (i + steps) % NZ) for i in range(NZ)])  55.4 us
    pallas_call x7, Pallas kernels, attend(): pl.pallas_call(functools.partial(attend_kernel, visits, state is None), o...  33.7 us
    ppermute x16, waiting for transfers between devices, ring(): return lax.ppermute(value, 'z', [(i, (i + steps) % NZ) for i in range(NZ)])  32.6 us
    ppermute x7, starting transfers between devices, hop(): return lax.ppermute(block, 'tp', perm)  23.1 us
    ppermute x5, starting transfers between devices, swap(): return lax.ppermute(value, axis, [(0, 1), (1, 0)])  15.1 us
    all_to_all x1, blocking collectives, gather_weight(): split = lax.all_to_all(split, 'tp', 0, 0)  11.8 us
    pallas_call x4, Pallas kernels, project(): pl.pallas_call(functools.partial(project_kernel, total is None), grid_spe...  10.9 us
    ppermute x5, waiting for transfers between devices, swap(): return lax.ppermute(value, axis, [(0, 1), (1, 0)])  8.98 us
  transfers between devices with their start and end apart: 29, of which 13 were waited for; matrix products, arithmetic and copies ran while one was open for 1% of the time, Pallas kernels for 19%

commit v1 on v0

--- a/solution.py
+++ b/solution.py
@@ -16,6 +16,7 @@
 WIDE = HEADS * HD
 STATE = WIDE + 16
 DEEP = 2 * HD
+COST = 64
 FLOOR = -1e29
 MASKED = -1e30
 NEG = (((1,), (1,)), ((), ()))
@@ -108,7 +109,7 @@
         ],
         input_output_aliases=aliases,
         cost_estimate=pl.CostEstimate(
-            flops=pairs * HD * 8, bytes_accessed=STATE * QROWS * 8, transcendentals=pairs
+            flops=pairs * HD * COST, bytes_accessed=STATE * QROWS * COST, transcendentals=pairs
         ),
         compiler_params=pltpu.CompilerParams(vmem_limit_bytes=VMEM),
     )(here, lengths, q, *operands)
@@ -147,47 +148,45 @@
     )(here, mine, other)
 
 
-def project_kernel(first, here_ref, near_ref, far_ref, own_ref, other_ref, *refs):
-    core, xh, xl = here_ref[2], here_ref[3], here_ref[4]
+def project_kernel(steps, here_ref, own_ref, other_ref, *refs):
+    z, core, xh, xl, y = (here_ref[i] for i in range(5))
     k = lax.broadcasted_iota(jnp.int32, (DEEP, DEEP), 0)
     g = lax.broadcasted_iota(jnp.int32, (DEEP, DEEP), 1)
-    source_core = core ^ (g >> 7)
     row = g & (HD - 1)
-    d = (xh ^ ((row >> 1) & 1)) * (NZ * 4) + (row >> 3) * 4 + source_core * 2 + (row & 1)
-    source_x = xl ^ (k >> 7)
-    match = ((k & (HD - 1)) == d) & (((row >> 2) & 1) == source_x)
+    d = (xh ^ ((row >> 1) & 1)) * (NZ * 4) + (row >> 3) * 4 + (core ^ (g >> 7)) * 2 + (row & 1)
+    match = ((k & (HD - 1)) == d) & (((row >> 2) & 1) == (xl ^ (k >> 7)))
     perm = jnp.where(match, 1.0, 0.0).astype(BF16)
-    total = jnp.zeros((ROWS, WIDE), F32) if first else refs[0][...]
-    for h in range(HEADS):
-        heads = slice(h * HD, (h + 1) * HD)
-        columns = slice(h * WIDE, (h + 1) * WIDE)
-        both = jnp.concatenate([near_ref[:, heads], far_ref[:, heads]], axis=1)
-        moved = jnp.dot(both, perm, preferred_element_type=F32).astype(BF16)
-        weight = jnp.concatenate([own_ref[:, columns], other_ref[:, columns]], axis=0)
-        total += jnp.dot(moved, weight, preferred_element_type=F32)
+    near_refs, far_refs = refs[: len(steps)], refs[len(steps) : 2 * len(steps)]
+    total = jnp.zeros((ROWS, WIDE), F32) if len(refs) == 2 * len(steps) + 1 else refs[-2][...]
+    for step, near_ref, far_ref in zip(steps, near_refs, far_refs):
+        start = ((y + step + NY) & (NY - 1)) * (HEADS * WIDE)
+        for h in range(HEADS):
+            heads = slice(h * HD, (h + 1) * HD)
+            columns = pl.ds(pl.multiple_of(start + h * WIDE, HD), WIDE)
+            both = jnp.concatenate([near_ref[:, heads], far_ref[:, heads]], axis=1)
+            moved = jnp.dot(both, perm, preferred_element_type=F32).astype(BF16)
+            weight = jnp.concatenate([own_ref[:, columns], other_ref[:, columns]], axis=0)
+            total += jnp.dot(moved, weight, preferred_element_type=F32)
     refs[-1][...] = total
 
 
-def project(where, near, far, weights, total):
-    block = pl.BlockSpec((ROWS, WIDE), lambda i, w: (0, 0))
-    weight = pl.BlockSpec((HD, HEADS * WIDE), lambda i, w: (0, w[0]))
-    totals = [] if total is None else [total]
+def project(here, weights, pairs, total):
+    steps = [step for step, _, _ in pairs]
+    operands = [near for _, near, _ in pairs] + [far for _, _, far in pairs]
+    operands += [] if total is None else [total]
+    vmem = pl.BlockSpec(memory_space=pltpu.VMEM)
     return pl.pallas_call(
-        functools.partial(project_kernel, total is None),
-        grid_spec=pltpu.PrefetchScalarGridSpec(
-            num_scalar_prefetch=1,
-            grid=(1,),
-            in_specs=[block, block, weight, weight] + [block] * len(totals),
-            out_specs=block,
-        ),
+        functools.partial(project_kernel, steps),
         out_shape=jax.ShapeDtypeStruct((ROWS, WIDE), F32),
+        in_specs=[pl.BlockSpec(memory_space=pltpu.SMEM)] + [vmem] * (2 + len(operands)),
+        out_specs=vmem,
         cost_estimate=pl.CostEstimate(
-            flops=2 * ROWS * DEEP * HEADS * (WIDE + DEEP),
-            bytes_accessed=DEEP * HEADS * WIDE * 2,
+            flops=2 * len(steps) * ROWS * DEEP * HEADS * (WIDE + DEEP),
+            bytes_accessed=DEEP * NY * HEADS * WIDE * 2,
             transcendentals=0,
         ),
         compiler_params=pltpu.CompilerParams(vmem_limit_bytes=VMEM),
-    )(where, near, far, *weights, *totals)
+    )(here, *weights, *operands)
 
 
 def swap(value, axis):
@@ -220,7 +219,7 @@
                 out_ref[row : row + 2, lanes] = ref[y * NX + e]
 
 
-def pass_kernel(across_ref, below_ref, weight_ref, out_ref):
+def pass_kernel(*refs):
     pass
 
 
@@ -243,63 +242,48 @@
     return lax.all_gather(rows, "z", axis=0, tiled=True)
 
 
-def exchange_weight(own, across, below):
+def exchange_weight(own, *after):
     whole = pl.BlockSpec(memory_space=pl.ANY)
     hbm = pl.BlockSpec(memory_space=pltpu.HBM)
     own = pl.pallas_call(
         pass_kernel,
         out_shape=jax.ShapeDtypeStruct(own.shape, own.dtype),
-        in_specs=[whole, whole, hbm],
+        in_specs=[whole] * len(after) + [hbm],
         out_specs=hbm,
-        input_output_aliases={2: 0},
-    )(across, below, own)
+        input_output_aliases={len(after): 0},
+    )(*after, own)
     return own, swap(own, "core")
 
 
 def body(queries, keys, values, doc_lengths, out_weight):
     xh, z, core, tp = (lax.axis_index(name) for name in ("xh", "z", "core", "tp"))
-    y, xl = tp // NX, tp % NX
-    here = jnp.stack([z, core, xh, xl]).astype(jnp.int32)
+    here = jnp.stack([z, core, xh, tp % NX, tp // NX]).astype(jnp.int32)
     own = jnp.concatenate([keys, values], axis=0)
     pair = jnp.concatenate([own, swap(own, "xh")], axis=0)
-    weight = gather_weight(out_weight, pair)
     other_q = swap(queries, "core")
     q = jnp.where(core == 0, jnp.concatenate([queries, other_q]), jnp.concatenate([other_q, queries]))
-    up, down = {0: pair}, {0: pair}
-    for s in range(1, NZ // 2):
-        up[s] = ring(up[s - 1], 1)
-        down[s] = ring(down[s - 1], -1)
+    up, down = [pair], [pair]
     far = NZ // 2
-    last_up = ring(up[far - 1][:QROWS], 1)
-    last_down = ring(down[far - 1][QROWS:], -1)
+    for _ in range(1, far):
+        up.append(ring(up[-1], 1))
+        down.append(ring(down[-1], -1))
+    last = [ring(up[-1][:QROWS], 1), ring(down[-1][QROWS:], -1)]
+    weight = gather_weight(out_weight, up[1])
 
     state = attend(here, doc_lengths, q, [(0, 0, 0, False), (0, 1, 0, True)], [pair], None)
-    for steps in ((1,), (2, 3), (4, 5), (6,), (7,)):
-        visits, operands = [], []
-        for s in steps:
-            for offset, block in ((s, up[s]), (-s, down[s])):
-                visits += [(len(operands), 0, offset, False), (len(operands), 1, offset, True)]
-                operands.append(block)
-        state = attend(here, doc_lengths, q, visits, operands, state)
-    visits = [(0, 0, far, False), (1, 0, far, True)]
-    state = attend(here, doc_lengths, q, visits, [last_up, last_down], state)
+    for s in range(1, far):
+        visits = [(0, 0, s, False), (0, 1, s, True), (1, 0, -s, False), (1, 1, -s, True)]
+        state = attend(here, doc_lengths, q, visits, [up[s], down[s]], state)
+    state = attend(here, doc_lengths, q, [(0, 0, far, False), (1, 0, far, True)], last, state)
     attended, a = merge(here, state, swap(state, "core"))
 
-    across = hop(a, 0, 1)
     below, above = hop(a, 1, 0), hop(a, -1, 0)
-    weights = exchange_weight(weight, across, below)
-    two = hop(below, 1, 0)
-    across_below, across_above = hop(across, 1, 0), hop(across, -1, 0)
-    across_two = hop(across_above, -1, 0)
-    projected = None
-    for dy, near, far in (
-        (0, a, across),
-        (-1, below, across_below),
-        (1, above, across_above),
-        (2, two, across_two),
-    ):
-        where = jnp.stack([(y + dy + NY) % NY, z, core, xh, xl]).astype(jnp.int32)
-        projected = project(where, near, far, weights, projected)
+    across_below, across_above, across = hop(a, 1, 1), hop(a, -1, 1), hop(a, 0, 1)
+    two, across_two = hop(below, 1, 0), hop(across_above, -1, 0)
+    weights = exchange_weight(weight, below, above, across_below, across_above, across)
+    pairs = [(0, a, across), (-1, below, across_below), (1, above, across_above)]
+    projected = project(here, weights, pairs, None)
+    projected = project(here, weights, [(2, two, across_two)], projected)
     return (attended, projected)
 
 

time: 230 us -> 209 us (0.909)
  the two profiles are of different devices: /device:TPU:6 before, /device:TPU:231 now
where the time goes in v1:
time: 209 us; the launch traced here: 208 us
  starting transfers between devices  108 us (52%)
  waiting for transfers between devices  50.5 us (24%)
  Pallas kernels  22.5 us (11%)
  between operations  14.6 us (7%)
  local copies, waits for them, and re-layouts  10.5 us (5%)
    ppermute x16, starting transfers between devices, ring(): return lax.ppermute(value, 'z', [(i, (i + steps) % NZ) for i in range(NZ)])  54.5 us
    ppermute x16, waiting for transfers between devices, ring(): return lax.ppermute(value, 'z', [(i, (i + steps) % NZ) for i in range(NZ)])  30.1 us
    ppermute x5, starting transfers between devices, swap(): return lax.ppermute(value, axis, [(0, 1), (1, 0)])  25.3 us
    ppermute x7, starting transfers between devices, hop(): return lax.ppermute(block, 'tp', perm)  22.5 us
    ppermute x7, waiting for transfers between devices, hop(): return lax.ppermute(block, 'tp', perm)  13.1 us
    pallas_call x9, Pallas kernels, attend(): pl.pallas_call(functools.partial(attend_kernel, visits, state is None), o...  11.1 us
    unnamed x34, local copies, waits for them, and re-layouts  10.4 us
    ppermute x5, waiting for transfers between devices, swap(): return lax.ppermute(value, axis, [(0, 1), (1, 0)])  7.36 us
  transfers between devices with their start and end apart: 30, of which 14 were waited for; matrix products, arithmetic and copies ran while one was open for 2% of the time, Pallas kernels for 10%

profile of v1, /device:TPU:231, one launch (start us, length us, event | category | flops | bytes accessed | tf_op | source)
XLA Modules:
  0.0 207.9 jit_solution(11595461085472595400)
XLA Ops:
  10.6 3.0 %collective-permute-start.1 = (bf16[448,128]{1,0:T(8,128)(2,1)S(1)}, bf16[448,128]{1,0:T(8,128)(2,1)S(1)}, u32[]{:S(2)}, u32[]{:S(2)}) collective-permute-start(bf16[448,128]{1,0:T(8,128)(2,1)S(1)} %pad_maximum_fusion), channel_id=1, source_target_pairs={{0,256},{256,0},{1,257},{257,1},{2,258},{258,2},{3,259},{259,3},{4... | collective-permute-start | bytes 344072 | tf_op jit(solution)/shard_map/ppermute | solution.py:193
  15.3 3.5 %collective-permute-done.1 = bf16[448,128]{1,0:T(8,128)(2,1)S(1)} collective-permute-done((bf16[448,128]{1,0:T(8,128)(2,1)S(1)}, bf16[448,128]{1,0:T(8,128)(2,1)S(1)}, u32[]{:S(2)}, u32[]{:S(2)}) %collective-permute-start.1) | collective-permute-done | bytes 114720 | tf_op jit(solution)/shard_map/ppermute | solution.py:193
  18.8 4.8 %collective-permute-start.2 = (bf16[896,128]{1,0:T(8,128)(2,1)S(1)}, bf16[896,128]{1,0:T(8,128)(2,1)S(1)}, u32[]{:S(2)}, u32[]{:S(2)}) collective-permute-start(bf16[896,128]{1,0:T(8,128)(2,1)S(1)} %constant_dynamic-update-slice_fusion.refs_0_), channel_id=1, source_target_pairs={{0,16},{16,32},{32,48},{48,64},{64,80},{80,96},{96,112},{112,128},... | collective-permute-start | bytes 688136 | tf_op jit(solution)/shard_map/ppermute | solution.py:197
  29.9 5.4 %all-to-all-start = ((bf16[8,2,3200]{2,1,0:T(2,128)(2,1)}), bf16[8,2,3200]{2,1,0:T(2,128)(2,1)S(1)}, u32[]{:S(2)}, u32[]{:S(2)}) async-start(bf16[8,2,3200]{2,1,0:T(2,128)(2,1)} %shard_map.78), calls=%async_computation | async-start | bytes 204800 | tf_op jit(solution)/shard_map/all_to_all | solution.py:235
  37.8 5.3 %collective-permute-start.3 = (bf16[896,128]{1,0:T(8,128)(2,1)S(1)}, bf16[896,128]{1,0:T(8,128)(2,1)S(1)}, u32[]{:S(2)}, u32[]{:S(2)}) collective-permute-start(bf16[896,128]{1,0:T(8,128)(2,1)S(1)} %copy-done.12), channel_id=1, source_target_pairs={{0,16},{16,32},{32,48},{48,64},{64,80},{80,96},{96,112},{112,128},... | collective-permute-start | bytes 688136 | tf_op jit(solution)/shard_map/ppermute | solution.py:197
  45.1 3.0 %collective-permute-start.24 = (bf16[8,2,3200]{2,1,0:T(2,128)(2,1)S(1)}, bf16[8,2,3200]{2,1,0:T(2,128)(2,1)S(1)}, u32[]{:S(2)}, u32[]{:S(2)}) collective-permute-start(bf16[8,2,3200]{2,1,0:T(2,128)(2,1)S(1)} %all-to-all-done.mine_ref), channel_id=1, source_target_pairs={{0,256},{256,0},{1,257},{257,1},{2,258},{258,2},{3,259},{259,3},{4... | collective-permute-start | bytes 307208 | tf_op jit(solution)/shard_map/ppermute | solution.py:193
  54.5 4.6 %collective-permute-start.4 = (bf16[896,128]{1,0:T(8,128)(2,1)S(1)}, bf16[896,128]{1,0:T(8,128)(2,1)S(1)}, u32[]{:S(2)}, u32[]{:S(2)}) collective-permute-start(bf16[896,128]{1,0:T(8,128)(2,1)S(1)} %collective-permute-done.3.refs_0_), channel_id=1, source_target_pairs={{0,16},{16,32},{32,48},{48,64},{64,80},{80,96},{96,112},{112,128},... | collective-permute-start | bytes 688136 | tf_op jit(solution)/shard_map/ppermute | solution.py:197
  62.0 5.0 %collective-permute-start.5 = (bf16[896,128]{1,0:T(8,128)(2,1)S(1)}, bf16[896,128]{1,0:T(8,128)(2,1)S(1)}, u32[]{:S(2)}, u32[]{:S(2)}) collective-permute-start(bf16[896,128]{1,0:T(8,128)(2,1)S(1)} %collective-permute-done.4.refs_0_), channel_id=1, source_target_pairs={{0,16},{16,32},{32,48},{48,64},{64,80},{80,96},{96,112},{112,128},... | collective-permute-start | bytes 688136 | tf_op jit(solution)/shard_map/ppermute | solution.py:197
  69.9 5.0 %collective-permute-start.6 = (bf16[896,128]{1,0:T(8,128)(2,1)S(1)}, bf16[896,128]{1,0:T(8,128)(2,1)S(1)}, u32[]{:S(2)}, u32[]{:S(2)}) collective-permute-start(bf16[896,128]{1,0:T(8,128)(2,1)S(1)} %collective-permute-done.5.refs_0_), channel_id=1, source_target_pairs={{0,16},{16,32},{32,48},{48,64},{64,80},{80,96},{96,112},{112,128},... | collective-permute-start | bytes 688136 | tf_op jit(solution)/shard_map/ppermute | solution.py:197
  80.7 5.1 %collective-permute-start.7 = (bf16[896,128]{1,0:T(8,128)(2,1)S(1)}, bf16[896,128]{1,0:T(8,128)(2,1)S(1)}, u32[]{:S(2)}, u32[]{:S(2)}) collective-permute-start(bf16[896,128]{1,0:T(8,128)(2,1)S(1)} %collective-permute-done.6.refs_0_), channel_id=1, source_target_pairs={{0,16},{16,32},{32,48},{48,64},{64,80},{80,96},{96,112},{112,128},... | collective-permute-start | bytes 688136 | tf_op jit(solution)/shard_map/ppermute | solution.py:197
  85.8 4.0 %collective-permute-done.14.refs_1_ = bf16[896,128]{1,0:T(8,128)(2,1)S(1)} collective-permute-done((bf16[896,128]{1,0:T(8,128)(2,1)S(1)}, bf16[896,128]{1,0:T(8,128)(2,1)S(1)}, u32[]{:S(2)}, u32[]{:S(2)}) %collective-permute-start.14) | collective-permute-done | bytes 229408 | tf_op jit(solution)/shard_map/ppermute | solution.py:197
  93.8 4.8 %collective-permute-start.8 = (bf16[896,128]{1,0:T(8,128)(2,1)S(1)}, bf16[896,128]{1,0:T(8,128)(2,1)S(1)}, u32[]{:S(2)}, u32[]{:S(2)}) collective-permute-start(bf16[896,128]{1,0:T(8,128)(2,1)S(1)} %collective-permute-done.7.refs_0_), channel_id=1, source_target_pairs={{0,16},{16,32},{32,48},{48,64},{64,80},{80,96},{96,112},{112,128},... | collective-permute-start | bytes 688136 | tf_op jit(solution)/shard_map/ppermute | solution.py:197
  98.6 5.9 %collective-permute-done.15.refs_1_ = bf16[896,128]{1,0:T(8,128)(2,1)S(1)} collective-permute-done((bf16[896,128]{1,0:T(8,128)(2,1)S(1)}, bf16[896,128]{1,0:T(8,128)(2,1)S(1)}, u32[]{:S(2)}, u32[]{:S(2)}) %collective-permute-start.15) | collective-permute-done | bytes 229408 | tf_op jit(solution)/shard_map/ppermute | solution.py:197
  107.5 4.6 %collective-permute-start.9 = (bf16[448,128]{1,0:T(8,128)(2,1)S(1)}, bf16[448,128]{1,0:T(8,128)(2,1)S(1)}, u32[]{:S(2)}, u32[]{:S(2)}) collective-permute-start(bf16[448,128]{1,0:T(8,128)(2,1)S(1)} %slice.8), channel_id=1, source_target_pairs={{0,16},{16,32},{32,48},{48,64},{64,80},{80,96},{96,112},{112,128},... | collective-permute-start | bytes 344072 | tf_op jit(solution)/shard_map/ppermute | solution.py:197
  112.1 7.2 %collective-permute-done.16.refs_1_ = bf16[896,128]{1,0:T(8,128)(2,1)S(1)} collective-permute-done((bf16[896,128]{1,0:T(8,128)(2,1)S(1)}, bf16[896,128]{1,0:T(8,128)(2,1)S(1)}, u32[]{:S(2)}, u32[]{:S(2)}) %collective-permute-start.16) | collective-permute-done | bytes 229408 | tf_op jit(solution)/shard_map/ppermute | solution.py:197
  122.1 7.5 %collective-permute-done.17.refs_1_ = bf16[448,128]{1,0:T(8,128)(2,1)S(1)} collective-permute-done((bf16[448,128]{1,0:T(8,128)(2,1)S(1)}, bf16[448,128]{1,0:T(8,128)(2,1)S(1)}, u32[]{:S(2)}, u32[]{:S(2)}) %collective-permute-start.17) | collective-permute-done | bytes 114720 | tf_op jit(solution)/shard_map/ppermute | solution.py:197
  130.4 12.9 %collective-permute-start.18 = (f32[656,448]{1,0:T(8,128)S(1)}, f32[656,448]{1,0:T(8,128)S(1)}, u32[]{:S(2)}, u32[]{:S(2)}) collective-permute-start(f32[656,448]{1,0:T(8,128)S(1)} %shard_map.76.mine_ref), channel_id=1, source_target_pairs={{0,8},{8,0},{1,9},{9,1},{2,10},{10,2},{3,11},{11,3},{4,12},{12,4},... | collective-permute-start | bytes 3526664 | tf_op jit(solution)/shard_map/ppermute | solution.py:193
  147.9 4.3 %collective-permute-start.19 = (bf16[224,640]{1,0:T(8,128)(2,1)S(1)}, bf16[224,640]{1,0:T(8,128)(2,1)S(1)}, u32[]{:S(2)}, u32[]{:S(2)}) collective-permute-start(bf16[224,640]{1,0:T(8,128)(2,1)S(1)} %get-tuple-element.5.refs_0_), channel_id=1, source_target_pairs={{0,2},{1,3},{2,4},{3,5},{4,6},{5,7},{6,0},{7,1},{8,10},{9,11},{10,... | collective-permute-start | bytes 860168 | tf_op jit(solution)/shard_map/ppermute | solution.py:204
  157.3 4.4 %collective-permute-start.22 = (bf16[224,640]{1,0:T(8,128)(2,1)S(1)}, bf16[224,640]{1,0:T(8,128)(2,1)S(1)}, u32[]{:S(2)}, u32[]{:S(2)}) collective-permute-start(bf16[224,640]{1,0:T(8,128)(2,1)S(1)} %get-tuple-element.5.refs_0_), channel_id=1, source_target_pairs={{0,7},{1,6},{2,1},{3,0},{4,3},{5,2},{6,5},{7,4},{8,15},{9,14},{10,... | collective-permute-start | bytes 860168 | tf_op jit(solution)/shard_map/ppermute | solution.py:204
  165.8 4.8 %collective-permute-done.22.refs_3_.refs_5_ = bf16[224,640]{1,0:T(8,128)(2,1)S(1)} collective-permute-done((bf16[224,640]{1,0:T(8,128)(2,1)S(1)}, bf16[224,640]{1,0:T(8,128)(2,1)S(1)}, u32[]{:S(2)}, u32[]{:S(2)}) %collective-permute-start.22) | collective-permute-done | bytes 286752 | tf_op jit(solution)/shard_map/ppermute | solution.py:204
  170.6 6.2 %collective-permute-done.23.refs_4_.refs_3_ = bf16[224,640]{1,0:T(8,128)(2,1)S(1)} collective-permute-done((bf16[224,640]{1,0:T(8,128)(2,1)S(1)}, bf16[224,640]{1,0:T(8,128)(2,1)S(1)}, u32[]{:S(2)}, u32[]{:S(2)}) %collective-permute-start.23) | collective-permute-done | bytes 286752 | tf_op jit(solution)/shard_map/ppermute | solution.py:204
  177.5 3.7 %collective-permute-start.25 = (bf16[128,12800]{1,0:T(8,128)(2,1)}, bf16[128,12800]{1,0:T(8,128)(2,1)S(1)}, u32[]{:S(2)}, u32[]{:S(2)}) collective-permute-start(bf16[128,12800]{1,0:T(8,128)(2,1)} %shard_map.80.own_ref), channel_id=1, source_target_pairs={{0,8},{8,0},{1,9},{9,1},{2,10},{10,2},{3,11},{11,3},{4,12},{12,4},... | collective-permute-start | bytes 9830408 | tf_op jit(solution)/shard_map/ppermute | solution.py:193
  183.4 4.6 %collective-permute-start.27 = (bf16[224,640]{1,0:T(8,128)(2,1)}, bf16[224,640]{1,0:T(8,128)(2,1)S(1)}, u32[]{:S(2)}, u32[]{:S(2)}) collective-permute-start(bf16[224,640]{1,0:T(8,128)(2,1)} %copy-done.5), channel_id=1, source_target_pairs={{0,6},{1,7},{2,0},{3,1},{4,2},{5,3},{6,4},{7,5},{8,14},{9,15},{10,... | collective-permute-start | bytes 860168 | tf_op jit(solution)/shard_map/ppermute | solution.py:204
  194.8 3.7 %shard_map.81.refs_2_ = f32[224,640]{1,0:T(8,128)S(1)} custom-call(s32[5]{0:T(128)S(1)} %stack.23.here_ref, bf16[128,12800]{1,0:T(8,128)(2,1)S(1)} %copy-done, bf16[128,12800]{1,0:T(8,128)(2,1)S(1)} %collective-permute-done.25.other_ref, bf16[224,640]{1,0:T(8,128)(2,1)S(1)} %get-tuple-element.5.refs_0_, bf16[224,640]{1,0:T(8,128)(2,1)S(1)} %copy-done.2, ...), custom_call_target="tpu_custom_call" | custom-call | flops 1541406720 | bytes 6553600 | tf_op jit(solution)/shard_map/pallas_call | solution.py:178
  (92 shorter events, 69.8 us)
Async XLA Ops:
  7.2 18.4 %collective-permute-start = (bf16[224,640]{1,0:T(8,128)(2,1)}, bf16[224,640]{1,0:T(8,128)(2,1)S(1)}, u32[]{:S(2)}, u32[]{:S(2)}) collective-permute-start(bf16[224,640]{1,0:T(8,128)(2,1)} %param.5), channel_id=1, source_target_pairs={{0,8},{8,0},{1,9},{9,1},{2,10},{10,2},{3,11},{11,3},{4,12},{12,4},... | collective-permute-start | bytes 860168 | tf_op jit(solution)/shard_map/ppermute | solution.py:193
  18.8 8.9 %collective-permute-start.2 = (bf16[896,128]{1,0:T(8,128)(2,1)S(1)}, bf16[896,128]{1,0:T(8,128)(2,1)S(1)}, u32[]{:S(2)}, u32[]{:S(2)}) collective-permute-start(bf16[896,128]{1,0:T(8,128)(2,1)S(1)} %constant_dynamic-update-slice_fusion.refs_0_), channel_id=1, source_target_pairs={{0,16},{16,32},{32,48},{48,64},{64,80},{80,96},{96,112},{112,128},... | collective-permute-start | bytes 688136 | tf_op jit(solution)/shard_map/ppermute | solution.py:197
  23.7 19.5 %collective-permute-start.10 = (bf16[896,128]{1,0:T(8,128)(2,1)S(1)}, bf16[896,128]{1,0:T(8,128)(2,1)S(1)}, u32[]{:S(2)}, u32[]{:S(2)}) collective-permute-start(bf16[896,128]{1,0:T(8,128)(2,1)S(1)} %constant_dynamic-update-slice_fusion.refs_0_), channel_id=1, source_target_pairs={{0,240},{16,0},{32,16},{48,32},{64,48},{80,64},{96,80},{112,96},{1... | collective-permute-start | bytes 688136 | tf_op jit(solution)/shard_map/ppermute | solution.py:197
  29.9 15.2 %all-to-all-start = ((bf16[8,2,3200]{2,1,0:T(2,128)(2,1)}), bf16[8,2,3200]{2,1,0:T(2,128)(2,1)S(1)}, u32[]{:S(2)}, u32[]{:S(2)}) async-start(bf16[8,2,3200]{2,1,0:T(2,128)(2,1)} %shard_map.78), calls=%async_computation | async-start | bytes 204800 | tf_op jit(solution)/shard_map/all_to_all | solution.py:235
  35.3 141.5 %all-gather.2.cloned.1.call-start = ((), (), s32[]{:S(2)}) async-start(), calls=%async_computation.1 | async-start | bytes 3481600 | tf_op jit(solution)/shard_map/all_gather | solution.py:242
  37.8 16.6 %collective-permute-start.3 = (bf16[896,128]{1,0:T(8,128)(2,1)S(1)}, bf16[896,128]{1,0:T(8,128)(2,1)S(1)}, u32[]{:S(2)}, u32[]{:S(2)}) collective-permute-start(bf16[896,128]{1,0:T(8,128)(2,1)S(1)} %copy-done.12), channel_id=1, source_target_pairs={{0,16},{16,32},{32,48},{48,64},{64,80},{80,96},{96,112},{112,128},... | collective-permute-start | bytes 688136 | tf_op jit(solution)/shard_map/ppermute | solution.py:197
  43.2 15.9 %collective-permute-start.11 = (bf16[896,128]{1,0:T(8,128)(2,1)S(1)}, bf16[896,128]{1,0:T(8,128)(2,1)S(1)}, u32[]{:S(2)}, u32[]{:S(2)}) collective-permute-start(bf16[896,128]{1,0:T(8,128)(2,1)S(1)} %collective-permute-done.10.refs_1_), channel_id=1, source_target_pairs={{0,240},{16,0},{32,16},{48,32},{64,48},{80,64},{96,80},{112,96},{1... | collective-permute-start | bytes 688136 | tf_op jit(solution)/shard_map/ppermute | solution.py:197
  69.9 10.8 %collective-permute-start.6 = (bf16[896,128]{1,0:T(8,128)(2,1)S(1)}, bf16[896,128]{1,0:T(8,128)(2,1)S(1)}, u32[]{:S(2)}, u32[]{:S(2)}) collective-permute-start(bf16[896,128]{1,0:T(8,128)(2,1)S(1)} %collective-permute-done.5.refs_0_), channel_id=1, source_target_pairs={{0,16},{16,32},{32,48},{48,64},{64,80},{80,96},{96,112},{112,128},... | collective-permute-start | bytes 688136 | tf_op jit(solution)/shard_map/ppermute | solution.py:197
  75.0 14.9 %collective-permute-start.14 = (bf16[896,128]{1,0:T(8,128)(2,1)S(1)}, bf16[896,128]{1,0:T(8,128)(2,1)S(1)}, u32[]{:S(2)}, u32[]{:S(2)}) collective-permute-start(bf16[896,128]{1,0:T(8,128)(2,1)S(1)} %collective-permute-done.13.refs_1_), channel_id=1, source_target_pairs={{0,240},{16,0},{32,16},{48,32},{64,48},{80,64},{96,80},{112,96},{1... | collective-permute-start | bytes 688136 | tf_op jit(solution)/shard_map/ppermute | solution.py:197
  80.7 13.1 %collective-permute-start.7 = (bf16[896,128]{1,0:T(8,128)(2,1)S(1)}, bf16[896,128]{1,0:T(8,128)(2,1)S(1)}, u32[]{:S(2)}, u32[]{:S(2)}) collective-permute-start(bf16[896,128]{1,0:T(8,128)(2,1)S(1)} %collective-permute-done.6.refs_0_), channel_id=1, source_target_pairs={{0,16},{16,32},{32,48},{48,64},{64,80},{80,96},{96,112},{112,128},... | collective-permute-start | bytes 688136 | tf_op jit(solution)/shard_map/ppermute | solution.py:197
  89.9 14.7 %collective-permute-start.15 = (bf16[896,128]{1,0:T(8,128)(2,1)S(1)}, bf16[896,128]{1,0:T(8,128)(2,1)S(1)}, u32[]{:S(2)}, u32[]{:S(2)}) collective-permute-start(bf16[896,128]{1,0:T(8,128)(2,1)S(1)} %collective-permute-done.14.refs_1_), channel_id=1, source_target_pairs={{0,240},{16,0},{32,16},{48,32},{64,48},{80,64},{96,80},{112,96},{1... | collective-permute-start | bytes 688136 | tf_op jit(solution)/shard_map/ppermute | solution.py:197
  93.8 13.7 %collective-permute-start.8 = (bf16[896,128]{1,0:T(8,128)(2,1)S(1)}, bf16[896,128]{1,0:T(8,128)(2,1)S(1)}, u32[]{:S(2)}, u32[]{:S(2)}) collective-permute-start(bf16[896,128]{1,0:T(8,128)(2,1)S(1)} %collective-permute-done.7.refs_0_), channel_id=1, source_target_pairs={{0,16},{16,32},{32,48},{48,64},{64,80},{80,96},{96,112},{112,128},... | collective-permute-start | bytes 688136 | tf_op jit(solution)/shard_map/ppermute | solution.py:197
  104.5 14.8 %collective-permute-start.16 = (bf16[896,128]{1,0:T(8,128)(2,1)S(1)}, bf16[896,128]{1,0:T(8,128)(2,1)S(1)}, u32[]{:S(2)}, u32[]{:S(2)}) collective-permute-start(bf16[896,128]{1,0:T(8,128)(2,1)S(1)} %collective-permute-done.15.refs_1_), channel_id=1, source_target_pairs={{0,240},{16,0},{32,16},{48,32},{64,48},{80,64},{96,80},{112,96},{1... | collective-permute-start | bytes 688136 | tf_op jit(solution)/shard_map/ppermute | solution.py:197
  107.5 14.6 %collective-permute-start.9 = (bf16[448,128]{1,0:T(8,128)(2,1)S(1)}, bf16[448,128]{1,0:T(8,128)(2,1)S(1)}, u32[]{:S(2)}, u32[]{:S(2)}) collective-permute-start(bf16[448,128]{1,0:T(8,128)(2,1)S(1)} %slice.8), channel_id=1, source_target_pairs={{0,16},{16,32},{32,48},{48,64},{64,80},{80,96},{96,112},{112,128},... | collective-permute-start | bytes 344072 | tf_op jit(solution)/shard_map/ppermute | solution.py:197
  119.3 10.3 %collective-permute-start.17 = (bf16[448,128]{1,0:T(8,128)(2,1)S(1)}, bf16[448,128]{1,0:T(8,128)(2,1)S(1)}, u32[]{:S(2)}, u32[]{:S(2)}) collective-permute-start(bf16[448,128]{1,0:T(8,128)(2,1)S(1)} %slice.9), channel_id=1, source_target_pairs={{0,240},{16,0},{32,16},{48,32},{64,48},{80,64},{96,80},{112,96},{1... | collective-permute-start | bytes 344072 | tf_op jit(solution)/shard_map/ppermute | solution.py:197
  130.4 15.6 %collective-permute-start.18 = (f32[656,448]{1,0:T(8,128)S(1)}, f32[656,448]{1,0:T(8,128)S(1)}, u32[]{:S(2)}, u32[]{:S(2)}) collective-permute-start(f32[656,448]{1,0:T(8,128)S(1)} %shard_map.76.mine_ref), channel_id=1, source_target_pairs={{0,8},{8,0},{1,9},{9,1},{2,10},{10,2},{3,11},{11,3},{4,12},{12,4},... | collective-permute-start | bytes 3526664 | tf_op jit(solution)/shard_map/ppermute | solution.py:193
  147.9 15.8 %collective-permute-start.19 = (bf16[224,640]{1,0:T(8,128)(2,1)S(1)}, bf16[224,640]{1,0:T(8,128)(2,1)S(1)}, u32[]{:S(2)}, u32[]{:S(2)}) collective-permute-start(bf16[224,640]{1,0:T(8,128)(2,1)S(1)} %get-tuple-element.5.refs_0_), channel_id=1, source_target_pairs={{0,2},{1,3},{2,4},{3,5},{4,6},{5,7},{6,0},{7,1},{8,10},{9,11},{10,... | collective-permute-start | bytes 860168 | tf_op jit(solution)/shard_map/ppermute | solution.py:204
  152.1 11.6 %collective-permute-start.20 = (bf16[224,640]{1,0:T(8,128)(2,1)S(1)}, bf16[224,640]{1,0:T(8,128)(2,1)S(1)}, u32[]{:S(2)}, u32[]{:S(2)}) collective-permute-start(bf16[224,640]{1,0:T(8,128)(2,1)S(1)} %get-tuple-element.5.refs_0_), channel_id=1, source_target_pairs={{0,6},{1,7},{2,0},{3,1},{4,2},{5,3},{6,4},{7,5},{8,14},{9,15},{10,... | collective-permute-start | bytes 860168 | tf_op jit(solution)/shard_map/ppermute | solution.py:204
  154.3 11.4 %collective-permute-start.21 = (bf16[224,640]{1,0:T(8,128)(2,1)S(1)}, bf16[224,640]{1,0:T(8,128)(2,1)S(1)}, u32[]{:S(2)}, u32[]{:S(2)}) collective-permute-start(bf16[224,640]{1,0:T(8,128)(2,1)S(1)} %get-tuple-element.5.refs_0_), channel_id=1, source_target_pairs={{0,3},{1,2},{2,5},{3,4},{4,7},{5,6},{6,1},{7,0},{8,11},{9,10},{10,... | collective-permute-start | bytes 860168 | tf_op jit(solution)/shard_map/ppermute | solution.py:204
  157.3 13.3 %collective-permute-start.22 = (bf16[224,640]{1,0:T(8,128)(2,1)S(1)}, bf16[224,640]{1,0:T(8,128)(2,1)S(1)}, u32[]{:S(2)}, u32[]{:S(2)}) collective-permute-start(bf16[224,640]{1,0:T(8,128)(2,1)S(1)} %get-tuple-element.5.refs_0_), channel_id=1, source_target_pairs={{0,7},{1,6},{2,1},{3,0},{4,3},{5,2},{6,5},{7,4},{8,15},{9,14},{10,... | collective-permute-start | bytes 860168 | tf_op jit(solution)/shard_map/ppermute | solution.py:204
  161.8 15.0 %collective-permute-start.23 = (bf16[224,640]{1,0:T(8,128)(2,1)S(1)}, bf16[224,640]{1,0:T(8,128)(2,1)S(1)}, u32[]{:S(2)}, u32[]{:S(2)}) collective-permute-start(bf16[224,640]{1,0:T(8,128)(2,1)S(1)} %get-tuple-element.5.refs_0_), channel_id=1, source_target_pairs={{0,1},{1,0},{2,3},{3,2},{4,5},{5,4},{6,7},{7,6},{8,9},{9,8},{10,11... | collective-permute-start | bytes 860168 | tf_op jit(solution)/shard_map/ppermute | solution.py:204
  177.5 10.5 %collective-permute-start.25 = (bf16[128,12800]{1,0:T(8,128)(2,1)}, bf16[128,12800]{1,0:T(8,128)(2,1)S(1)}, u32[]{:S(2)}, u32[]{:S(2)}) collective-permute-start(bf16[128,12800]{1,0:T(8,128)(2,1)} %shard_map.80.own_ref), channel_id=1, source_target_pairs={{0,8},{8,0},{1,9},{9,1},{2,10},{10,2},{3,11},{11,3},{4,12},{12,4},... | collective-permute-start | bytes 9830408 | tf_op jit(solution)/shard_map/ppermute | solution.py:193
  181.3 17.2 %collective-permute-start.26 = (bf16[224,640]{1,0:T(8,128)(2,1)}, bf16[224,640]{1,0:T(8,128)(2,1)S(1)}, u32[]{:S(2)}, u32[]{:S(2)}) collective-permute-start(bf16[224,640]{1,0:T(8,128)(2,1)} %copy-done.1), channel_id=1, source_target_pairs={{0,2},{1,3},{2,4},{3,5},{4,6},{5,7},{6,0},{7,1},{8,10},{9,11},{10,... | collective-permute-start | bytes 860168 | tf_op jit(solution)/shard_map/ppermute | solution.py:204
  183.4 15.1 %collective-permute-start.27 = (bf16[224,640]{1,0:T(8,128)(2,1)}, bf16[224,640]{1,0:T(8,128)(2,1)S(1)}, u32[]{:S(2)}, u32[]{:S(2)}) collective-permute-start(bf16[224,640]{1,0:T(8,128)(2,1)} %copy-done.5), channel_id=1, source_target_pairs={{0,6},{1,7},{2,0},{3,1},{4,2},{5,3},{6,4},{7,5},{8,14},{9,15},{10,... | collective-permute-start | bytes 860168 | tf_op jit(solution)/shard_map/ppermute | solution.py:204
  (22 other events, 135.1 us)
Sparse Core Ops, SparseCore 0:
  54.6 79.4 all-gather.1

commit v2 on v1

v2 whole, which is shorter than its diff:
```python
import functools
import math

import jax
import jax.numpy as jnp
from jax import lax
from jax.experimental import pallas as pl
from jax.experimental.pallas import tpu as pltpu
from jax.sharding import Mesh, PartitionSpec as P

HD = 128
XH, NZ, NC, NY, NX = 2, 16, 2, 4, 2
ROWS = 224
QROWS = NC * ROWS
HEADS = 5
WIDE = HEADS * HD
STATE = WIDE + 16
DEEP = 2 * HD
FLOOR = -1e29
MASKED = -1e30
NEG = (((1,), (1,)), ((), ()))
VMEM = 40 * 1024 * 1024
F32 = jnp.float32
BF16 = jnp.bfloat16


def attend_kernel(here_ref, len_ref, q_ref, own_ref, far_ref, state):
    state[:WIDE] = jnp.zeros((WIDE, QROWS), F32)
    state[WIDE : WIDE + 8] = jnp.full((8, QROWS), FLOOR, F32)
    state[WIDE + 8 :] = jnp.zeros((8, QROWS), F32)
    z, core, xh = here_ref[0], here_ref[1], here_ref[2]
    q_start = (xh * NZ + z) * QROWS
    q_last = q_start + QROWS - 1
    q_pos = q_start + lax.broadcasted_iota(jnp.int32, (1, QROWS), 1)
    doc_start = jnp.zeros((1, QROWS), jnp.int32)
    low, high, end = jnp.int32(0), jnp.int32(0), jnp.int32(0)
    for i in range(len_ref.shape[0]):
        end = end + len_ref[i]
        doc_start = jnp.where(q_pos >= end, end, doc_start)
        low = jnp.where(q_start >= end, end, low)
        high = jnp.where(q_last >= end, end, high)
    scale = math.log2(math.e) / math.sqrt(HD)

    def visit(keys, values, k_start, partial):
        values = values.T
        if partial:
            k_pos = k_start + lax.broadcasted_iota(jnp.int32, (ROWS, QROWS), 0)
            allowed = (k_pos >= doc_start) & (k_pos <= q_pos)
        for h in range(HEADS):
            rows = slice(h * HD, (h + 1) * HD)
            scores = scale * lax.dot_general(keys, q_ref[:, rows], NEG, preferred_element_type=F32)
            if partial:
                scores = jnp.where(allowed, scores, MASKED)
            old = state[WIDE + h : WIDE + h + 1]
            new = jnp.maximum(old, jnp.max(scores, axis=0, keepdims=True))
            fix = jnp.exp2(old - new)
            weights = jnp.exp2(scores - new)
            state[WIDE + h : WIDE + h + 1] = new
            total = slice(WIDE + 8 + h, WIDE + 9 + h)
            state[total] = state[total] * fix + jnp.sum(weights, axis=0, keepdims=True)
            mixed = jnp.dot(values, weights.astype(BF16), preferred_element_type=F32)
            state[rows] = state[rows] * fix + mixed

    visit(own_ref[:ROWS], own_ref[ROWS:], q_start + core * ROWS, True)

    @pl.loop(0, NZ)
    def _(source):
        plane = jnp.where(source < z, xh, xh ^ 1)
        k_start = (plane * NZ + source) * QROWS + core * ROWS
        needed = (k_start + ROWS > low) & (k_start <= q_last)
        whole = (k_start >= high) & (k_start + ROWS <= q_start + 1)

        def far(partial):
            visit(far_ref[source, :ROWS], far_ref[source, ROWS:], k_start, partial)

        pl.when(needed & whole)(functools.partial(far, False))
        pl.when(needed & jnp.logical_not(whole))(functools.partial(far, True))


def attend(here, lengths, q, own, far):
    smem = pl.BlockSpec(memory_space=pltpu.SMEM)
    vmem = pl.BlockSpec(memory_space=pltpu.VMEM)
    pairs = NZ * QROWS * ROWS * HEADS
    return pl.pallas_call(
        attend_kernel,
        out_shape=jax.ShapeDtypeStruct((STATE, QROWS), F32),
        in_specs=[smem, smem, vmem, vmem, vmem],
        out_specs=vmem,
        cost_estimate=pl.CostEstimate(
            flops=pairs * HD * 4, bytes_accessed=STATE * QROWS * 8, transcendentals=pairs
        ),
        compiler_params=pltpu.CompilerParams(vmem_limit_bytes=VMEM),
    )(here, lengths, q, own, far)


def merge_kernel(here_ref, mine_ref, other_ref, out_ref, a_ref, full):
    for h in range(HEADS):
        rows = slice(h * HD, (h + 1) * HD)
        top = slice(WIDE + h, WIDE + h + 1)
        total = slice(WIDE + 8 + h, WIDE + 9 + h)
        m = jnp.maximum(mine_ref[top], other_ref[top])
        mine, other = jnp.exp2(mine_ref[top] - m), jnp.exp2(other_ref[top] - m)
        den = mine * mine_ref[total] + other * other_ref[total]
        mixed = (mine_ref[rows] * mine + other_ref[rows] * other) / den
        full[:, rows] = mixed.T
    own = full[pl.ds(pl.multiple_of(here_ref[1] * ROWS, ROWS), ROWS)]
    out_ref[...] = own
    a_ref[...] = own.astype(BF16)


def merge(here, mine, other):
    vmem = pl.BlockSpec(memory_space=pltpu.VMEM)
    return pl.pallas_call(
        merge_kernel,
        out_shape=(
            jax.ShapeDtypeStruct((ROWS, WIDE), F32),
            jax.ShapeDtypeStruct((ROWS, WIDE), BF16),
        ),
        in_specs=[pl.BlockSpec(memory_space=pltpu.SMEM), vmem, vmem],
        out_specs=(vmem, vmem),
        scratch_shapes=[pltpu.VMEM((QROWS, WIDE), F32)],
        cost_estimate=pl.CostEstimate(
            flops=QROWS * WIDE * 100, bytes_accessed=STATE * QROWS * 12, transcendentals=QROWS * 16
        ),
        compiler_params=pltpu.CompilerParams(vmem_limit_bytes=VMEM),
    )(here, mine, other)


def project_kernel(here_ref, own_ref, other_ref, a_ref, out_ref):
    core, xh = here_ref[1], here_ref[2]
    k = lax.broadcasted_iota(jnp.int32, (DEEP, DEEP), 0)
    g = lax.broadcasted_iota(jnp.int32, (DEEP, DEEP), 1)
    row = g & (HD - 1)
    d = (xh ^ ((row >> 1) & 1)) * (NZ * 4) + (row >> 3) * 4 + (core ^ (g >> 7)) * 2 + (row & 1)
    match = ((k & (HD - 1)) == d) & (((row >> 2) & 1) == (k >> 7))
    perm = jnp.where(match, 1.0, 0.0).astype(BF16)
    total = jnp.zeros((ROWS, WIDE), F32)
    for y in range(NY):
        for h in range(HEADS):
            heads = slice(h * HD, (h + 1) * HD)
            columns = slice((y * HEADS + h) * WIDE, (y * HEADS + h + 1) * WIDE)
            both = jnp.concatenate([a_ref[y * NX + x, :, heads] for x in range(NX)], axis=1)
            moved = jnp.dot(both, perm, preferred_element_type=F32).astype(BF16)
            weight = jnp.concatenate([own_ref[:, columns], other_ref[:, columns]], axis=0)
            total += jnp.dot(moved, weight, preferred_element_type=F32)
    out_ref[...] = total


def project(here, weights, a):
    vmem = pl.BlockSpec(memory_space=pltpu.VMEM)
    return pl.pallas_call(
        project_kernel,
        out_shape=jax.ShapeDtypeStruct((ROWS, WIDE), F32),
        in_specs=[pl.BlockSpec(memory_space=pltpu.SMEM), vmem, vmem, vmem],
        out_specs=vmem,
        cost_estimate=pl.CostEstimate(
            flops=2 * NY * ROWS * DEEP * HEADS * (WIDE + DEEP),
            bytes_accessed=DEEP * NY * HEADS * WIDE * 2,
            transcendentals=0,
        ),
        compiler_params=pltpu.CompilerParams(vmem_limit_bytes=VMEM),
    )(here, *weights, a)


def swap(value, axis):
    return lax.ppermute(value, axis, [(0, 1), (1, 0)])


def split_kernel(after_ref, weight_ref, out_ref):
    for j in range(NY * NX):
        for h in range(HEADS):
            out_ref[j, :, h * WIDE : (h + 1) * WIDE] = weight_ref[h, :, j * WIDE : (j + 1) * WIDE]


def stack_kernel(mine_ref, other_ref, out_ref):
    for e in range(NX):
        for rel, ref in enumerate((mine_ref, other_ref)):
            row = e * 4 + rel * 2
            for y in range(NY):
                lanes = slice(y * HEADS * WIDE, (y + 1) * HEADS * WIDE)
                out_ref[row : row + 2, lanes] = ref[y * NX + e]


def pass_kernel(*refs):
    pass


def gather_weight(out_weight, after):
    whole = pl.BlockSpec(memory_space=pl.ANY)
    vmem = pl.BlockSpec(memory_space=pltpu.VMEM)
    split = pl.pallas_call(
        split_kernel,
        out_shape=jax.ShapeDtypeStruct((NY * NX, 2, HEADS * WIDE), BF16),
        in_specs=[whole, vmem],
        out_specs=vmem,
    )(after, out_weight)
    split = lax.all_to_all(split, "tp", 0, 0)
    rows = pl.pallas_call(
        stack_kernel,
        out_shape=jax.ShapeDtypeStruct((8, NY * HEADS * WIDE), BF16),
        in_specs=[vmem, vmem],
        out_specs=vmem,
    )(split, swap(split, "xh"))
    return lax.all_gather(rows, "z", axis=0, tiled=True)


def exchange_weight(own, *after):
    whole = pl.BlockSpec(memory_space=pl.ANY)
    hbm = pl.BlockSpec(memory_space=pltpu.HBM)
    own = pl.pallas_call(
        pass_kernel,
        out_shape=jax.ShapeDtypeStruct(own.shape, own.dtype),
        in_specs=[whole] * len(after) + [hbm],
        out_specs=hbm,
        input_output_aliases={len(after): 0},
    )(*after, own)
    return own, swap(own, "core")


def body(queries, keys, values, doc_lengths, out_weight):
    xh, z, core = (lax.axis_index(name) for name in ("xh", "z", "core"))
    here = jnp.stack([z, core, xh]).astype(jnp.int32)
    own = jnp.concatenate([keys, values], axis=0)
    other = swap(own, "xh")
    above = jnp.arange(NZ, dtype=jnp.int32)[:, None, None] > z
    blocks = jnp.where(above, own[None], other[None])
    far = lax.all_to_all(blocks, "z", 0, 0)
    weight = gather_weight(out_weight, blocks)
    other_q = swap(queries, "core")
    q = jnp.where(core == 0, jnp.concatenate([queries, other_q]), jnp.concatenate([other_q, queries]))
    state = attend(here, doc_lengths, q, own, far)
    attended, a = merge(here, state, swap(state, "core"))
    sources = lax.all_to_all(jnp.broadcast_to(a[None], (NY * NX, ROWS, WIDE)), "tp", 0, 0)
    projected = project(here, exchange_weight(weight, a), sources)
    return (attended, projected)


def solution(mesh):
    fine = Mesh(mesh.devices.reshape(XH, NZ, NC, NY * NX), ("xh", "z", "core", "tp"))
    ctx = ("xh", "z", "core")
    in_specs = (P(ctx, "tp"), P(ctx, "tp"), P(ctx, "tp"), P(), P("tp", ctx, None))
    out_specs = (P(ctx, "tp"), P(ctx, "tp"))
    return jax.shard_map(body, mesh=fine, in_specs=in_specs, out_specs=out_specs, check_vma=False)
```

time: 209 us -> 224 us (1.072)
  the two profiles are of different devices: /device:TPU:231 before, /device:TPU:6 now
where the time goes in v2:
time: 224 us; the launch traced here: 223 us
  waiting for transfers between devices  118 us (53%)
  blocking collectives  44.9 us (20%)
  starting transfers between devices  27.4 us (12%)
  between operations  14.2 us (6%)
  Pallas kernels  13.4 us (6%)
  local copies, waits for them, and re-layouts  3.2 us (1%)
    all_to_all x1, waiting for transfers between devices, body(): far = lax.all_to_all(blocks, 'z', 0, 0)  79.2 us
    all_to_all x1, blocking collectives, body(): lax.all_to_all(jnp.broadcast_to(a[None], (NY * NX, ROWS, WIDE)), 'tp', 0, 0)  33.3 us
    all_gather x1, waiting for transfers between devices, gather_weight(): return lax.all_gather(rows, 'z', axis=0, tiled=True)  24.9 us
    all_to_all x1, starting transfers between devices, body(): far = lax.all_to_all(blocks, 'z', 0, 0)  14.9 us
    ppermute x5, waiting for transfers between devices, swap(): return lax.ppermute(value, axis, [(0, 1), (1, 0)])  14.2 us
    ppermute x5, starting transfers between devices, swap(): return lax.ppermute(value, axis, [(0, 1), (1, 0)])  12.5 us
    all_to_all x1, blocking collectives, gather_weight(): split = lax.all_to_all(split, 'tp', 0, 0)  11.6 us
    pallas_call x1, Pallas kernels, project(): pl.pallas_call(project_kernel, out_shape=jax.ShapeDtypeStruct((ROWS, WIDE...  5.5 us
  transfers between devices with their start and end apart: 7, of which 6 were waited for; matrix products, arithmetic and copies ran while one was open for 0% of the time, Pallas kernels for 3%

profile of v2, /device:TPU:6, one launch (start us, length us, event | category | flops | bytes accessed | tf_op | source)
XLA Modules:
  0.0 223.1 jit_solution(10857961141347030670)
XLA Ops:
  7.2 0.8 constant_dynamic-update-slice_fusion.1
  8.0 0.8 constant_dynamic-update-slice_fusion.own_ref
  8.8 3.3 %collective-permute-start.1 = (bf16[448,128]{1,0:T(8,128)(2,1)S(1)}, bf16[448,128]{1,0:T(8,128)(2,1)S(1)}, u32[]{:S(2)}, u32[]{:S(2)}) collective-permute-start(bf16[448,128]{1,0:T(8,128)(2,1)S(1)} %constant_dynamic-update-slice_fusion.own_ref), channel_id=1, source_target_pairs={{0,256},{256,0},{1,257},{257,1},{2,258},{258,2},{3,259},{259,3},{4... | collective-permute-start | bytes 344072 | tf_op jit(solution)/shard_map/ppermute | solution.py:166
  12.2 4.9 %collective-permute-done.1 = bf16[448,128]{1,0:T(8,128)(2,1)S(1)} collective-permute-done((bf16[448,128]{1,0:T(8,128)(2,1)S(1)}, bf16[448,128]{1,0:T(8,128)(2,1)S(1)}, u32[]{:S(2)}, u32[]{:S(2)}) %collective-permute-start.1) | collective-permute-done | bytes 114720 | tf_op jit(solution)/shard_map/ppermute | solution.py:166
  17.1 1.4 broadcast_select_fusion.after_ref
  18.5 1.5 shard_map.70
  20.1 11.6 %all_to_all.15.mine_ref = bf16[8,2,3200]{2,1,0:T(2,128)(2,1)S(1)} all-to-all(bf16[8,2,3200]{2,1,0:T(2,128)(2,1)} %shard_map.70), channel_id=1, replica_groups=mesh['xh'=2,'z'=16,'core'=2,'tp'=8] {'tp'}, dimensions={0} | all-to-all | bytes 204800 | tf_op jit(solution)/shard_map/all_to_all | solution.py:197
  31.7 14.9 %all-to-all-start = ((bf16[16,448,128]{2,1,0:T(8,128)(2,1)}), bf16[16,448,128]{2,1,0:T(8,128)(2,1)S(1)}, u32[]{:S(2)}, u32[]{:S(2)}) async-start(bf16[16,448,128]{2,1,0:T(8,128)(2,1)} %broadcast_select_fusion.after_ref), calls=%async_computation | async-start | bytes 3670016 | tf_op jit(solution)/shard_map/all_to_all | solution.py:227
  46.7 3.3 %collective-permute-start.3 = (bf16[8,2,3200]{2,1,0:T(2,128)(2,1)S(1)}, bf16[8,2,3200]{2,1,0:T(2,128)(2,1)S(1)}, u32[]{:S(2)}, u32[]{:S(2)}) collective-permute-start(bf16[8,2,3200]{2,1,0:T(2,128)(2,1)S(1)} %all_to_all.15.mine_ref), channel_id=1, source_target_pairs={{0,256},{256,0},{1,257},{257,1},{2,258},{258,2},{3,259},{259,3},{4... | collective-permute-start | bytes 307208 | tf_op jit(solution)/shard_map/ppermute | solution.py:166
  50.0 4.7 %collective-permute-done.3.other_ref = bf16[8,2,3200]{2,1,0:T(2,128)(2,1)S(1)} collective-permute-done((bf16[8,2,3200]{2,1,0:T(2,128)(2,1)S(1)}, bf16[8,2,3200]{2,1,0:T(2,128)(2,1)S(1)}, u32[]{:S(2)}, u32[]{:S(2)}) %collective-permute-start.3) | collective-permute-done | bytes 102432 | tf_op jit(solution)/shard_map/ppermute | solution.py:166
  54.7 0.6 copy-done.6
  55.4 1.8 shard_map.71
  57.2 1.9 collective-permute-start
  59.2 1.5 collective-permute-done
  60.8 79.2 %all-to-all-done.far_ref = bf16[16,448,128]{2,1,0:T(8,128)(2,1)S(1)} async-done(((bf16[16,448,128]{2,1,0:T(8,128)(2,1)}), bf16[16,448,128]{2,1,0:T(8,128)(2,1)S(1)}, u32[]{:S(2)}, u32[]{:S(2)}) %all-to-all-start) | async-done | bytes 1835040 | tf_op jit(solution)/shard_map/all_to_all | solution.py:227
  140.0 2.8 %shard_map.68.mine_ref = f32[656,448]{1,0:T(8,128)S(1)} custom-call(s32[3]{0:T(128)S(1)} %pad_add_fusion.here_ref, s32[16]{0:T(128)S(1)} %copy-done.3, bf16[448,640]{1,0:T(8,128)(2,1)S(1)} %maximum_select_fusion.q_ref, bf16[448,128]{1,0:T(8,128)(2,1)S(1)} %constant_dynamic-update-slice_fusion.own_ref, bf16[16,448,128]{2,1,0:T(8,128)(2,1)S(1)} %all-to-all-done.far_ref), custom_call_target="tpu_custom_call" | custom-call | flops 4110417920 | bytes 2351104 | tf_op jit(solution)/shard_map/pallas_call | solution.py:84
  142.8 1.9 collective-permute-start.2
  144.7 3.0 %collective-permute-done.2.other_ref = f32[656,448]{1,0:T(8,128)S(1)} collective-permute-done((f32[656,448]{1,0:T(8,128)S(1)}, f32[656,448]{1,0:T(8,128)S(1)}, u32[]{:S(2)}, u32[]{:S(2)}) %collective-permute-start.2) | collective-permute-done | bytes 1175584 | tf_op jit(solution)/shard_map/ppermute | solution.py:166
  147.8 1.8 shard_map.69
  149.6 0.7 copy-done.1
  150.3 24.9 %all-gather.2.cloned.1.call-done.refs_1_ = bf16[128,12800]{1,0:T(8,128)(2,1)} async-done(((bf16[8,12800]{1,0:T(8,128)(2,1)}), bf16[128,12800]{1,0:T(8,128)(2,1)}) %all-gather.2.cloned.1.call-update) | async-done | bytes 3276816 | tf_op jit(solution)/shard_map/all_gather | solution.py:204
  175.2 2.0 collective-permute-start.4
  177.4 33.3 %all_to_all.16.a_ref = bf16[8,224,640]{2,1,0:T(8,128)(2,1)S(1)} all-to-all(bf16[8,224,640]{2,1,0:T(8,128)(2,1)S(1)} %broadcast_in_dim.36), channel_id=1, replica_groups=mesh['xh'=2,'z'=16,'core'=2,'tp'=8] {'tp'}, dimensions={0} | all-to-all | bytes 4587520 | tf_op jit(solution)/shard_map/all_to_all | solution.py:233
  210.7 5.5 %shard_map.73 = f32[224,640]{1,0:T(8,128)} custom-call(s32[3]{0:T(128)S(1)} %pad_add_fusion.here_ref, bf16[128,12800]{1,0:T(8,128)(2,1)S(1)} %copy-done, bf16[128,12800]{1,0:T(8,128)(2,1)S(1)} %collective-permute-done.4.other_ref, bf16[8,224,640]{2,1,0:T(8,128)(2,1)S(1)} %all_to_all.16.a_ref), custom_call_target="tpu_custom_call" | custom-call | flops 2055208960 | bytes 6553600 | tf_op jit(solution)/shard_map/pallas_call | solution.py:151
  (20 shorter events, 0.5 us)
Async XLA Ops:
  8.8 8.3 %collective-permute-start.1 = (bf16[448,128]{1,0:T(8,128)(2,1)S(1)}, bf16[448,128]{1,0:T(8,128)(2,1)S(1)}, u32[]{:S(2)}, u32[]{:S(2)}) collective-permute-start(bf16[448,128]{1,0:T(8,128)(2,1)S(1)} %constant_dynamic-update-slice_fusion.own_ref), channel_id=1, source_target_pairs={{0,256},{256,0},{1,257},{257,1},{2,258},{258,2},{3,259},{259,3},{4... | collective-permute-start | bytes 344072 | tf_op jit(solution)/shard_map/ppermute | solution.py:166
  31.7 15.0 %copy-start.4 = (bf16[8,2,3200]{2,1,0:T(2,128)(2,1)}, bf16[8,2,3200]{2,1,0:T(2,128)(2,1)S(1)}, u32[]{:S(2)}) copy-start(bf16[8,2,3200]{2,1,0:T(2,128)(2,1)S(1)} %all_to_all.15.mine_ref) | copy-start | bytes 307204
  31.7 25.4 %copy-start.5 = (bf16[224,640]{1,0:T(8,128)(2,1)S(1)}, bf16[224,640]{1,0:T(8,128)(2,1)}, u32[]{:S(2)}) copy-start(bf16[224,640]{1,0:T(8,128)(2,1)} %param.5) | copy-start | bytes 860164
  31.7 108.3 %copy-start.3 = (s32[16]{0:T(128)S(1)}, s32[16]{0:T(128)}, u32[]{:S(2)}) copy-start(s32[16]{0:T(128)} %len_ref.1) | copy-start | bytes 196
  31.7 108.3 %all-to-all-start = ((bf16[16,448,128]{2,1,0:T(8,128)(2,1)}), bf16[16,448,128]{2,1,0:T(8,128)(2,1)S(1)}, u32[]{:S(2)}, u32[]{:S(2)}) async-start(bf16[16,448,128]{2,1,0:T(8,128)(2,1)} %broadcast_select_fusion.after_ref), calls=%async_computation | async-start | bytes 3670016 | tf_op jit(solution)/shard_map/all_to_all | solution.py:227
  46.6 128.6 %all-gather.2.cloned.1.call-start = ((), (), s32[]{:S(2)}) async-start(), calls=%async_computation.3 | async-start | bytes 3481600 | tf_op jit(solution)/shard_map/all_gather | solution.py:204
  46.7 8.1 %collective-permute-start.3 = (bf16[8,2,3200]{2,1,0:T(2,128)(2,1)S(1)}, bf16[8,2,3200]{2,1,0:T(2,128)(2,1)S(1)}, u32[]{:S(2)}, u32[]{:S(2)}) collective-permute-start(bf16[8,2,3200]{2,1,0:T(2,128)(2,1)S(1)} %all_to_all.15.mine_ref), channel_id=1, source_target_pairs={{0,256},{256,0},{1,257},{257,1},{2,258},{258,2},{3,259},{259,3},{4... | collective-permute-start | bytes 307208 | tf_op jit(solution)/shard_map/ppermute | solution.py:166
  54.7 0.6 copy-start.6
  57.2 3.5 %collective-permute-start = (bf16[224,640]{1,0:T(8,128)(2,1)S(1)}, bf16[224,640]{1,0:T(8,128)(2,1)S(1)}, u32[]{:S(2)}, u32[]{:S(2)}) collective-permute-start(bf16[224,640]{1,0:T(8,128)(2,1)S(1)} %copy-done.5), channel_id=1, source_target_pairs={{0,8},{8,0},{1,9},{9,1},{2,10},{10,2},{3,11},{11,3},{4,12},{12,4},... | collective-permute-start | bytes 860168 | tf_op jit(solution)/shard_map/ppermute | solution.py:166
  142.8 5.0 %collective-permute-start.2 = (f32[656,448]{1,0:T(8,128)S(1)}, f32[656,448]{1,0:T(8,128)S(1)}, u32[]{:S(2)}, u32[]{:S(2)}) collective-permute-start(f32[656,448]{1,0:T(8,128)S(1)} %shard_map.68.mine_ref), channel_id=1, source_target_pairs={{0,8},{8,0},{1,9},{9,1},{2,10},{10,2},{3,11},{11,3},{4,12},{12,4},... | collective-permute-start | bytes 3526664 | tf_op jit(solution)/shard_map/ppermute | solution.py:166
  149.6 0.7 copy-start.1
  175.2 2.1 copy-start.2
  175.2 35.5 %collective-permute-start.4 = (bf16[128,12800]{1,0:T(8,128)(2,1)}, bf16[128,12800]{1,0:T(8,128)(2,1)S(1)}, u32[]{:S(2)}, u32[]{:S(2)}) collective-permute-start(bf16[128,12800]{1,0:T(8,128)(2,1)} %shard_map.72.own_ref), channel_id=1, source_target_pairs={{0,8},{8,0},{1,9},{9,1},{2,10},{10,2},{3,11},{11,3},{4,12},{12,4},... | collective-permute-start | bytes 9830408 | tf_op jit(solution)/shard_map/ppermute | solution.py:166
  177.4 33.3 %copy-start = (bf16[128,12800]{1,0:T(8,128)(2,1)S(1)}, bf16[128,12800]{1,0:T(8,128)(2,1)}, u32[]{:S(2)}) copy-start(bf16[128,12800]{1,0:T(8,128)(2,1)} %shard_map.72.own_ref) | copy-start | bytes 9830404
Sparse Core Ops, SparseCore 0:
  57.3 117.8 all-gather.1

commit v3 on v1

--- a/solution.py
+++ b/solution.py
@@ -148,45 +148,40 @@
     )(here, mine, other)
 
 
-def project_kernel(steps, here_ref, own_ref, other_ref, *refs):
-    z, core, xh, xl, y = (here_ref[i] for i in range(5))
+def project_kernel(here_ref, own_ref, other_ref, a_ref, out_ref):
+    core, xh = here_ref[1], here_ref[2]
     k = lax.broadcasted_iota(jnp.int32, (DEEP, DEEP), 0)
     g = lax.broadcasted_iota(jnp.int32, (DEEP, DEEP), 1)
     row = g & (HD - 1)
     d = (xh ^ ((row >> 1) & 1)) * (NZ * 4) + (row >> 3) * 4 + (core ^ (g >> 7)) * 2 + (row & 1)
-    match = ((k & (HD - 1)) == d) & (((row >> 2) & 1) == (xl ^ (k >> 7)))
+    match = ((k & (HD - 1)) == d) & (((row >> 2) & 1) == (k >> 7))
     perm = jnp.where(match, 1.0, 0.0).astype(BF16)
-    near_refs, far_refs = refs[: len(steps)], refs[len(steps) : 2 * len(steps)]
-    total = jnp.zeros((ROWS, WIDE), F32) if len(refs) == 2 * len(steps) + 1 else refs[-2][...]
-    for step, near_ref, far_ref in zip(steps, near_refs, far_refs):
-        start = ((y + step + NY) & (NY - 1)) * (HEADS * WIDE)
+    total = jnp.zeros((ROWS, WIDE), F32)
+    for y in range(NY):
         for h in range(HEADS):
             heads = slice(h * HD, (h + 1) * HD)
-            columns = pl.ds(pl.multiple_of(start + h * WIDE, HD), WIDE)
-            both = jnp.concatenate([near_ref[:, heads], far_ref[:, heads]], axis=1)
+            columns = slice((y * HEADS + h) * WIDE, (y * HEADS + h + 1) * WIDE)
+            both = jnp.concatenate([a_ref[y * NX + x, :, heads] for x in range(NX)], axis=1)
             moved = jnp.dot(both, perm, preferred_element_type=F32).astype(BF16)
             weight = jnp.concatenate([own_ref[:, columns], other_ref[:, columns]], axis=0)
             total += jnp.dot(moved, weight, preferred_element_type=F32)
-    refs[-1][...] = total
-
-
-def project(here, weights, pairs, total):
-    steps = [step for step, _, _ in pairs]
-    operands = [near for _, near, _ in pairs] + [far for _, _, far in pairs]
-    operands += [] if total is None else [total]
-    vmem = pl.BlockSpec(memory_space=pltpu.VMEM)
-    return pl.pallas_call(
-        functools.partial(project_kernel, steps),
+    out_ref[...] = total
+
+
+def project(here, weights, a):
+    vmem = pl.BlockSpec(memory_space=pltpu.VMEM)
+    return pl.pallas_call(
+        project_kernel,
         out_shape=jax.ShapeDtypeStruct((ROWS, WIDE), F32),
-        in_specs=[pl.BlockSpec(memory_space=pltpu.SMEM)] + [vmem] * (2 + len(operands)),
+        in_specs=[pl.BlockSpec(memory_space=pltpu.SMEM), vmem, vmem, vmem],
         out_specs=vmem,
         cost_estimate=pl.CostEstimate(
-            flops=2 * len(steps) * ROWS * DEEP * HEADS * (WIDE + DEEP),
+            flops=2 * NY * ROWS * DEEP * HEADS * (WIDE + DEEP),
             bytes_accessed=DEEP * NY * HEADS * WIDE * 2,
             transcendentals=0,
         ),
         compiler_params=pltpu.CompilerParams(vmem_limit_bytes=VMEM),
-    )(here, *weights, *operands)
+    )(here, *weights, a)
 
 
 def swap(value, axis):
@@ -195,13 +190,6 @@
 
 def ring(value, steps):
     return lax.ppermute(value, "z", [(i, (i + steps) % NZ) for i in range(NZ)])
-
-
-def hop(block, dy, dx):
-    perm = [
-        (sy * NX + sx, (sy + dy) % NY * NX + (sx ^ dx)) for sy in range(NY) for sx in range(NX)
-    ]
-    return lax.ppermute(block, "tp", perm)
 
 
 def split_kernel(after_ref, weight_ref, out_ref):
@@ -223,7 +211,18 @@
     pass
 
 
-def gather_weight(out_weight, after):
+def behind(value, *after):
+    whole = pl.BlockSpec(memory_space=pl.ANY)
+    return pl.pallas_call(
+        pass_kernel,
+        out_shape=jax.ShapeDtypeStruct(value.shape, value.dtype),
+        in_specs=[whole] * (1 + len(after)),
+        out_specs=whole,
+        input_output_aliases={0: 0},
+    )(value, *after)
+
+
+def split_weight(out_weight, after):
     whole = pl.BlockSpec(memory_space=pl.ANY)
     vmem = pl.BlockSpec(memory_space=pltpu.VMEM)
     split = pl.pallas_call(
@@ -232,7 +231,11 @@
         in_specs=[whole, vmem],
         out_specs=vmem,
     )(after, out_weight)
-    split = lax.all_to_all(split, "tp", 0, 0)
+    return lax.all_to_all(split, "tp", 0, 0)
+
+
+def gather_weight(split):
+    vmem = pl.BlockSpec(memory_space=pltpu.VMEM)
     rows = pl.pallas_call(
         stack_kernel,
         out_shape=jax.ShapeDtypeStruct((8, NY * HEADS * WIDE), BF16),
@@ -242,22 +245,9 @@
     return lax.all_gather(rows, "z", axis=0, tiled=True)
 
 
-def exchange_weight(own, *after):
-    whole = pl.BlockSpec(memory_space=pl.ANY)
-    hbm = pl.BlockSpec(memory_space=pltpu.HBM)
-    own = pl.pallas_call(
-        pass_kernel,
-        out_shape=jax.ShapeDtypeStruct(own.shape, own.dtype),
-        in_specs=[whole] * len(after) + [hbm],
-        out_specs=hbm,
-        input_output_aliases={len(after): 0},
-    )(*after, own)
-    return own, swap(own, "core")
-
-
 def body(queries, keys, values, doc_lengths, out_weight):
-    xh, z, core, tp = (lax.axis_index(name) for name in ("xh", "z", "core", "tp"))
-    here = jnp.stack([z, core, xh, tp % NX, tp // NX]).astype(jnp.int32)
+    xh, z, core = (lax.axis_index(name) for name in ("xh", "z", "core"))
+    here = jnp.stack([z, core, xh]).astype(jnp.int32)
     own = jnp.concatenate([keys, values], axis=0)
     pair = jnp.concatenate([own, swap(own, "xh")], axis=0)
     other_q = swap(queries, "core")
@@ -268,22 +258,19 @@
         up.append(ring(up[-1], 1))
         down.append(ring(down[-1], -1))
     last = [ring(up[-1][:QROWS], 1), ring(down[-1][QROWS:], -1)]
-    weight = gather_weight(out_weight, up[1])
+    split = split_weight(out_weight, own)
 
     state = attend(here, doc_lengths, q, [(0, 0, 0, False), (0, 1, 0, True)], [pair], None)
+    weight = gather_weight(behind(split, state))
     for s in range(1, far):
         visits = [(0, 0, s, False), (0, 1, s, True), (1, 0, -s, False), (1, 1, -s, True)]
         state = attend(here, doc_lengths, q, visits, [up[s], down[s]], state)
     state = attend(here, doc_lengths, q, [(0, 0, far, False), (1, 0, far, True)], last, state)
     attended, a = merge(here, state, swap(state, "core"))
 
-    below, above = hop(a, 1, 0), hop(a, -1, 0)
-    across_below, across_above, across = hop(a, 1, 1), hop(a, -1, 1), hop(a, 0, 1)
-    two, across_two = hop(below, 1, 0), hop(across_above, -1, 0)
-    weights = exchange_weight(weight, below, above, across_below, across_above, across)
-    pairs = [(0, a, across), (-1, below, across_below), (1, above, across_above)]
-    projected = project(here, weights, pairs, None)
-    projected = project(here, weights, [(2, two, across_two)], projected)
+    weight = behind(weight, a)
+    sources = lax.all_to_all(jnp.broadcast_to(a[None], (NY * NX, ROWS, WIDE)), "tp", 0, 0)
+    projected = project(here, (weight, swap(weight, "core")), sources)
     return (attended, projected)
 
 

time: 209 us -> 193 us (0.923)
  the two profiles are of different devices: /device:TPU:231 before, /device:TPU:6 now
where the time goes in v3:
time: 193 us
  starting transfers between devices  83.1 us (43%)
  Pallas kernels  38.5 us (20%)
  blocking collectives  34 us (18%)
  waiting for transfers between devices  16.8 us (9%)
  between operations  14.5 us (8%)
  local copies, waits for them, and re-layouts  4.99 us (3%)
    ppermute x16, starting transfers between devices, ring(): return lax.ppermute(value, 'z', [(i, (i + steps) % NZ) for i in range(NZ)])  61.1 us
    all_to_all x1, blocking collectives, body(): lax.all_to_all(jnp.broadcast_to(a[None], (NY * NX, ROWS, WIDE)), 'tp', 0, 0)  34 us
    pallas_call x9, Pallas kernels, attend(): pl.pallas_call(functools.partial(attend_kernel, visits, state is None), o...  27.8 us
    ppermute x16, waiting for transfers between devices, ring(): return lax.ppermute(value, 'z', [(i, (i + steps) % NZ) for i in range(NZ)])  13.8 us
    ppermute x5, starting transfers between devices, swap(): return lax.ppermute(value, axis, [(0, 1), (1, 0)])  13.5 us
    all_to_all x1, starting transfers between devices, split_weight(): return lax.all_to_all(split, 'tp', 0, 0)  8.57 us
    pallas_call x1, Pallas kernels, project(): pl.pallas_call(project_kernel, out_shape=jax.ShapeDtypeStruct((ROWS, WIDE...  5.5 us
    unnamed x19, local copies, waits for them, and re-layouts  3.93 us
  transfers between devices with their start and end apart: 23, of which 6 were waited for; matrix products, arithmetic and copies ran while one was open for 2% of the time, Pallas kernels for 17%

profile of v3, /device:TPU:6, one launch (start us, length us, event | category | flops | bytes accessed | tf_op | source)
XLA Modules:
  0.0 193.2 jit_solution(6269114233998806759)
XLA Ops:
  10.8 3.3 %collective-permute-start.1 = (bf16[448,128]{1,0:T(8,128)(2,1)S(1)}, bf16[448,128]{1,0:T(8,128)(2,1)S(1)}, u32[]{:S(2)}, u32[]{:S(2)}) collective-permute-start(bf16[448,128]{1,0:T(8,128)(2,1)S(1)} %get-tuple-element.6.after_ref), channel_id=1, source_target_pairs={{0,256},{256,0},{1,257},{257,1},{2,258},{258,2},{3,259},{259,3},{4... | collective-permute-start | bytes 344072 | tf_op jit(solution)/shard_map/ppermute | solution.py:188
  15.7 8.6 %all-to-all-start = ((bf16[8,2,3200]{2,1,0:T(2,128)(2,1)}), bf16[8,2,3200]{2,1,0:T(2,128)(2,1)S(1)}, u32[]{:S(2)}, u32[]{:S(2)}) async-start(bf16[8,2,3200]{2,1,0:T(2,128)(2,1)} %shard_map.78), calls=%async_computation | async-start | bytes 204800 | tf_op jit(solution)/shard_map/all_to_all | solution.py:234
  24.4 8.8 %collective-permute-start.10 = (bf16[896,128]{1,0:T(8,128)(2,1)S(1)}, bf16[896,128]{1,0:T(8,128)(2,1)S(1)}, u32[]{:S(2)}, u32[]{:S(2)}) collective-permute-start(bf16[896,128]{1,0:T(8,128)(2,1)S(1)} %constant_dynamic-update-slice_fusion.2.refs_0_), channel_id=1, source_target_pairs={{0,240},{16,0},{32,16},{48,32},{64,48},{80,64},{96,80},{112,96},{1... | collective-permute-start | bytes 688136 | tf_op jit(solution)/shard_map/ppermute | solution.py:192
  40.6 4.2 %collective-permute-start.19 = (bf16[8,2,3200]{2,1,0:T(2,128)(2,1)}, bf16[8,2,3200]{2,1,0:T(2,128)(2,1)S(1)}, u32[]{:S(2)}, u32[]{:S(2)}) collective-permute-start(bf16[8,2,3200]{2,1,0:T(2,128)(2,1)} %shard_map.79.mine_ref), channel_id=1, source_target_pairs={{0,256},{256,0},{1,257},{257,1},{2,258},{258,2},{3,259},{259,3},{4... | collective-permute-start | bytes 307208 | tf_op jit(solution)/shard_map/ppermute | solution.py:188
  44.8 5.1 %collective-permute-start.11 = (bf16[896,128]{1,0:T(8,128)(2,1)S(1)}, bf16[896,128]{1,0:T(8,128)(2,1)S(1)}, u32[]{:S(2)}, u32[]{:S(2)}) collective-permute-start(bf16[896,128]{1,0:T(8,128)(2,1)S(1)} %collective-permute-done.10.refs_1_), channel_id=1, source_target_pairs={{0,240},{16,0},{32,16},{48,32},{64,48},{80,64},{96,80},{112,96},{1... | collective-permute-start | bytes 688136 | tf_op jit(solution)/shard_map/ppermute | solution.py:192
  51.8 2.6 %shard_map.69.refs_2_ = f32[656,448]{1,0:T(8,128)S(1)} custom-call(s32[3]{0:T(128)S(1)} %pad_add_fusion.here_ref, s32[16]{0:T(128)S(1)} %copy-done.5, bf16[448,640]{1,0:T(8,128)(2,1)S(1)} %maximum_select_fusion.q_ref, bf16[896,128]{1,0:T(8,128)(2,1)S(1)} %collective-permute-done.2.refs_0_, ...), custom_call_target="tpu_custom_call", output_to_operand_aliasing={{}: (5, {})} | custom-call | flops 8220835840 | bytes 18808832 | tf_op jit(solution)/shard_map/pallas_call | solution.py:101
  56.9 3.3 %collective-permute-start.12 = (bf16[896,128]{1,0:T(8,128)(2,1)S(1)}, bf16[896,128]{1,0:T(8,128)(2,1)S(1)}, u32[]{:S(2)}, u32[]{:S(2)}) collective-permute-start(bf16[896,128]{1,0:T(8,128)(2,1)S(1)} %collective-permute-done.11.refs_1_), channel_id=1, source_target_pairs={{0,240},{16,0},{32,16},{48,32},{64,48},{80,64},{96,80},{112,96},{1... | collective-permute-start | bytes 688136 | tf_op jit(solution)/shard_map/ppermute | solution.py:192
  62.8 2.6 %shard_map.70.refs_2_ = f32[656,448]{1,0:T(8,128)S(1)} custom-call(s32[3]{0:T(128)S(1)} %pad_add_fusion.here_ref, s32[16]{0:T(128)S(1)} %copy-done.5, bf16[448,640]{1,0:T(8,128)(2,1)S(1)} %maximum_select_fusion.q_ref, bf16[896,128]{1,0:T(8,128)(2,1)S(1)} %collective-permute-done.3.refs_0_, ...), custom_call_target="tpu_custom_call", output_to_operand_aliasing={{}: (5, {})} | custom-call | flops 8220835840 | bytes 18808832 | tf_op jit(solution)/shard_map/pallas_call | solution.py:101
  65.5 5.5 %collective-permute-start.13 = (bf16[896,128]{1,0:T(8,128)(2,1)S(1)}, bf16[896,128]{1,0:T(8,128)(2,1)S(1)}, u32[]{:S(2)}, u32[]{:S(2)}) collective-permute-start(bf16[896,128]{1,0:T(8,128)(2,1)S(1)} %collective-permute-done.12.refs_1_), channel_id=1, source_target_pairs={{0,240},{16,0},{32,16},{48,32},{64,48},{80,64},{96,80},{112,96},{1... | collective-permute-start | bytes 688136 | tf_op jit(solution)/shard_map/ppermute | solution.py:192
  72.9 2.8 %shard_map.71.refs_2_ = f32[656,448]{1,0:T(8,128)S(1)} custom-call(s32[3]{0:T(128)S(1)} %pad_add_fusion.here_ref, s32[16]{0:T(128)S(1)} %copy-done.5, bf16[448,640]{1,0:T(8,128)(2,1)S(1)} %maximum_select_fusion.q_ref, bf16[896,128]{1,0:T(8,128)(2,1)S(1)} %collective-permute-done.4.refs_0_, ...), custom_call_target="tpu_custom_call", output_to_operand_aliasing={{}: (5, {})} | custom-call | flops 8220835840 | bytes 18808832 | tf_op jit(solution)/shard_map/pallas_call | solution.py:101
  75.7 2.9 %collective-permute-done.13.refs_1_ = bf16[896,128]{1,0:T(8,128)(2,1)S(1)} collective-permute-done((bf16[896,128]{1,0:T(8,128)(2,1)S(1)}, bf16[896,128]{1,0:T(8,128)(2,1)S(1)}, u32[]{:S(2)}, u32[]{:S(2)}) %collective-permute-start.13) | collective-permute-done | bytes 229408 | tf_op jit(solution)/shard_map/ppermute | solution.py:192
  78.6 5.6 %collective-permute-start.14 = (bf16[896,128]{1,0:T(8,128)(2,1)S(1)}, bf16[896,128]{1,0:T(8,128)(2,1)S(1)}, u32[]{:S(2)}, u32[]{:S(2)}) collective-permute-start(bf16[896,128]{1,0:T(8,128)(2,1)S(1)} %collective-permute-done.13.refs_1_), channel_id=1, source_target_pairs={{0,240},{16,0},{32,16},{48,32},{64,48},{80,64},{96,80},{112,96},{1... | collective-permute-start | bytes 688136 | tf_op jit(solution)/shard_map/ppermute | solution.py:192
  86.8 2.6 %shard_map.72.refs_2_ = f32[656,448]{1,0:T(8,128)S(1)} custom-call(s32[3]{0:T(128)S(1)} %pad_add_fusion.here_ref, s32[16]{0:T(128)S(1)} %copy-done.5, bf16[448,640]{1,0:T(8,128)(2,1)S(1)} %maximum_select_fusion.q_ref, bf16[896,128]{1,0:T(8,128)(2,1)S(1)} %collective-permute-done.5.refs_0_, ...), custom_call_target="tpu_custom_call", output_to_operand_aliasing={{}: (5, {})} | custom-call | flops 8220835840 | bytes 18808832 | tf_op jit(solution)/shard_map/pallas_call | solution.py:101
  89.4 4.0 %collective-permute-done.14.refs_1_ = bf16[896,128]{1,0:T(8,128)(2,1)S(1)} collective-permute-done((bf16[896,128]{1,0:T(8,128)(2,1)S(1)}, bf16[896,128]{1,0:T(8,128)(2,1)S(1)}, u32[]{:S(2)}, u32[]{:S(2)}) %collective-permute-start.14) | collective-permute-done | bytes 229408 | tf_op jit(solution)/shard_map/ppermute | solution.py:192
  93.4 5.6 %collective-permute-start.15 = (bf16[896,128]{1,0:T(8,128)(2,1)S(1)}, bf16[896,128]{1,0:T(8,128)(2,1)S(1)}, u32[]{:S(2)}, u32[]{:S(2)}) collective-permute-start(bf16[896,128]{1,0:T(8,128)(2,1)S(1)} %collective-permute-done.14.refs_1_), channel_id=1, source_target_pairs={{0,240},{16,0},{32,16},{48,32},{64,48},{80,64},{96,80},{112,96},{1... | collective-permute-start | bytes 688136 | tf_op jit(solution)/shard_map/ppermute | solution.py:192
  101.0 2.6 %shard_map.73.refs_2_ = f32[656,448]{1,0:T(8,128)S(1)} custom-call(s32[3]{0:T(128)S(1)} %pad_add_fusion.here_ref, s32[16]{0:T(128)S(1)} %copy-done.5, bf16[448,640]{1,0:T(8,128)(2,1)S(1)} %maximum_select_fusion.q_ref, bf16[896,128]{1,0:T(8,128)(2,1)S(1)} %collective-permute-done.6.refs_0_, ...), custom_call_target="tpu_custom_call", output_to_operand_aliasing={{}: (5, {})} | custom-call | flops 8220835840 | bytes 18808832 | tf_op jit(solution)/shard_map/pallas_call | solution.py:101
  103.6 4.4 %collective-permute-done.15.refs_1_ = bf16[896,128]{1,0:T(8,128)(2,1)S(1)} collective-permute-done((bf16[896,128]{1,0:T(8,128)(2,1)S(1)}, bf16[896,128]{1,0:T(8,128)(2,1)S(1)}, u32[]{:S(2)}, u32[]{:S(2)}) %collective-permute-start.15) | collective-permute-done | bytes 229408 | tf_op jit(solution)/shard_map/ppermute | solution.py:192
  108.0 5.6 %collective-permute-start.16 = (bf16[896,128]{1,0:T(8,128)(2,1)S(1)}, bf16[896,128]{1,0:T(8,128)(2,1)S(1)}, u32[]{:S(2)}, u32[]{:S(2)}) collective-permute-start(bf16[896,128]{1,0:T(8,128)(2,1)S(1)} %collective-permute-done.15.refs_1_), channel_id=1, source_target_pairs={{0,240},{16,0},{32,16},{48,32},{64,48},{80,64},{96,80},{112,96},{1... | collective-permute-start | bytes 688136 | tf_op jit(solution)/shard_map/ppermute | solution.py:192
  115.6 4.7 %shard_map.74.refs_2_ = f32[656,448]{1,0:T(8,128)S(1)} custom-call(s32[3]{0:T(128)S(1)} %pad_add_fusion.here_ref, s32[16]{0:T(128)S(1)} %copy-done.5, bf16[448,640]{1,0:T(8,128)(2,1)S(1)} %maximum_select_fusion.q_ref, bf16[896,128]{1,0:T(8,128)(2,1)S(1)} %collective-permute-done.7.refs_0_, ...), custom_call_target="tpu_custom_call", output_to_operand_aliasing={{}: (5, {})} | custom-call | flops 8220835840 | bytes 18808832 | tf_op jit(solution)/shard_map/pallas_call | solution.py:101
  120.3 5.5 %collective-permute-start.17 = (bf16[448,128]{1,0:T(8,128)(2,1)S(1)}, bf16[448,128]{1,0:T(8,128)(2,1)S(1)}, u32[]{:S(2)}, u32[]{:S(2)}) collective-permute-start(bf16[448,128]{1,0:T(8,128)(2,1)S(1)} %slice.9), channel_id=1, source_target_pairs={{0,240},{16,0},{32,16},{48,32},{64,48},{80,64},{96,80},{112,96},{1... | collective-permute-start | bytes 344072 | tf_op jit(solution)/shard_map/ppermute | solution.py:192
  128.0 4.5 %shard_map.75.refs_2_ = f32[656,448]{1,0:T(8,128)S(1)} custom-call(s32[3]{0:T(128)S(1)} %pad_add_fusion.here_ref, s32[16]{0:T(128)S(1)} %copy-done.5, bf16[448,640]{1,0:T(8,128)(2,1)S(1)} %maximum_select_fusion.q_ref, bf16[896,128]{1,0:T(8,128)(2,1)S(1)} %collective-permute-done.8.refs_0_, ...), custom_call_target="tpu_custom_call", output_to_operand_aliasing={{}: (5, {})} | custom-call | flops 8220835840 | bytes 18808832 | tf_op jit(solution)/shard_map/pallas_call | solution.py:101
  138.9 3.0 %collective-permute-done.18.other_ref = f32[656,448]{1,0:T(8,128)S(1)} collective-permute-done((f32[656,448]{1,0:T(8,128)S(1)}, f32[656,448]{1,0:T(8,128)S(1)}, u32[]{:S(2)}, u32[]{:S(2)}) %collective-permute-start.18) | collective-permute-done | bytes 1175584 | tf_op jit(solution)/shard_map/ppermute | solution.py:188
  146.9 34.0 %all_to_all.10.a_ref = bf16[8,224,640]{2,1,0:T(8,128)(2,1)S(1)} all-to-all(bf16[8,224,640]{2,1,0:T(8,128)(2,1)S(1)} %broadcast_in_dim.2), channel_id=1, replica_groups=mesh['xh'=2,'z'=16,'core'=2,'tp'=8] {'tp'}, dimensions={0} | all-to-all | bytes 4587520 | tf_op jit(solution)/shard_map/all_to_all | solution.py:272
  180.9 5.5 %shard_map.82 = f32[224,640]{1,0:T(8,128)} custom-call(s32[3]{0:T(128)S(1)} %pad_add_fusion.here_ref, bf16[128,12800]{1,0:T(8,128)(2,1)S(1)} %copy-done, bf16[128,12800]{1,0:T(8,128)(2,1)S(1)} %collective-permute-done.20.other_ref, bf16[8,224,640]{2,1,0:T(8,128)(2,1)S(1)} %all_to_all.10.a_ref), custom_call_target="tpu_custom_call" | custom-call | flops 2055208960 | bytes 6553600 | tf_op jit(solution)/shard_map/pallas_call | solution.py:173
  (65 shorter events, 41.2 us)
Async XLA Ops:
  7.2 27.9 %collective-permute-start = (bf16[224,640]{1,0:T(8,128)(2,1)}, bf16[224,640]{1,0:T(8,128)(2,1)S(1)}, u32[]{:S(2)}, u32[]{:S(2)}) collective-permute-start(bf16[224,640]{1,0:T(8,128)(2,1)} %param.5), channel_id=1, source_target_pairs={{0,8},{8,0},{1,9},{9,1},{2,10},{10,2},{3,11},{11,3},{4,12},{12,4},... | collective-permute-start | bytes 860168 | tf_op jit(solution)/shard_map/ppermute | solution.py:188
  10.8 13.5 %collective-permute-start.1 = (bf16[448,128]{1,0:T(8,128)(2,1)S(1)}, bf16[448,128]{1,0:T(8,128)(2,1)S(1)}, u32[]{:S(2)}, u32[]{:S(2)}) collective-permute-start(bf16[448,128]{1,0:T(8,128)(2,1)S(1)} %get-tuple-element.6.after_ref), channel_id=1, source_target_pairs={{0,256},{256,0},{1,257},{257,1},{2,258},{258,2},{3,259},{259,3},{4... | collective-permute-start | bytes 344072 | tf_op jit(solution)/shard_map/ppermute | solution.py:188
  15.7 24.2 %all-to-all-start = ((bf16[8,2,3200]{2,1,0:T(2,128)(2,1)}), bf16[8,2,3200]{2,1,0:T(2,128)(2,1)S(1)}, u32[]{:S(2)}, u32[]{:S(2)}) async-start(bf16[8,2,3200]{2,1,0:T(2,128)(2,1)} %shard_map.78), calls=%async_computation | async-start | bytes 204800 | tf_op jit(solution)/shard_map/all_to_all | solution.py:234
  24.3 120.2 %all-gather.2.cloned.1.call-start = ((), (), s32[]{:S(2)}) async-start(), calls=%async_computation.2 | async-start | bytes 3481600 | tf_op jit(solution)/shard_map/all_gather | solution.py:245
  24.4 20.4 %collective-permute-start.10 = (bf16[896,128]{1,0:T(8,128)(2,1)S(1)}, bf16[896,128]{1,0:T(8,128)(2,1)S(1)}, u32[]{:S(2)}, u32[]{:S(2)}) collective-permute-start(bf16[896,128]{1,0:T(8,128)(2,1)S(1)} %constant_dynamic-update-slice_fusion.2.refs_0_), channel_id=1, source_target_pairs={{0,240},{16,0},{32,16},{48,32},{64,48},{80,64},{96,80},{112,96},{1... | collective-permute-start | bytes 688136 | tf_op jit(solution)/shard_map/ppermute | solution.py:192
  33.1 16.8 %collective-permute-start.2 = (bf16[896,128]{1,0:T(8,128)(2,1)S(1)}, bf16[896,128]{1,0:T(8,128)(2,1)S(1)}, u32[]{:S(2)}, u32[]{:S(2)}) collective-permute-start(bf16[896,128]{1,0:T(8,128)(2,1)S(1)} %constant_dynamic-update-slice_fusion.2.refs_0_), channel_id=1, source_target_pairs={{0,16},{16,32},{32,48},{48,64},{64,80},{80,96},{96,112},{112,128},... | collective-permute-start | bytes 688136 | tf_op jit(solution)/shard_map/ppermute | solution.py:192
  40.6 13.9 %collective-permute-start.19 = (bf16[8,2,3200]{2,1,0:T(2,128)(2,1)}, bf16[8,2,3200]{2,1,0:T(2,128)(2,1)S(1)}, u32[]{:S(2)}, u32[]{:S(2)}) collective-permute-start(bf16[8,2,3200]{2,1,0:T(2,128)(2,1)} %shard_map.79.mine_ref), channel_id=1, source_target_pairs={{0,256},{256,0},{1,257},{257,1},{2,258},{258,2},{3,259},{259,3},{4... | collective-permute-start | bytes 307208 | tf_op jit(solution)/shard_map/ppermute | solution.py:188
  44.8 12.2 %collective-permute-start.11 = (bf16[896,128]{1,0:T(8,128)(2,1)S(1)}, bf16[896,128]{1,0:T(8,128)(2,1)S(1)}, u32[]{:S(2)}, u32[]{:S(2)}) collective-permute-start(bf16[896,128]{1,0:T(8,128)(2,1)S(1)} %collective-permute-done.10.refs_1_), channel_id=1, source_target_pairs={{0,240},{16,0},{32,16},{48,32},{64,48},{80,64},{96,80},{112,96},{1... | collective-permute-start | bytes 688136 | tf_op jit(solution)/shard_map/ppermute | solution.py:192
  49.9 10.3 %collective-permute-start.3 = (bf16[896,128]{1,0:T(8,128)(2,1)S(1)}, bf16[896,128]{1,0:T(8,128)(2,1)S(1)}, u32[]{:S(2)}, u32[]{:S(2)}) collective-permute-start(bf16[896,128]{1,0:T(8,128)(2,1)S(1)} %collective-permute-done.2.refs_0_), channel_id=1, source_target_pairs={{0,16},{16,32},{32,48},{48,64},{64,80},{80,96},{96,112},{112,128},... | collective-permute-start | bytes 688136 | tf_op jit(solution)/shard_map/ppermute | solution.py:192
  56.9 8.5 %collective-permute-start.12 = (bf16[896,128]{1,0:T(8,128)(2,1)S(1)}, bf16[896,128]{1,0:T(8,128)(2,1)S(1)}, u32[]{:S(2)}, u32[]{:S(2)}) collective-permute-start(bf16[896,128]{1,0:T(8,128)(2,1)S(1)} %collective-permute-done.11.refs_1_), channel_id=1, source_target_pairs={{0,240},{16,0},{32,16},{48,32},{64,48},{80,64},{96,80},{112,96},{1... | collective-permute-start | bytes 688136 | tf_op jit(solution)/shard_map/ppermute | solution.py:192
  60.2 10.7 %collective-permute-start.4 = (bf16[896,128]{1,0:T(8,128)(2,1)S(1)}, bf16[896,128]{1,0:T(8,128)(2,1)S(1)}, u32[]{:S(2)}, u32[]{:S(2)}) collective-permute-start(bf16[896,128]{1,0:T(8,128)(2,1)S(1)} %collective-permute-done.3.refs_0_), channel_id=1, source_target_pairs={{0,16},{16,32},{32,48},{48,64},{64,80},{80,96},{96,112},{112,128},... | collective-permute-start | bytes 688136 | tf_op jit(solution)/shard_map/ppermute | solution.py:192
  65.5 13.2 %collective-permute-start.13 = (bf16[896,128]{1,0:T(8,128)(2,1)S(1)}, bf16[896,128]{1,0:T(8,128)(2,1)S(1)}, u32[]{:S(2)}, u32[]{:S(2)}) collective-permute-start(bf16[896,128]{1,0:T(8,128)(2,1)S(1)} %collective-permute-done.12.refs_1_), channel_id=1, source_target_pairs={{0,240},{16,0},{32,16},{48,32},{64,48},{80,64},{96,80},{112,96},{1... | collective-permute-start | bytes 688136 | tf_op jit(solution)/shard_map/ppermute | solution.py:192
  71.0 13.9 %collective-permute-start.5 = (bf16[896,128]{1,0:T(8,128)(2,1)S(1)}, bf16[896,128]{1,0:T(8,128)(2,1)S(1)}, u32[]{:S(2)}, u32[]{:S(2)}) collective-permute-start(bf16[896,128]{1,0:T(8,128)(2,1)S(1)} %collective-permute-done.4.refs_0_), channel_id=1, source_target_pairs={{0,16},{16,32},{32,48},{48,64},{64,80},{80,96},{96,112},{112,128},... | collective-permute-start | bytes 688136 | tf_op jit(solution)/shard_map/ppermute | solution.py:192
  78.6 14.8 %collective-permute-start.14 = (bf16[896,128]{1,0:T(8,128)(2,1)S(1)}, bf16[896,128]{1,0:T(8,128)(2,1)S(1)}, u32[]{:S(2)}, u32[]{:S(2)}) collective-permute-start(bf16[896,128]{1,0:T(8,128)(2,1)S(1)} %collective-permute-done.13.refs_1_), channel_id=1, source_target_pairs={{0,240},{16,0},{32,16},{48,32},{64,48},{80,64},{96,80},{112,96},{1... | collective-permute-start | bytes 688136 | tf_op jit(solution)/shard_map/ppermute | solution.py:192
  84.8 14.2 %collective-permute-start.6 = (bf16[896,128]{1,0:T(8,128)(2,1)S(1)}, bf16[896,128]{1,0:T(8,128)(2,1)S(1)}, u32[]{:S(2)}, u32[]{:S(2)}) collective-permute-start(bf16[896,128]{1,0:T(8,128)(2,1)S(1)} %collective-permute-done.5.refs_0_), channel_id=1, source_target_pairs={{0,16},{16,32},{32,48},{48,64},{64,80},{80,96},{96,112},{112,128},... | collective-permute-start | bytes 688136 | tf_op jit(solution)/shard_map/ppermute | solution.py:192
  93.4 14.6 %collective-permute-start.15 = (bf16[896,128]{1,0:T(8,128)(2,1)S(1)}, bf16[896,128]{1,0:T(8,128)(2,1)S(1)}, u32[]{:S(2)}, u32[]{:S(2)}) collective-permute-start(bf16[896,128]{1,0:T(8,128)(2,1)S(1)} %collective-permute-done.14.refs_1_), channel_id=1, source_target_pairs={{0,240},{16,0},{32,16},{48,32},{64,48},{80,64},{96,80},{112,96},{1... | collective-permute-start | bytes 688136 | tf_op jit(solution)/shard_map/ppermute | solution.py:192
  99.0 14.6 %collective-permute-start.7 = (bf16[896,128]{1,0:T(8,128)(2,1)S(1)}, bf16[896,128]{1,0:T(8,128)(2,1)S(1)}, u32[]{:S(2)}, u32[]{:S(2)}) collective-permute-start(bf16[896,128]{1,0:T(8,128)(2,1)S(1)} %collective-permute-done.6.refs_0_), channel_id=1, source_target_pairs={{0,16},{16,32},{32,48},{48,64},{64,80},{80,96},{96,112},{112,128},... | collective-permute-start | bytes 688136 | tf_op jit(solution)/shard_map/ppermute | solution.py:192
  108.0 12.3 %collective-permute-start.16 = (bf16[896,128]{1,0:T(8,128)(2,1)S(1)}, bf16[896,128]{1,0:T(8,128)(2,1)S(1)}, u32[]{:S(2)}, u32[]{:S(2)}) collective-permute-start(bf16[896,128]{1,0:T(8,128)(2,1)S(1)} %collective-permute-done.15.refs_1_), channel_id=1, source_target_pairs={{0,240},{16,0},{32,16},{48,32},{64,48},{80,64},{96,80},{112,96},{1... | collective-permute-start | bytes 688136 | tf_op jit(solution)/shard_map/ppermute | solution.py:192
  113.6 12.2 %collective-permute-start.8 = (bf16[896,128]{1,0:T(8,128)(2,1)S(1)}, bf16[896,128]{1,0:T(8,128)(2,1)S(1)}, u32[]{:S(2)}, u32[]{:S(2)}) collective-permute-start(bf16[896,128]{1,0:T(8,128)(2,1)S(1)} %collective-permute-done.7.refs_0_), channel_id=1, source_target_pairs={{0,16},{16,32},{32,48},{48,64},{64,80},{80,96},{96,112},{112,128},... | collective-permute-start | bytes 688136 | tf_op jit(solution)/shard_map/ppermute | solution.py:192
  120.3 12.2 %collective-permute-start.17 = (bf16[448,128]{1,0:T(8,128)(2,1)S(1)}, bf16[448,128]{1,0:T(8,128)(2,1)S(1)}, u32[]{:S(2)}, u32[]{:S(2)}) collective-permute-start(bf16[448,128]{1,0:T(8,128)(2,1)S(1)} %slice.9), channel_id=1, source_target_pairs={{0,240},{16,0},{32,16},{48,32},{64,48},{80,64},{96,80},{112,96},{1... | collective-permute-start | bytes 344072 | tf_op jit(solution)/shard_map/ppermute | solution.py:192
  125.9 8.4 %collective-permute-start.9 = (bf16[448,128]{1,0:T(8,128)(2,1)S(1)}, bf16[448,128]{1,0:T(8,128)(2,1)S(1)}, u32[]{:S(2)}, u32[]{:S(2)}) collective-permute-start(bf16[448,128]{1,0:T(8,128)(2,1)S(1)} %slice.8), channel_id=1, source_target_pairs={{0,16},{16,32},{32,48},{48,64},{64,80},{80,96},{96,112},{112,128},... | collective-permute-start | bytes 344072 | tf_op jit(solution)/shard_map/ppermute | solution.py:192
  137.0 5.0 %collective-permute-start.18 = (f32[656,448]{1,0:T(8,128)S(1)}, f32[656,448]{1,0:T(8,128)S(1)}, u32[]{:S(2)}, u32[]{:S(2)}) collective-permute-start(f32[656,448]{1,0:T(8,128)S(1)} %shard_map.76.mine_ref), channel_id=1, source_target_pairs={{0,8},{8,0},{1,9},{9,1},{2,10},{10,2},{3,11},{11,3},{4,12},{12,4},... | collective-permute-start | bytes 3526664 | tf_op jit(solution)/shard_map/ppermute | solution.py:188
  144.5 36.4 %collective-permute-start.20 = (bf16[128,12800]{1,0:T(8,128)(2,1)}, bf16[128,12800]{1,0:T(8,128)(2,1)S(1)}, u32[]{:S(2)}, u32[]{:S(2)}) collective-permute-start(bf16[128,12800]{1,0:T(8,128)(2,1)} %shard_map.81.own_ref), channel_id=1, source_target_pairs={{0,8},{8,0},{1,9},{9,1},{2,10},{10,2},{3,11},{11,3},{4,12},{12,4},... | collective-permute-start | bytes 9830408 | tf_op jit(solution)/shard_map/ppermute | solution.py:188
  146.8 34.0 %copy-start = (bf16[128,12800]{1,0:T(8,128)(2,1)S(1)}, bf16[128,12800]{1,0:T(8,128)(2,1)}, u32[]{:S(2)}) copy-start(bf16[128,12800]{1,0:T(8,128)(2,1)} %shard_map.81.own_ref) | copy-start | bytes 9830404
  (8 other events, 49.0 us)
Sparse Core Ops, SparseCore 0:
  57.1 77.9 all-gather.1

commit v4 on v0

--- a/solution.py
+++ b/solution.py
@@ -16,6 +16,7 @@
 WIDE = HEADS * HD
 STATE = WIDE + 16
 DEEP = 2 * HD
+COST = 64
 FLOOR = -1e29
 MASKED = -1e30
 NEG = (((1,), (1,)), ((), ()))
@@ -69,7 +70,7 @@
     count = jnp.int32(0)
     for operand, block, offset, other in visits:
         plane = xh ^ 1 if other else xh
-        k_start = (plane * NZ + ((z + NZ - offset) & (NZ - 1))) * QROWS + core * ROWS
+        k_start = (plane * NZ + ((z + NZ - offset * (1 - 2 * core)) & (NZ - 1))) * QROWS + core * ROWS
         needed = (k_start + ROWS > low) & (k_start <= q_last)
 
         @pl.when(needed)
@@ -108,7 +109,7 @@
         ],
         input_output_aliases=aliases,
         cost_estimate=pl.CostEstimate(
-            flops=pairs * HD * 8, bytes_accessed=STATE * QROWS * 8, transcendentals=pairs
+            flops=pairs * HD * COST, bytes_accessed=STATE * QROWS * COST, transcendentals=pairs
         ),
         compiler_params=pltpu.CompilerParams(vmem_limit_bytes=VMEM),
     )(here, lengths, q, *operands)
@@ -195,7 +196,8 @@
 
 
 def ring(value, steps):
-    return lax.ppermute(value, "z", [(i, (i + steps) % NZ) for i in range(NZ)])
+    perm = [(i * NC + c, (i + steps * (1 - 2 * c)) % NZ * NC + c) for i in range(NZ) for c in range(NC)]
+    return lax.ppermute(value, ("z", "core"), perm)
 
 
 def hop(block, dy, dx):
@@ -220,11 +222,22 @@
                 out_ref[row : row + 2, lanes] = ref[y * NX + e]
 
 
-def pass_kernel(across_ref, below_ref, weight_ref, out_ref):
+def pass_kernel(*refs):
     pass
 
 
-def gather_weight(out_weight, after):
+def behind(value, *after):
+    whole = pl.BlockSpec(memory_space=pl.ANY)
+    return pl.pallas_call(
+        pass_kernel,
+        out_shape=jax.ShapeDtypeStruct(value.shape, value.dtype),
+        in_specs=[whole] * (1 + len(after)),
+        out_specs=whole,
+        input_output_aliases={0: 0},
+    )(value, *after)
+
+
+def split_weight(out_weight, after):
     whole = pl.BlockSpec(memory_space=pl.ANY)
     vmem = pl.BlockSpec(memory_space=pltpu.VMEM)
     split = pl.pallas_call(
@@ -233,7 +246,11 @@
         in_specs=[whole, vmem],
         out_specs=vmem,
     )(after, out_weight)
-    split = lax.all_to_all(split, "tp", 0, 0)
+    return lax.all_to_all(split, "tp", 0, 0)
+
+
+def gather_weight(split):
+    vmem = pl.BlockSpec(memory_space=pltpu.VMEM)
     rows = pl.pallas_call(
         stack_kernel,
         out_shape=jax.ShapeDtypeStruct((8, NY * HEADS * WIDE), BF16),
@@ -243,54 +260,35 @@
     return lax.all_gather(rows, "z", axis=0, tiled=True)
 
 
-def exchange_weight(own, across, below):
-    whole = pl.BlockSpec(memory_space=pl.ANY)
-    hbm = pl.BlockSpec(memory_space=pltpu.HBM)
-    own = pl.pallas_call(
-        pass_kernel,
-        out_shape=jax.ShapeDtypeStruct(own.shape, own.dtype),
-        in_specs=[whole, whole, hbm],
-        out_specs=hbm,
-        input_output_aliases={2: 0},
-    )(across, below, own)
-    return own, swap(own, "core")
-
-
 def body(queries, keys, values, doc_lengths, out_weight):
     xh, z, core, tp = (lax.axis_index(name) for name in ("xh", "z", "core", "tp"))
     y, xl = tp // NX, tp % NX
-    here = jnp.stack([z, core, xh, xl]).astype(jnp.int32)
+    here = jnp.stack([z, core, xh]).astype(jnp.int32)
     own = jnp.concatenate([keys, values], axis=0)
     pair = jnp.concatenate([own, swap(own, "xh")], axis=0)
-    weight = gather_weight(out_weight, pair)
     other_q = swap(queries, "core")
     q = jnp.where(core == 0, jnp.concatenate([queries, other_q]), jnp.concatenate([other_q, queries]))
-    up, down = {0: pair}, {0: pair}
-    for s in range(1, NZ // 2):
-        up[s] = ring(up[s - 1], 1)
-        down[s] = ring(down[s - 1], -1)
+    up, down = [pair], [pair]
     far = NZ // 2
-    last_up = ring(up[far - 1][:QROWS], 1)
-    last_down = ring(down[far - 1][QROWS:], -1)
+    for _ in range(1, far):
+        up.append(ring(up[-1], 1))
+        down.append(ring(down[-1], -1))
+    last = [ring(up[-1][:QROWS], 1), ring(down[-1][QROWS:], -1)]
+    split = split_weight(out_weight, own)
 
     state = attend(here, doc_lengths, q, [(0, 0, 0, False), (0, 1, 0, True)], [pair], None)
-    for steps in ((1,), (2, 3), (4, 5), (6,), (7,)):
-        visits, operands = [], []
-        for s in steps:
-            for offset, block in ((s, up[s]), (-s, down[s])):
-                visits += [(len(operands), 0, offset, False), (len(operands), 1, offset, True)]
-                operands.append(block)
-        state = attend(here, doc_lengths, q, visits, operands, state)
-    visits = [(0, 0, far, False), (1, 0, far, True)]
-    state = attend(here, doc_lengths, q, visits, [last_up, last_down], state)
+    weight = gather_weight(behind(split, state))
+    for s in range(1, far):
+        visits = [(0, 0, s, False), (0, 1, s, True), (1, 0, -s, False), (1, 1, -s, True)]
+        state = attend(here, doc_lengths, q, visits, [up[s], down[s]], state)
+    state = attend(here, doc_lengths, q, [(0, 0, far, False), (1, 0, far, True)], last, state)
     attended, a = merge(here, state, swap(state, "core"))
 
-    across = hop(a, 0, 1)
+    weight = behind(weight, a)
+    weights = (weight, swap(weight, "core"))
     below, above = hop(a, 1, 0), hop(a, -1, 0)
-    weights = exchange_weight(weight, across, below)
-    two = hop(below, 1, 0)
-    across_below, across_above = hop(across, 1, 0), hop(across, -1, 0)
-    across_two = hop(across_above, -1, 0)
+    across_below, across_above, across = hop(a, 1, 1), hop(a, -1, 1), hop(a, 0, 1)
+    two, across_two = hop(below, 1, 0), hop(across_above, -1, 0)
     projected = None
     for dy, near, far in (
         (0, a, across),

time: 230 us -> 200 us (0.87)
  Pallas kernels: 49.8 us -> 29.1 us
  waiting for transfers between devices: 50.1 us -> 36.1 us
  starting transfers between devices: 93.6 us -> 107 us
  blocking collectives: 11.8 us -> 0 us
    pallas_call x7 -> x9, Pallas kernels: 33.7 us -> 13 us  [attend(): pl.pallas_call(functools.partial(attend_kernel, visits, state is None), o...]
    all_to_all x1 -> x0, blocking collectives: 11.8 us -> none  [gather_weight(): split = lax.all_to_all(split, 'tp', 0, 0)]
    all_to_all x0 -> x1, starting transfers between devices: none -> 8.57 us  [split_weight(): return lax.all_to_all(split, 'tp', 0, 0)]
    ppermute x7, waiting for transfers between devices: 8.54 us -> 0.02 us  [hop(): return lax.ppermute(block, 'tp', perm)]
    ppermute x5, waiting for transfers between devices: 8.98 us -> 3.06 us  [swap(): return lax.ppermute(value, axis, [(0, 1), (1, 0)])]
    ppermute x16, starting transfers between devices: 55.4 us -> 60.5 us  [ring(): return lax.ppermute(value, ('z', 'core'), perm)]
    unnamed x28 -> x23, local copies, waits for them, and re-layouts: 7.55 us -> 8.5 us
  transfers between devices with their start and end apart: 29 -> 30, of which waited for: 13 -> 11; matrix products, arithmetic and copies ran while one was open for 1% -> 2% of each run, Pallas kernels for 19% -> 13%
where the time goes in v4:
time: 200 us; the launch traced here: 198 us
  starting transfers between devices  107 us (54%)
  waiting for transfers between devices  36.1 us (18%)
  Pallas kernels  29.1 us (15%)
  between operations  14.6 us (7%)
  local copies, waits for them, and re-layouts  9.72 us (5%)
    ppermute x16, starting transfers between devices, ring(): return lax.ppermute(value, ('z', 'core'), perm)  60.5 us
    ppermute x16, waiting for transfers between devices, ring(): return lax.ppermute(value, ('z', 'core'), perm)  33 us
    ppermute x7, starting transfers between devices, hop(): return lax.ppermute(block, 'tp', perm)  24.9 us
    ppermute x5, starting transfers between devices, swap(): return lax.ppermute(value, axis, [(0, 1), (1, 0)])  13.3 us
    pallas_call x9, Pallas kernels, attend(): pl.pallas_call(functools.partial(attend_kernel, visits, state is None), o...  13 us
    pallas_call x4, Pallas kernels, project(): pl.pallas_call(functools.partial(project_kernel, total is None), grid_spe...  11 us
    all_to_all x1, starting transfers between devices, split_weight(): return lax.all_to_all(split, 'tp', 0, 0)  8.57 us
    unnamed x23, local copies, waits for them, and re-layouts  8.5 us
  transfers between devices with their start and end apart: 30, of which 11 were waited for; matrix products, arithmetic and copies ran while one was open for 2% of the time, Pallas kernels for 13%

profile of v4, /device:TPU:6, one launch (start us, length us, event | category | flops | bytes accessed | tf_op | source)
XLA Modules:
  0.0 198.1 jit_solution(14266996874060081032)
XLA Ops:
  10.8 3.3 %collective-permute-start.1 = (bf16[448,128]{1,0:T(8,128)(2,1)S(1)}, bf16[448,128]{1,0:T(8,128)(2,1)S(1)}, u32[]{:S(2)}, u32[]{:S(2)}) collective-permute-start(bf16[448,128]{1,0:T(8,128)(2,1)S(1)} %get-tuple-element.6.after_ref), channel_id=1, source_target_pairs={{0,256},{256,0},{1,257},{257,1},{2,258},{258,2},{3,259},{259,3},{4... | collective-permute-start | bytes 344072 | tf_op jit(solution)/shard_map/ppermute | solution.py:195
  15.7 8.6 %all-to-all-start = ((bf16[8,2,3200]{2,1,0:T(2,128)(2,1)}), bf16[8,2,3200]{2,1,0:T(2,128)(2,1)S(1)}, u32[]{:S(2)}, u32[]{:S(2)}) async-start(bf16[8,2,3200]{2,1,0:T(2,128)(2,1)} %shard_map.78), calls=%async_computation | async-start | bytes 204800 | tf_op jit(solution)/shard_map/all_to_all | solution.py:249
  24.4 8.8 %collective-permute-start.10 = (bf16[896,128]{1,0:T(8,128)(2,1)S(1)}, bf16[896,128]{1,0:T(8,128)(2,1)S(1)}, u32[]{:S(2)}, u32[]{:S(2)}) collective-permute-start(bf16[896,128]{1,0:T(8,128)(2,1)S(1)} %constant_dynamic-update-slice_fusion.2.refs_0_), channel_id=1, source_target_pairs={{0,240},{8,24},{16,0},{24,40},{32,16},{40,56},{48,32},{56,72},{64,... | collective-permute-start | bytes 688136 | tf_op jit(solution)/shard_map/ppermute | solution.py:200
  40.6 4.2 %collective-permute-start.23 = (bf16[8,2,3200]{2,1,0:T(2,128)(2,1)}, bf16[8,2,3200]{2,1,0:T(2,128)(2,1)S(1)}, u32[]{:S(2)}, u32[]{:S(2)}) collective-permute-start(bf16[8,2,3200]{2,1,0:T(2,128)(2,1)} %shard_map.79.mine_ref), channel_id=1, source_target_pairs={{0,256},{256,0},{1,257},{257,1},{2,258},{258,2},{3,259},{259,3},{4... | collective-permute-start | bytes 307208 | tf_op jit(solution)/shard_map/ppermute | solution.py:195
  44.8 5.1 %collective-permute-start.11 = (bf16[896,128]{1,0:T(8,128)(2,1)S(1)}, bf16[896,128]{1,0:T(8,128)(2,1)S(1)}, u32[]{:S(2)}, u32[]{:S(2)}) collective-permute-start(bf16[896,128]{1,0:T(8,128)(2,1)S(1)} %collective-permute-done.10.refs_1_), channel_id=1, source_target_pairs={{0,240},{8,24},{16,0},{24,40},{32,16},{40,56},{48,32},{56,72},{64,... | collective-permute-start | bytes 688136 | tf_op jit(solution)/shard_map/ppermute | solution.py:200
  57.0 5.1 %collective-permute-start.12 = (bf16[896,128]{1,0:T(8,128)(2,1)S(1)}, bf16[896,128]{1,0:T(8,128)(2,1)S(1)}, u32[]{:S(2)}, u32[]{:S(2)}) collective-permute-start(bf16[896,128]{1,0:T(8,128)(2,1)S(1)} %collective-permute-done.11.refs_1_), channel_id=1, source_target_pairs={{0,240},{8,24},{16,0},{24,40},{32,16},{40,56},{48,32},{56,72},{64,... | collective-permute-start | bytes 688136 | tf_op jit(solution)/shard_map/ppermute | solution.py:200
  67.3 5.6 %collective-permute-start.13 = (bf16[896,128]{1,0:T(8,128)(2,1)S(1)}, bf16[896,128]{1,0:T(8,128)(2,1)S(1)}, u32[]{:S(2)}, u32[]{:S(2)}) collective-permute-start(bf16[896,128]{1,0:T(8,128)(2,1)S(1)} %collective-permute-done.12.refs_1_), channel_id=1, source_target_pairs={{0,240},{8,24},{16,0},{24,40},{32,16},{40,56},{48,32},{56,72},{64,... | collective-permute-start | bytes 688136 | tf_op jit(solution)/shard_map/ppermute | solution.py:200
  75.8 5.0 %collective-permute-done.13.refs_1_ = bf16[896,128]{1,0:T(8,128)(2,1)S(1)} collective-permute-done((bf16[896,128]{1,0:T(8,128)(2,1)S(1)}, bf16[896,128]{1,0:T(8,128)(2,1)S(1)}, u32[]{:S(2)}, u32[]{:S(2)}) %collective-permute-start.13) | collective-permute-done | bytes 229408 | tf_op jit(solution)/shard_map/ppermute | solution.py:200
  80.9 5.0 %collective-permute-start.14 = (bf16[896,128]{1,0:T(8,128)(2,1)S(1)}, bf16[896,128]{1,0:T(8,128)(2,1)S(1)}, u32[]{:S(2)}, u32[]{:S(2)}) collective-permute-start(bf16[896,128]{1,0:T(8,128)(2,1)S(1)} %collective-permute-done.13.refs_1_), channel_id=1, source_target_pairs={{0,240},{8,24},{16,0},{24,40},{32,16},{40,56},{48,32},{56,72},{64,... | collective-permute-start | bytes 688136 | tf_op jit(solution)/shard_map/ppermute | solution.py:200
  90.7 3.9 %collective-permute-done.14.refs_1_ = bf16[896,128]{1,0:T(8,128)(2,1)S(1)} collective-permute-done((bf16[896,128]{1,0:T(8,128)(2,1)S(1)}, bf16[896,128]{1,0:T(8,128)(2,1)S(1)}, u32[]{:S(2)}, u32[]{:S(2)}) %collective-permute-start.14) | collective-permute-done | bytes 229408 | tf_op jit(solution)/shard_map/ppermute | solution.py:200
  94.6 4.1 %collective-permute-start.15 = (bf16[896,128]{1,0:T(8,128)(2,1)S(1)}, bf16[896,128]{1,0:T(8,128)(2,1)S(1)}, u32[]{:S(2)}, u32[]{:S(2)}) collective-permute-start(bf16[896,128]{1,0:T(8,128)(2,1)S(1)} %collective-permute-done.14.refs_1_), channel_id=1, source_target_pairs={{0,240},{8,24},{16,0},{24,40},{32,16},{40,56},{48,32},{56,72},{64,... | collective-permute-start | bytes 688136 | tf_op jit(solution)/shard_map/ppermute | solution.py:200
  98.7 4.6 %collective-permute-done.6.refs_0_ = bf16[896,128]{1,0:T(8,128)(2,1)S(1)} collective-permute-done((bf16[896,128]{1,0:T(8,128)(2,1)S(1)}, bf16[896,128]{1,0:T(8,128)(2,1)S(1)}, u32[]{:S(2)}, u32[]{:S(2)}) %collective-permute-start.6) | collective-permute-done | bytes 229408 | tf_op jit(solution)/shard_map/ppermute | solution.py:200
  107.9 5.6 %collective-permute-start.16 = (bf16[896,128]{1,0:T(8,128)(2,1)S(1)}, bf16[896,128]{1,0:T(8,128)(2,1)S(1)}, u32[]{:S(2)}, u32[]{:S(2)}) collective-permute-start(bf16[896,128]{1,0:T(8,128)(2,1)S(1)} %collective-permute-done.15.refs_1_), channel_id=1, source_target_pairs={{0,240},{8,24},{16,0},{24,40},{32,16},{40,56},{48,32},{56,72},{64,... | collective-permute-start | bytes 688136 | tf_op jit(solution)/shard_map/ppermute | solution.py:200
  113.5 5.6 %collective-permute-done.7.refs_0_ = bf16[896,128]{1,0:T(8,128)(2,1)S(1)} collective-permute-done((bf16[896,128]{1,0:T(8,128)(2,1)S(1)}, bf16[896,128]{1,0:T(8,128)(2,1)S(1)}, u32[]{:S(2)}, u32[]{:S(2)}) %collective-permute-start.7) | collective-permute-done | bytes 229408 | tf_op jit(solution)/shard_map/ppermute | solution.py:200
  122.1 5.6 %collective-permute-start.17 = (bf16[448,128]{1,0:T(8,128)(2,1)S(1)}, bf16[448,128]{1,0:T(8,128)(2,1)S(1)}, u32[]{:S(2)}, u32[]{:S(2)}) collective-permute-start(bf16[448,128]{1,0:T(8,128)(2,1)S(1)} %slice.9), channel_id=1, source_target_pairs={{0,240},{8,24},{16,0},{24,40},{32,16},{40,56},{48,32},{56,72},{64,... | collective-permute-start | bytes 344072 | tf_op jit(solution)/shard_map/ppermute | solution.py:200
  127.7 4.3 %collective-permute-done.8.refs_0_ = bf16[896,128]{1,0:T(8,128)(2,1)S(1)} collective-permute-done((bf16[896,128]{1,0:T(8,128)(2,1)S(1)}, bf16[896,128]{1,0:T(8,128)(2,1)S(1)}, u32[]{:S(2)}, u32[]{:S(2)}) %collective-permute-start.8) | collective-permute-done | bytes 229408 | tf_op jit(solution)/shard_map/ppermute | solution.py:200
  134.8 5.2 %collective-permute-done.9.refs_0_ = bf16[448,128]{1,0:T(8,128)(2,1)S(1)} collective-permute-done((bf16[448,128]{1,0:T(8,128)(2,1)S(1)}, bf16[448,128]{1,0:T(8,128)(2,1)S(1)}, u32[]{:S(2)}, u32[]{:S(2)}) %collective-permute-start.9) | collective-permute-done | bytes 114720 | tf_op jit(solution)/shard_map/ppermute | solution.py:200
  142.6 3.0 %collective-permute-done.18.other_ref = f32[656,448]{1,0:T(8,128)S(1)} collective-permute-done((f32[656,448]{1,0:T(8,128)S(1)}, f32[656,448]{1,0:T(8,128)S(1)}, u32[]{:S(2)}, u32[]{:S(2)}) %collective-permute-start.18) | collective-permute-done | bytes 1175584 | tf_op jit(solution)/shard_map/ppermute | solution.py:195
  152.9 3.2 %collective-permute-start.19 = (bf16[224,640]{1,0:T(8,128)(2,1)}, bf16[224,640]{1,0:T(8,128)(2,1)}, u32[]{:S(2)}, u32[]{:S(2)}) collective-permute-start(bf16[224,640]{1,0:T(8,128)(2,1)} %copy-done.3), channel_id=1, source_target_pairs={{0,2},{1,3},{2,4},{3,5},{4,6},{5,7},{6,0},{7,1},{8,10},{9,11},{10,... | collective-permute-start | bytes 860168 | tf_op jit(solution)/shard_map/ppermute | solution.py:207
  156.1 4.8 %collective-permute-start.21 = (bf16[224,640]{1,0:T(8,128)(2,1)}, bf16[224,640]{1,0:T(8,128)(2,1)}, u32[]{:S(2)}, u32[]{:S(2)}) collective-permute-start(bf16[224,640]{1,0:T(8,128)(2,1)} %copy-done.3), channel_id=1, source_target_pairs={{0,7},{1,6},{2,1},{3,0},{4,3},{5,2},{6,5},{7,4},{8,15},{9,14},{10,... | collective-permute-start | bytes 860168 | tf_op jit(solution)/shard_map/ppermute | solution.py:207
  163.6 5.0 %collective-permute-start.25 = (bf16[224,640]{1,0:T(8,128)(2,1)}, bf16[224,640]{1,0:T(8,128)(2,1)}, u32[]{:S(2)}, u32[]{:S(2)}) collective-permute-start(bf16[224,640]{1,0:T(8,128)(2,1)} %copy-done.3), channel_id=1, source_target_pairs={{0,6},{1,7},{2,0},{3,1},{4,2},{5,3},{6,4},{7,5},{8,14},{9,15},{10,... | collective-permute-start | bytes 860168 | tf_op jit(solution)/shard_map/ppermute | solution.py:207
  170.6 5.4 %collective-permute-start.22 = (bf16[224,640]{1,0:T(8,128)(2,1)}, bf16[224,640]{1,0:T(8,128)(2,1)}, u32[]{:S(2)}, u32[]{:S(2)}) collective-permute-start(bf16[224,640]{1,0:T(8,128)(2,1)} %collective-permute-done.21.far_ref), channel_id=1, source_target_pairs={{0,6},{1,7},{2,0},{3,1},{4,2},{5,3},{6,4},{7,5},{8,14},{9,15},{10,... | collective-permute-start | bytes 860168 | tf_op jit(solution)/shard_map/ppermute | solution.py:207
  182.0 2.8 %shard_map.83.refs_0_ = f32[224,640]{1,0:T(8,128)S(1)} custom-call(s32[5]{0:T(128)S(1)} %stack.64.here_ref, bf16[224,640]{1,0:T(8,128)(2,1)} %collective-permute-done.19.near_ref, bf16[224,640]{1,0:T(8,128)(2,1)} %collective-permute-done.26.far_ref, bf16[128,12800]{1,0:T(8,128)(2,1)S(1)} %copy-done, ...), custom_call_target="tpu_custom_call" | custom-call | flops 513802240 | bytes 1638400 | tf_op jit(solution)/shard_map/pallas_call | solution.py:176
  187.6 3.6 %shard_map.85 = f32[224,640]{1,0:T(8,128)} custom-call(s32[5]{0:T(128)S(1)} %stack.60.here_ref, bf16[224,640]{1,0:T(8,128)(2,1)} %collective-permute-done.20.near_ref, bf16[224,640]{1,0:T(8,128)(2,1)} %collective-permute-done.22.far_ref, bf16[128,12800]{1,0:T(8,128)(2,1)S(1)} %copy-done, bf16[128,12800]{1,0:T(8,128)(2,1)S(1)} %collective-permute-done.24.other_ref, ...), custom_call_target="tpu_custom_call" | custom-call | flops 513802240 | bytes 1638400 | tf_op jit(solution)/shard_map/pallas_call | solution.py:176
  (88 shorter events, 66.1 us)
Async XLA Ops:
  7.2 27.9 %collective-permute-start = (bf16[224,640]{1,0:T(8,128)(2,1)}, bf16[224,640]{1,0:T(8,128)(2,1)S(1)}, u32[]{:S(2)}, u32[]{:S(2)}) collective-permute-start(bf16[224,640]{1,0:T(8,128)(2,1)} %param.5), channel_id=1, source_target_pairs={{0,8},{8,0},{1,9},{9,1},{2,10},{10,2},{3,11},{11,3},{4,12},{12,4},... | collective-permute-start | bytes 860168 | tf_op jit(solution)/shard_map/ppermute | solution.py:195
  10.8 13.5 %collective-permute-start.1 = (bf16[448,128]{1,0:T(8,128)(2,1)S(1)}, bf16[448,128]{1,0:T(8,128)(2,1)S(1)}, u32[]{:S(2)}, u32[]{:S(2)}) collective-permute-start(bf16[448,128]{1,0:T(8,128)(2,1)S(1)} %get-tuple-element.6.after_ref), channel_id=1, source_target_pairs={{0,256},{256,0},{1,257},{257,1},{2,258},{258,2},{3,259},{259,3},{4... | collective-permute-start | bytes 344072 | tf_op jit(solution)/shard_map/ppermute | solution.py:195
  15.7 24.3 %all-to-all-start = ((bf16[8,2,3200]{2,1,0:T(2,128)(2,1)}), bf16[8,2,3200]{2,1,0:T(2,128)(2,1)S(1)}, u32[]{:S(2)}, u32[]{:S(2)}) async-start(bf16[8,2,3200]{2,1,0:T(2,128)(2,1)} %shard_map.78), calls=%async_computation | async-start | bytes 204800 | tf_op jit(solution)/shard_map/all_to_all | solution.py:249
  24.3 124.0 %all-gather.2.cloned.1.call-start = ((), (), s32[]{:S(2)}) async-start(), calls=%async_computation.1 | async-start | bytes 3481600 | tf_op jit(solution)/shard_map/all_gather | solution.py:260
  24.4 20.4 %collective-permute-start.10 = (bf16[896,128]{1,0:T(8,128)(2,1)S(1)}, bf16[896,128]{1,0:T(8,128)(2,1)S(1)}, u32[]{:S(2)}, u32[]{:S(2)}) collective-permute-start(bf16[896,128]{1,0:T(8,128)(2,1)S(1)} %constant_dynamic-update-slice_fusion.2.refs_0_), channel_id=1, source_target_pairs={{0,240},{8,24},{16,0},{24,40},{32,16},{40,56},{48,32},{56,72},{64,... | collective-permute-start | bytes 688136 | tf_op jit(solution)/shard_map/ppermute | solution.py:200
  33.1 16.8 %collective-permute-start.2 = (bf16[896,128]{1,0:T(8,128)(2,1)S(1)}, bf16[896,128]{1,0:T(8,128)(2,1)S(1)}, u32[]{:S(2)}, u32[]{:S(2)}) collective-permute-start(bf16[896,128]{1,0:T(8,128)(2,1)S(1)} %constant_dynamic-update-slice_fusion.2.refs_0_), channel_id=1, source_target_pairs={{0,16},{8,248},{16,32},{24,8},{32,48},{40,24},{48,64},{56,40},{64,... | collective-permute-start | bytes 688136 | tf_op jit(solution)/shard_map/ppermute | solution.py:200
  40.6 13.9 %collective-permute-start.23 = (bf16[8,2,3200]{2,1,0:T(2,128)(2,1)}, bf16[8,2,3200]{2,1,0:T(2,128)(2,1)S(1)}, u32[]{:S(2)}, u32[]{:S(2)}) collective-permute-start(bf16[8,2,3200]{2,1,0:T(2,128)(2,1)} %shard_map.79.mine_ref), channel_id=1, source_target_pairs={{0,256},{256,0},{1,257},{257,1},{2,258},{258,2},{3,259},{259,3},{4... | collective-permute-start | bytes 307208 | tf_op jit(solution)/shard_map/ppermute | solution.py:195
  67.3 13.5 %collective-permute-start.13 = (bf16[896,128]{1,0:T(8,128)(2,1)S(1)}, bf16[896,128]{1,0:T(8,128)(2,1)S(1)}, u32[]{:S(2)}, u32[]{:S(2)}) collective-permute-start(bf16[896,128]{1,0:T(8,128)(2,1)S(1)} %collective-permute-done.12.refs_1_), channel_id=1, source_target_pairs={{0,240},{8,24},{16,0},{24,40},{32,16},{40,56},{48,32},{56,72},{64,... | collective-permute-start | bytes 688136 | tf_op jit(solution)/shard_map/ppermute | solution.py:200
  72.9 14.8 %collective-permute-start.5 = (bf16[896,128]{1,0:T(8,128)(2,1)S(1)}, bf16[896,128]{1,0:T(8,128)(2,1)S(1)}, u32[]{:S(2)}, u32[]{:S(2)}) collective-permute-start(bf16[896,128]{1,0:T(8,128)(2,1)S(1)} %collective-permute-done.4.refs_0_), channel_id=1, source_target_pairs={{0,16},{8,248},{16,32},{24,8},{32,48},{40,24},{48,64},{56,40},{64,... | collective-permute-start | bytes 688136 | tf_op jit(solution)/shard_map/ppermute | solution.py:200
  80.9 13.7 %collective-permute-start.14 = (bf16[896,128]{1,0:T(8,128)(2,1)S(1)}, bf16[896,128]{1,0:T(8,128)(2,1)S(1)}, u32[]{:S(2)}, u32[]{:S(2)}) collective-permute-start(bf16[896,128]{1,0:T(8,128)(2,1)S(1)} %collective-permute-done.13.refs_1_), channel_id=1, source_target_pairs={{0,240},{8,24},{16,0},{24,40},{32,16},{40,56},{48,32},{56,72},{64,... | collective-permute-start | bytes 688136 | tf_op jit(solution)/shard_map/ppermute | solution.py:200
  87.8 15.5 %collective-permute-start.6 = (bf16[896,128]{1,0:T(8,128)(2,1)S(1)}, bf16[896,128]{1,0:T(8,128)(2,1)S(1)}, u32[]{:S(2)}, u32[]{:S(2)}) collective-permute-start(bf16[896,128]{1,0:T(8,128)(2,1)S(1)} %collective-permute-done.5.refs_0_), channel_id=1, source_target_pairs={{0,16},{8,248},{16,32},{24,8},{32,48},{40,24},{48,64},{56,40},{64,... | collective-permute-start | bytes 688136 | tf_op jit(solution)/shard_map/ppermute | solution.py:200
  94.6 13.3 %collective-permute-start.15 = (bf16[896,128]{1,0:T(8,128)(2,1)S(1)}, bf16[896,128]{1,0:T(8,128)(2,1)S(1)}, u32[]{:S(2)}, u32[]{:S(2)}) collective-permute-start(bf16[896,128]{1,0:T(8,128)(2,1)S(1)} %collective-permute-done.14.refs_1_), channel_id=1, source_target_pairs={{0,240},{8,24},{16,0},{24,40},{32,16},{40,56},{48,32},{56,72},{64,... | collective-permute-start | bytes 688136 | tf_op jit(solution)/shard_map/ppermute | solution.py:200
  103.3 15.8 %collective-permute-start.7 = (bf16[896,128]{1,0:T(8,128)(2,1)S(1)}, bf16[896,128]{1,0:T(8,128)(2,1)S(1)}, u32[]{:S(2)}, u32[]{:S(2)}) collective-permute-start(bf16[896,128]{1,0:T(8,128)(2,1)S(1)} %collective-permute-done.6.refs_0_), channel_id=1, source_target_pairs={{0,16},{8,248},{16,32},{24,8},{32,48},{40,24},{48,64},{56,40},{64,... | collective-permute-start | bytes 688136 | tf_op jit(solution)/shard_map/ppermute | solution.py:200
  107.9 14.2 %collective-permute-start.16 = (bf16[896,128]{1,0:T(8,128)(2,1)S(1)}, bf16[896,128]{1,0:T(8,128)(2,1)S(1)}, u32[]{:S(2)}, u32[]{:S(2)}) collective-permute-start(bf16[896,128]{1,0:T(8,128)(2,1)S(1)} %collective-permute-done.15.refs_1_), channel_id=1, source_target_pairs={{0,240},{8,24},{16,0},{24,40},{32,16},{40,56},{48,32},{56,72},{64,... | collective-permute-start | bytes 688136 | tf_op jit(solution)/shard_map/ppermute | solution.py:200
  119.1 12.9 %collective-permute-start.8 = (bf16[896,128]{1,0:T(8,128)(2,1)S(1)}, bf16[896,128]{1,0:T(8,128)(2,1)S(1)}, u32[]{:S(2)}, u32[]{:S(2)}) collective-permute-start(bf16[896,128]{1,0:T(8,128)(2,1)S(1)} %collective-permute-done.7.refs_0_), channel_id=1, source_target_pairs={{0,16},{8,248},{16,32},{24,8},{32,48},{40,24},{48,64},{56,40},{64,... | collective-permute-start | bytes 688136 | tf_op jit(solution)/shard_map/ppermute | solution.py:200
  122.1 12.6 %collective-permute-start.17 = (bf16[448,128]{1,0:T(8,128)(2,1)S(1)}, bf16[448,128]{1,0:T(8,128)(2,1)S(1)}, u32[]{:S(2)}, u32[]{:S(2)}) collective-permute-start(bf16[448,128]{1,0:T(8,128)(2,1)S(1)} %slice.9), channel_id=1, source_target_pairs={{0,240},{8,24},{16,0},{24,40},{32,16},{40,56},{48,32},{56,72},{64,... | collective-permute-start | bytes 344072 | tf_op jit(solution)/shard_map/ppermute | solution.py:200
  148.2 28.2 %collective-permute-start.24 = (bf16[128,12800]{1,0:T(8,128)(2,1)}, bf16[128,12800]{1,0:T(8,128)(2,1)S(1)}, u32[]{:S(2)}, u32[]{:S(2)}) collective-permute-start(bf16[128,12800]{1,0:T(8,128)(2,1)} %shard_map.81.own_ref), channel_id=1, source_target_pairs={{0,8},{8,0},{1,9},{9,1},{2,10},{10,2},{3,11},{11,3},{4,12},{12,4},... | collective-permute-start | bytes 9830408 | tf_op jit(solution)/shard_map/ppermute | solution.py:195
  150.3 12.6 %collective-permute-start.27 = (bf16[224,640]{1,0:T(8,128)(2,1)}, bf16[224,640]{1,0:T(8,128)(2,1)S(1)}, u32[]{:S(2)}, u32[]{:S(2)}) collective-permute-start(bf16[224,640]{1,0:T(8,128)(2,1)} %copy-done.3), channel_id=1, source_target_pairs={{0,1},{1,0},{2,3},{3,2},{4,5},{5,4},{6,7},{7,6},{8,9},{9,8},{10,11... | collective-permute-start | bytes 860168 | tf_op jit(solution)/shard_map/ppermute | solution.py:207
  152.9 15.8 %collective-permute-start.19 = (bf16[224,640]{1,0:T(8,128)(2,1)}, bf16[224,640]{1,0:T(8,128)(2,1)}, u32[]{:S(2)}, u32[]{:S(2)}) collective-permute-start(bf16[224,640]{1,0:T(8,128)(2,1)} %copy-done.3), channel_id=1, source_target_pairs={{0,2},{1,3},{2,4},{3,5},{4,6},{5,7},{6,0},{7,1},{8,10},{9,11},{10,... | collective-permute-start | bytes 860168 | tf_op jit(solution)/shard_map/ppermute | solution.py:207
  156.1 14.4 %collective-permute-start.21 = (bf16[224,640]{1,0:T(8,128)(2,1)}, bf16[224,640]{1,0:T(8,128)(2,1)}, u32[]{:S(2)}, u32[]{:S(2)}) collective-permute-start(bf16[224,640]{1,0:T(8,128)(2,1)} %copy-done.3), channel_id=1, source_target_pairs={{0,7},{1,6},{2,1},{3,0},{4,3},{5,2},{6,5},{7,4},{8,15},{9,14},{10,... | collective-permute-start | bytes 860168 | tf_op jit(solution)/shard_map/ppermute | solution.py:207
  160.9 21.0 %collective-permute-start.26 = (bf16[224,640]{1,0:T(8,128)(2,1)}, bf16[224,640]{1,0:T(8,128)(2,1)}, u32[]{:S(2)}, u32[]{:S(2)}) collective-permute-start(bf16[224,640]{1,0:T(8,128)(2,1)} %copy-done.3), channel_id=1, source_target_pairs={{0,3},{1,2},{2,5},{3,4},{4,7},{5,6},{6,1},{7,0},{8,11},{9,10},{10,... | collective-permute-start | bytes 860168 | tf_op jit(solution)/shard_map/ppermute | solution.py:207
  163.6 21.2 %collective-permute-start.25 = (bf16[224,640]{1,0:T(8,128)(2,1)}, bf16[224,640]{1,0:T(8,128)(2,1)}, u32[]{:S(2)}, u32[]{:S(2)}) collective-permute-start(bf16[224,640]{1,0:T(8,128)(2,1)} %copy-done.3), channel_id=1, source_target_pairs={{0,6},{1,7},{2,0},{3,1},{4,2},{5,3},{6,4},{7,5},{8,14},{9,15},{10,... | collective-permute-start | bytes 860168 | tf_op jit(solution)/shard_map/ppermute | solution.py:207
  168.6 19.0 %collective-permute-start.20 = (bf16[224,640]{1,0:T(8,128)(2,1)}, bf16[224,640]{1,0:T(8,128)(2,1)}, u32[]{:S(2)}, u32[]{:S(2)}) collective-permute-start(bf16[224,640]{1,0:T(8,128)(2,1)} %collective-permute-done.19.near_ref), channel_id=1, source_target_pairs={{0,2},{1,3},{2,4},{3,5},{4,6},{5,7},{6,0},{7,1},{8,10},{9,11},{10,... | collective-permute-start | bytes 860168 | tf_op jit(solution)/shard_map/ppermute | solution.py:207
  170.6 17.1 %collective-permute-start.22 = (bf16[224,640]{1,0:T(8,128)(2,1)}, bf16[224,640]{1,0:T(8,128)(2,1)}, u32[]{:S(2)}, u32[]{:S(2)}) collective-permute-start(bf16[224,640]{1,0:T(8,128)(2,1)} %collective-permute-done.21.far_ref), channel_id=1, source_target_pairs={{0,6},{1,7},{2,0},{3,1},{4,2},{5,3},{6,4},{7,5},{8,14},{9,15},{10,... | collective-permute-start | bytes 860168 | tf_op jit(solution)/shard_map/ppermute | solution.py:207
  (17 other events, 109.8 us)
Sparse Core Ops, SparseCore 0:
  57.1 79.3 all-gather.1

commit v5 on v3

--- a/solution.py
+++ b/solution.py
@@ -115,7 +115,7 @@
     )(here, lengths, q, *operands)
 
 
-def merge_kernel(here_ref, mine_ref, other_ref, out_ref, a_ref, full):
+def merge_kernel(mine_ref, other_ref, out_ref, a_ref):
     for h in range(HEADS):
         rows = slice(h * HD, (h + 1) * HD)
         top = slice(WIDE + h, WIDE + h + 1)
@@ -124,13 +124,12 @@
         mine, other = jnp.exp2(mine_ref[top] - m), jnp.exp2(other_ref[top] - m)
         den = mine * mine_ref[total] + other * other_ref[total]
         mixed = (mine_ref[rows] * mine + other_ref[rows] * other) / den
-        full[:, rows] = mixed.T
-    own = full[pl.ds(pl.multiple_of(here_ref[1] * ROWS, ROWS), ROWS)]
-    out_ref[...] = own
-    a_ref[...] = own.astype(BF16)
-
-
-def merge(here, mine, other):
+        mixed = mixed.T
+        out_ref[:, rows] = mixed
+        a_ref[:, rows] = mixed.astype(BF16)
+
+
+def merge(mine, other):
     vmem = pl.BlockSpec(memory_space=pltpu.VMEM)
     return pl.pallas_call(
         merge_kernel,
@@ -138,14 +137,13 @@
             jax.ShapeDtypeStruct((ROWS, WIDE), F32),
             jax.ShapeDtypeStruct((ROWS, WIDE), BF16),
         ),
-        in_specs=[pl.BlockSpec(memory_space=pltpu.SMEM), vmem, vmem],
+        in_specs=[vmem, vmem],
         out_specs=(vmem, vmem),
-        scratch_shapes=[pltpu.VMEM((QROWS, WIDE), F32)],
         cost_estimate=pl.CostEstimate(
             flops=QROWS * WIDE * 100, bytes_accessed=STATE * QROWS * 12, transcendentals=QROWS * 16
         ),
         compiler_params=pltpu.CompilerParams(vmem_limit_bytes=VMEM),
-    )(here, mine, other)
+    )(mine, other)
 
 
 def project_kernel(here_ref, own_ref, other_ref, a_ref, out_ref):
@@ -266,7 +264,9 @@
         visits = [(0, 0, s, False), (0, 1, s, True), (1, 0, -s, False), (1, 1, -s, True)]
         state = attend(here, doc_lengths, q, visits, [up[s], down[s]], state)
     state = attend(here, doc_lengths, q, [(0, 0, far, False), (1, 0, far, True)], last, state)
-    attended, a = merge(here, state, swap(state, "core"))
+    low, high = state[:, :ROWS], state[:, ROWS:]
+    sent, kept = jnp.where(core == 0, high, low), jnp.where(core == 0, low, high)
+    attended, a = merge(kept, swap(sent, "core"))
 
     weight = behind(weight, a)
     sources = lax.all_to_all(jnp.broadcast_to(a[None], (NY * NX, ROWS, WIDE)), "tp", 0, 0)

time: 193 us -> 192 us (level)
  Pallas kernels: 38.5 us -> 21 us
  waiting for transfers between devices: 16.8 us -> 31.2 us
    pallas_call x9, Pallas kernels: 27.8 us -> 11.1 us  [attend(): pl.pallas_call(functools.partial(attend_kernel, visits, state is None), o...]
    ppermute x16, waiting for transfers between devices: 13.8 us -> 29.1 us  [ring(): return lax.ppermute(value, 'z', [(i, (i + steps) % NZ) for i in range(NZ)])]
  transfers between devices with their start and end apart: 23 -> 23, of which waited for: 6 -> 11; matrix products, arithmetic and copies ran while one was open for 2% -> 2% of each run, Pallas kernels for 17% -> 8%
where the time goes in v5:
time: 192 us; the launch traced here: 191 us
  starting transfers between devices  83.5 us (43%)
  blocking collectives  33.9 us (18%)
  waiting for transfers between devices  31.2 us (16%)
  Pallas kernels  21 us (11%)
  between operations  14.4 us (8%)
  local copies, waits for them, and re-layouts  4.99 us (3%)
    ppermute x16, starting transfers between devices, ring(): return lax.ppermute(value, 'z', [(i, (i + steps) % NZ) for i in range(NZ)])  61.4 us
    all_to_all x1, blocking collectives, body(): lax.all_to_all(jnp.broadcast_to(a[None], (NY * NX, ROWS, WIDE)), 'tp', 0, 0)  33.9 us
    ppermute x16, waiting for transfers between devices, ring(): return lax.ppermute(value, 'z', [(i, (i + steps) % NZ) for i in range(NZ)])  29.1 us
    ppermute x5, starting transfers between devices, swap(): return lax.ppermute(value, axis, [(0, 1), (1, 0)])  13.5 us
    pallas_call x9, Pallas kernels, attend(): pl.pallas_call(functools.partial(attend_kernel, visits, state is None), o...  11.1 us
    all_to_all x1, starting transfers between devices, split_weight(): return lax.all_to_all(split, 'tp', 0, 0)  8.57 us
    pallas_call x1, Pallas kernels, project(): pl.pallas_call(project_kernel, out_shape=jax.ShapeDtypeStruct((ROWS, WIDE...  5.51 us
    unnamed x19, local copies, waits for them, and re-layouts  3.93 us
  transfers between devices with their start and end apart: 23, of which 11 were waited for; matrix products, arithmetic and copies ran while one was open for 2% of the time, Pallas kernels for 8%

profile of v5, /device:TPU:6, one launch (start us, length us, event | category | flops | bytes accessed | tf_op | source)
XLA Modules:
  0.0 190.5 jit_solution(4797041446600757730)
XLA Ops:
  10.8 3.3 %collective-permute-start.1 = (bf16[448,128]{1,0:T(8,128)(2,1)S(1)}, bf16[448,128]{1,0:T(8,128)(2,1)S(1)}, u32[]{:S(2)}, u32[]{:S(2)}) collective-permute-start(bf16[448,128]{1,0:T(8,128)(2,1)S(1)} %get-tuple-element.8.after_ref), channel_id=1, source_target_pairs={{0,256},{256,0},{1,257},{257,1},{2,258},{258,2},{3,259},{259,3},{4... | collective-permute-start | bytes 344072 | tf_op jit(solution)/shard_map/ppermute | solution.py:186
  15.7 8.6 %all-to-all-start = ((bf16[8,2,3200]{2,1,0:T(2,128)(2,1)}), bf16[8,2,3200]{2,1,0:T(2,128)(2,1)S(1)}, u32[]{:S(2)}, u32[]{:S(2)}) async-start(bf16[8,2,3200]{2,1,0:T(2,128)(2,1)} %shard_map.78), calls=%async_computation | async-start | bytes 204800 | tf_op jit(solution)/shard_map/all_to_all | solution.py:232
  24.4 8.8 %collective-permute-start.10 = (bf16[896,128]{1,0:T(8,128)(2,1)S(1)}, bf16[896,128]{1,0:T(8,128)(2,1)S(1)}, u32[]{:S(2)}, u32[]{:S(2)}) collective-permute-start(bf16[896,128]{1,0:T(8,128)(2,1)S(1)} %constant_dynamic-update-slice_fusion.2.refs_0_), channel_id=1, source_target_pairs={{0,240},{16,0},{32,16},{48,32},{64,48},{80,64},{96,80},{112,96},{1... | collective-permute-start | bytes 688136 | tf_op jit(solution)/shard_map/ppermute | solution.py:190
  36.3 2.5 %shard_map.68.refs_2_.refs_1_ = f32[656,448]{1,0:T(8,128)S(1)} custom-call(s32[3]{0:T(128)S(1)} %pad_add_fusion.here_ref, s32[16]{0:T(128)S(1)} %copy-done.5, bf16[448,640]{1,0:T(8,128)(2,1)S(1)} %maximum_select_fusion.q_ref, bf16[896,128]{1,0:T(8,128)(2,1)S(1)} %constant_dynamic-update-slice_fusion.2.refs_0_), custom_call_target="tpu_custom_call" | custom-call | flops 4110417920 | bytes 18808832 | tf_op jit(solution)/shard_map/pallas_call | solution.py:101
  40.6 4.2 %collective-permute-start.19 = (bf16[8,2,3200]{2,1,0:T(2,128)(2,1)}, bf16[8,2,3200]{2,1,0:T(2,128)(2,1)S(1)}, u32[]{:S(2)}, u32[]{:S(2)}) collective-permute-start(bf16[8,2,3200]{2,1,0:T(2,128)(2,1)} %shard_map.79.mine_ref), channel_id=1, source_target_pairs={{0,256},{256,0},{1,257},{257,1},{2,258},{258,2},{3,259},{259,3},{4... | collective-permute-start | bytes 307208 | tf_op jit(solution)/shard_map/ppermute | solution.py:186
  44.7 5.1 %collective-permute-start.11 = (bf16[896,128]{1,0:T(8,128)(2,1)S(1)}, bf16[896,128]{1,0:T(8,128)(2,1)S(1)}, u32[]{:S(2)}, u32[]{:S(2)}) collective-permute-start(bf16[896,128]{1,0:T(8,128)(2,1)S(1)} %collective-permute-done.10.refs_1_), channel_id=1, source_target_pairs={{0,240},{16,0},{32,16},{48,32},{64,48},{80,64},{96,80},{112,96},{1... | collective-permute-start | bytes 688136 | tf_op jit(solution)/shard_map/ppermute | solution.py:190
  54.3 2.7 %shard_map.69.refs_2_ = f32[656,448]{1,0:T(8,128)S(1)} custom-call(s32[3]{0:T(128)S(1)} %pad_add_fusion.here_ref, s32[16]{0:T(128)S(1)} %copy-done.5, bf16[448,640]{1,0:T(8,128)(2,1)S(1)} %maximum_select_fusion.q_ref, bf16[896,128]{1,0:T(8,128)(2,1)S(1)} %collective-permute-done.2.refs_0_, ...), custom_call_target="tpu_custom_call", output_to_operand_aliasing={{}: (5, {})} | custom-call | flops 8220835840 | bytes 18808832 | tf_op jit(solution)/shard_map/pallas_call | solution.py:101
  56.9 3.3 %collective-permute-start.12 = (bf16[896,128]{1,0:T(8,128)(2,1)S(1)}, bf16[896,128]{1,0:T(8,128)(2,1)S(1)}, u32[]{:S(2)}, u32[]{:S(2)}) collective-permute-start(bf16[896,128]{1,0:T(8,128)(2,1)S(1)} %collective-permute-done.11.refs_1_), channel_id=1, source_target_pairs={{0,240},{16,0},{32,16},{48,32},{64,48},{80,64},{96,80},{112,96},{1... | collective-permute-start | bytes 688136 | tf_op jit(solution)/shard_map/ppermute | solution.py:190
  60.2 2.6 %collective-permute-start.4 = (bf16[896,128]{1,0:T(8,128)(2,1)S(1)}, bf16[896,128]{1,0:T(8,128)(2,1)S(1)}, u32[]{:S(2)}, u32[]{:S(2)}) collective-permute-start(bf16[896,128]{1,0:T(8,128)(2,1)S(1)} %collective-permute-done.3.refs_0_), channel_id=1, source_target_pairs={{0,16},{16,32},{32,48},{48,64},{64,80},{80,96},{96,112},{112,128},... | collective-permute-start | bytes 688136 | tf_op jit(solution)/shard_map/ppermute | solution.py:190
  65.3 5.6 %collective-permute-start.13 = (bf16[896,128]{1,0:T(8,128)(2,1)S(1)}, bf16[896,128]{1,0:T(8,128)(2,1)S(1)}, u32[]{:S(2)}, u32[]{:S(2)}) collective-permute-start(bf16[896,128]{1,0:T(8,128)(2,1)S(1)} %collective-permute-done.12.refs_1_), channel_id=1, source_target_pairs={{0,240},{16,0},{32,16},{48,32},{64,48},{80,64},{96,80},{112,96},{1... | collective-permute-start | bytes 688136 | tf_op jit(solution)/shard_map/ppermute | solution.py:190
  73.8 5.2 %collective-permute-done.13.refs_1_ = bf16[896,128]{1,0:T(8,128)(2,1)S(1)} collective-permute-done((bf16[896,128]{1,0:T(8,128)(2,1)S(1)}, bf16[896,128]{1,0:T(8,128)(2,1)S(1)}, u32[]{:S(2)}, u32[]{:S(2)}) %collective-permute-start.13) | collective-permute-done | bytes 229408 | tf_op jit(solution)/shard_map/ppermute | solution.py:190
  79.1 5.5 %collective-permute-start.14 = (bf16[896,128]{1,0:T(8,128)(2,1)S(1)}, bf16[896,128]{1,0:T(8,128)(2,1)S(1)}, u32[]{:S(2)}, u32[]{:S(2)}) collective-permute-start(bf16[896,128]{1,0:T(8,128)(2,1)S(1)} %collective-permute-done.13.refs_1_), channel_id=1, source_target_pairs={{0,240},{16,0},{32,16},{48,32},{64,48},{80,64},{96,80},{112,96},{1... | collective-permute-start | bytes 688136 | tf_op jit(solution)/shard_map/ppermute | solution.py:190
  88.5 4.7 %collective-permute-done.14.refs_1_ = bf16[896,128]{1,0:T(8,128)(2,1)S(1)} collective-permute-done((bf16[896,128]{1,0:T(8,128)(2,1)S(1)}, bf16[896,128]{1,0:T(8,128)(2,1)S(1)}, u32[]{:S(2)}, u32[]{:S(2)}) %collective-permute-start.14) | collective-permute-done | bytes 229408 | tf_op jit(solution)/shard_map/ppermute | solution.py:190
  93.2 5.4 %collective-permute-start.15 = (bf16[896,128]{1,0:T(8,128)(2,1)S(1)}, bf16[896,128]{1,0:T(8,128)(2,1)S(1)}, u32[]{:S(2)}, u32[]{:S(2)}) collective-permute-start(bf16[896,128]{1,0:T(8,128)(2,1)S(1)} %collective-permute-done.14.refs_1_), channel_id=1, source_target_pairs={{0,240},{16,0},{32,16},{48,32},{64,48},{80,64},{96,80},{112,96},{1... | collective-permute-start | bytes 688136 | tf_op jit(solution)/shard_map/ppermute | solution.py:190
  99.3 2.4 %collective-permute-start.7 = (bf16[896,128]{1,0:T(8,128)(2,1)S(1)}, bf16[896,128]{1,0:T(8,128)(2,1)S(1)}, u32[]{:S(2)}, u32[]{:S(2)}) collective-permute-start(bf16[896,128]{1,0:T(8,128)(2,1)S(1)} %collective-permute-done.6.refs_0_), channel_id=1, source_target_pairs={{0,16},{16,32},{32,48},{48,64},{64,80},{80,96},{96,112},{112,128},... | collective-permute-start | bytes 688136 | tf_op jit(solution)/shard_map/ppermute | solution.py:190
  102.5 2.7 %collective-permute-done.15.refs_1_ = bf16[896,128]{1,0:T(8,128)(2,1)S(1)} collective-permute-done((bf16[896,128]{1,0:T(8,128)(2,1)S(1)}, bf16[896,128]{1,0:T(8,128)(2,1)S(1)}, u32[]{:S(2)}, u32[]{:S(2)}) %collective-permute-start.15) | collective-permute-done | bytes 229408 | tf_op jit(solution)/shard_map/ppermute | solution.py:190
  105.2 5.7 %collective-permute-start.16 = (bf16[896,128]{1,0:T(8,128)(2,1)S(1)}, bf16[896,128]{1,0:T(8,128)(2,1)S(1)}, u32[]{:S(2)}, u32[]{:S(2)}) collective-permute-start(bf16[896,128]{1,0:T(8,128)(2,1)S(1)} %collective-permute-done.15.refs_1_), channel_id=1, source_target_pairs={{0,240},{16,0},{32,16},{48,32},{64,48},{80,64},{96,80},{112,96},{1... | collective-permute-start | bytes 688136 | tf_op jit(solution)/shard_map/ppermute | solution.py:190
  110.9 2.6 %collective-permute-done.7.refs_0_ = bf16[896,128]{1,0:T(8,128)(2,1)S(1)} collective-permute-done((bf16[896,128]{1,0:T(8,128)(2,1)S(1)}, bf16[896,128]{1,0:T(8,128)(2,1)S(1)}, u32[]{:S(2)}, u32[]{:S(2)}) %collective-permute-start.7) | collective-permute-done | bytes 229408 | tf_op jit(solution)/shard_map/ppermute | solution.py:190
  118.0 5.7 %collective-permute-start.17 = (bf16[448,128]{1,0:T(8,128)(2,1)S(1)}, bf16[448,128]{1,0:T(8,128)(2,1)S(1)}, u32[]{:S(2)}, u32[]{:S(2)}) collective-permute-start(bf16[448,128]{1,0:T(8,128)(2,1)S(1)} %slice.17), channel_id=1, source_target_pairs={{0,240},{16,0},{32,16},{48,32},{64,48},{80,64},{96,80},{112,96},{1... | collective-permute-start | bytes 344072 | tf_op jit(solution)/shard_map/ppermute | solution.py:190
  123.7 3.4 %collective-permute-done.8.refs_0_ = bf16[896,128]{1,0:T(8,128)(2,1)S(1)} collective-permute-done((bf16[896,128]{1,0:T(8,128)(2,1)S(1)}, bf16[896,128]{1,0:T(8,128)(2,1)S(1)}, u32[]{:S(2)}, u32[]{:S(2)}) %collective-permute-start.8) | collective-permute-done | bytes 229408 | tf_op jit(solution)/shard_map/ppermute | solution.py:190
  129.9 5.2 %collective-permute-done.9.refs_0_ = bf16[448,128]{1,0:T(8,128)(2,1)S(1)} collective-permute-done((bf16[448,128]{1,0:T(8,128)(2,1)S(1)}, bf16[448,128]{1,0:T(8,128)(2,1)S(1)}, u32[]{:S(2)}, u32[]{:S(2)}) %collective-permute-start.9) | collective-permute-done | bytes 114720 | tf_op jit(solution)/shard_map/ppermute | solution.py:190
  141.8 2.2 %collective-permute-start.20 = (bf16[128,12800]{1,0:T(8,128)(2,1)}, bf16[128,12800]{1,0:T(8,128)(2,1)S(1)}, u32[]{:S(2)}, u32[]{:S(2)}) collective-permute-start(bf16[128,12800]{1,0:T(8,128)(2,1)} %shard_map.81.own_ref), channel_id=1, source_target_pairs={{0,8},{8,0},{1,9},{9,1},{2,10},{10,2},{3,11},{11,3},{4,12},{12,4},... | collective-permute-start | bytes 9830408 | tf_op jit(solution)/shard_map/ppermute | solution.py:186
  144.2 33.9 %all_to_all.10.a_ref = bf16[8,224,640]{2,1,0:T(8,128)(2,1)S(1)} all-to-all(bf16[8,224,640]{2,1,0:T(8,128)(2,1)S(1)} %broadcast_in_dim.2), channel_id=1, replica_groups=mesh['xh'=2,'z'=16,'core'=2,'tp'=8] {'tp'}, dimensions={0} | all-to-all | bytes 4587520 | tf_op jit(solution)/shard_map/all_to_all | solution.py:272
  178.2 5.5 %shard_map.82 = f32[224,640]{1,0:T(8,128)} custom-call(s32[3]{0:T(128)S(1)} %pad_add_fusion.here_ref, bf16[128,12800]{1,0:T(8,128)(2,1)S(1)} %copy-done, bf16[128,12800]{1,0:T(8,128)(2,1)S(1)} %collective-permute-done.20.other_ref, bf16[8,224,640]{2,1,0:T(8,128)(2,1)S(1)} %all_to_all.10.a_ref), custom_call_target="tpu_custom_call" | custom-call | flops 2055208960 | bytes 6553600 | tf_op jit(solution)/shard_map/pallas_call | solution.py:171
  (66 shorter events, 39.5 us)
Async XLA Ops:
  7.2 27.9 %collective-permute-start = (bf16[224,640]{1,0:T(8,128)(2,1)}, bf16[224,640]{1,0:T(8,128)(2,1)S(1)}, u32[]{:S(2)}, u32[]{:S(2)}) collective-permute-start(bf16[224,640]{1,0:T(8,128)(2,1)} %param.5), channel_id=1, source_target_pairs={{0,8},{8,0},{1,9},{9,1},{2,10},{10,2},{3,11},{11,3},{4,12},{12,4},... | collective-permute-start | bytes 860168 | tf_op jit(solution)/shard_map/ppermute | solution.py:186
  10.8 13.5 %collective-permute-start.1 = (bf16[448,128]{1,0:T(8,128)(2,1)S(1)}, bf16[448,128]{1,0:T(8,128)(2,1)S(1)}, u32[]{:S(2)}, u32[]{:S(2)}) collective-permute-start(bf16[448,128]{1,0:T(8,128)(2,1)S(1)} %get-tuple-element.8.after_ref), channel_id=1, source_target_pairs={{0,256},{256,0},{1,257},{257,1},{2,258},{258,2},{3,259},{259,3},{4... | collective-permute-start | bytes 344072 | tf_op jit(solution)/shard_map/ppermute | solution.py:186
  15.7 24.2 %all-to-all-start = ((bf16[8,2,3200]{2,1,0:T(2,128)(2,1)}), bf16[8,2,3200]{2,1,0:T(2,128)(2,1)S(1)}, u32[]{:S(2)}, u32[]{:S(2)}) async-start(bf16[8,2,3200]{2,1,0:T(2,128)(2,1)} %shard_map.78), calls=%async_computation | async-start | bytes 204800 | tf_op jit(solution)/shard_map/all_to_all | solution.py:232
  24.3 117.6 %all-gather.2.cloned.1.call-start = ((), (), s32[]{:S(2)}) async-start(), calls=%async_computation.2 | async-start | bytes 3481600 | tf_op jit(solution)/shard_map/all_gather | solution.py:243
  24.4 20.4 %collective-permute-start.10 = (bf16[896,128]{1,0:T(8,128)(2,1)S(1)}, bf16[896,128]{1,0:T(8,128)(2,1)S(1)}, u32[]{:S(2)}, u32[]{:S(2)}) collective-permute-start(bf16[896,128]{1,0:T(8,128)(2,1)S(1)} %constant_dynamic-update-slice_fusion.2.refs_0_), channel_id=1, source_target_pairs={{0,240},{16,0},{32,16},{48,32},{64,48},{80,64},{96,80},{112,96},{1... | collective-permute-start | bytes 688136 | tf_op jit(solution)/shard_map/ppermute | solution.py:190
  33.1 16.8 %collective-permute-start.2 = (bf16[896,128]{1,0:T(8,128)(2,1)S(1)}, bf16[896,128]{1,0:T(8,128)(2,1)S(1)}, u32[]{:S(2)}, u32[]{:S(2)}) collective-permute-start(bf16[896,128]{1,0:T(8,128)(2,1)S(1)} %constant_dynamic-update-slice_fusion.2.refs_0_), channel_id=1, source_target_pairs={{0,16},{16,32},{32,48},{48,64},{64,80},{80,96},{96,112},{112,128},... | collective-permute-start | bytes 688136 | tf_op jit(solution)/shard_map/ppermute | solution.py:190
  40.6 11.3 %collective-permute-start.19 = (bf16[8,2,3200]{2,1,0:T(2,128)(2,1)}, bf16[8,2,3200]{2,1,0:T(2,128)(2,1)S(1)}, u32[]{:S(2)}, u32[]{:S(2)}) collective-permute-start(bf16[8,2,3200]{2,1,0:T(2,128)(2,1)} %shard_map.79.mine_ref), channel_id=1, source_target_pairs={{0,256},{256,0},{1,257},{257,1},{2,258},{258,2},{3,259},{259,3},{4... | collective-permute-start | bytes 307208 | tf_op jit(solution)/shard_map/ppermute | solution.py:186
  44.7 12.2 %collective-permute-start.11 = (bf16[896,128]{1,0:T(8,128)(2,1)S(1)}, bf16[896,128]{1,0:T(8,128)(2,1)S(1)}, u32[]{:S(2)}, u32[]{:S(2)}) collective-permute-start(bf16[896,128]{1,0:T(8,128)(2,1)S(1)} %collective-permute-done.10.refs_1_), channel_id=1, source_target_pairs={{0,240},{16,0},{32,16},{48,32},{64,48},{80,64},{96,80},{112,96},{1... | collective-permute-start | bytes 688136 | tf_op jit(solution)/shard_map/ppermute | solution.py:190
  49.9 10.3 %collective-permute-start.3 = (bf16[896,128]{1,0:T(8,128)(2,1)S(1)}, bf16[896,128]{1,0:T(8,128)(2,1)S(1)}, u32[]{:S(2)}, u32[]{:S(2)}) collective-permute-start(bf16[896,128]{1,0:T(8,128)(2,1)S(1)} %collective-permute-done.2.refs_0_), channel_id=1, source_target_pairs={{0,16},{16,32},{32,48},{48,64},{64,80},{80,96},{96,112},{112,128},... | collective-permute-start | bytes 688136 | tf_op jit(solution)/shard_map/ppermute | solution.py:190
  56.9 8.4 %collective-permute-start.12 = (bf16[896,128]{1,0:T(8,128)(2,1)S(1)}, bf16[896,128]{1,0:T(8,128)(2,1)S(1)}, u32[]{:S(2)}, u32[]{:S(2)}) collective-permute-start(bf16[896,128]{1,0:T(8,128)(2,1)S(1)} %collective-permute-done.11.refs_1_), channel_id=1, source_target_pairs={{0,240},{16,0},{32,16},{48,32},{64,48},{80,64},{96,80},{112,96},{1... | collective-permute-start | bytes 688136 | tf_op jit(solution)/shard_map/ppermute | solution.py:190
  60.2 10.7 %collective-permute-start.4 = (bf16[896,128]{1,0:T(8,128)(2,1)S(1)}, bf16[896,128]{1,0:T(8,128)(2,1)S(1)}, u32[]{:S(2)}, u32[]{:S(2)}) collective-permute-start(bf16[896,128]{1,0:T(8,128)(2,1)S(1)} %collective-permute-done.3.refs_0_), channel_id=1, source_target_pairs={{0,16},{16,32},{32,48},{48,64},{64,80},{80,96},{96,112},{112,128},... | collective-permute-start | bytes 688136 | tf_op jit(solution)/shard_map/ppermute | solution.py:190
  65.3 13.8 %collective-permute-start.13 = (bf16[896,128]{1,0:T(8,128)(2,1)S(1)}, bf16[896,128]{1,0:T(8,128)(2,1)S(1)}, u32[]{:S(2)}, u32[]{:S(2)}) collective-permute-start(bf16[896,128]{1,0:T(8,128)(2,1)S(1)} %collective-permute-done.12.refs_1_), channel_id=1, source_target_pairs={{0,240},{16,0},{32,16},{48,32},{64,48},{80,64},{96,80},{112,96},{1... | collective-permute-start | bytes 688136 | tf_op jit(solution)/shard_map/ppermute | solution.py:190
  70.9 14.9 %collective-permute-start.5 = (bf16[896,128]{1,0:T(8,128)(2,1)S(1)}, bf16[896,128]{1,0:T(8,128)(2,1)S(1)}, u32[]{:S(2)}, u32[]{:S(2)}) collective-permute-start(bf16[896,128]{1,0:T(8,128)(2,1)S(1)} %collective-permute-done.4.refs_0_), channel_id=1, source_target_pairs={{0,16},{16,32},{32,48},{48,64},{64,80},{80,96},{96,112},{112,128},... | collective-permute-start | bytes 688136 | tf_op jit(solution)/shard_map/ppermute | solution.py:190
  79.1 14.1 %collective-permute-start.14 = (bf16[896,128]{1,0:T(8,128)(2,1)S(1)}, bf16[896,128]{1,0:T(8,128)(2,1)S(1)}, u32[]{:S(2)}, u32[]{:S(2)}) collective-permute-start(bf16[896,128]{1,0:T(8,128)(2,1)S(1)} %collective-permute-done.13.refs_1_), channel_id=1, source_target_pairs={{0,240},{16,0},{32,16},{48,32},{64,48},{80,64},{96,80},{112,96},{1... | collective-permute-start | bytes 688136 | tf_op jit(solution)/shard_map/ppermute | solution.py:190
  85.8 13.5 %collective-permute-start.6 = (bf16[896,128]{1,0:T(8,128)(2,1)S(1)}, bf16[896,128]{1,0:T(8,128)(2,1)S(1)}, u32[]{:S(2)}, u32[]{:S(2)}) collective-permute-start(bf16[896,128]{1,0:T(8,128)(2,1)S(1)} %collective-permute-done.5.refs_0_), channel_id=1, source_target_pairs={{0,16},{16,32},{32,48},{48,64},{64,80},{80,96},{96,112},{112,128},... | collective-permute-start | bytes 688136 | tf_op jit(solution)/shard_map/ppermute | solution.py:190
  93.2 12.0 %collective-permute-start.15 = (bf16[896,128]{1,0:T(8,128)(2,1)S(1)}, bf16[896,128]{1,0:T(8,128)(2,1)S(1)}, u32[]{:S(2)}, u32[]{:S(2)}) collective-permute-start(bf16[896,128]{1,0:T(8,128)(2,1)S(1)} %collective-permute-done.14.refs_1_), channel_id=1, source_target_pairs={{0,240},{16,0},{32,16},{48,32},{64,48},{80,64},{96,80},{112,96},{1... | collective-permute-start | bytes 688136 | tf_op jit(solution)/shard_map/ppermute | solution.py:190
  99.3 14.2 %collective-permute-start.7 = (bf16[896,128]{1,0:T(8,128)(2,1)S(1)}, bf16[896,128]{1,0:T(8,128)(2,1)S(1)}, u32[]{:S(2)}, u32[]{:S(2)}) collective-permute-start(bf16[896,128]{1,0:T(8,128)(2,1)S(1)} %collective-permute-done.6.refs_0_), channel_id=1, source_target_pairs={{0,16},{16,32},{32,48},{48,64},{64,80},{80,96},{96,112},{112,128},... | collective-permute-start | bytes 688136 | tf_op jit(solution)/shard_map/ppermute | solution.py:190
  105.2 12.8 %collective-permute-start.16 = (bf16[896,128]{1,0:T(8,128)(2,1)S(1)}, bf16[896,128]{1,0:T(8,128)(2,1)S(1)}, u32[]{:S(2)}, u32[]{:S(2)}) collective-permute-start(bf16[896,128]{1,0:T(8,128)(2,1)S(1)} %collective-permute-done.15.refs_1_), channel_id=1, source_target_pairs={{0,240},{16,0},{32,16},{48,32},{64,48},{80,64},{96,80},{112,96},{1... | collective-permute-start | bytes 688136 | tf_op jit(solution)/shard_map/ppermute | solution.py:190
  113.5 13.6 %collective-permute-start.8 = (bf16[896,128]{1,0:T(8,128)(2,1)S(1)}, bf16[896,128]{1,0:T(8,128)(2,1)S(1)}, u32[]{:S(2)}, u32[]{:S(2)}) collective-permute-start(bf16[896,128]{1,0:T(8,128)(2,1)S(1)} %collective-permute-done.7.refs_0_), channel_id=1, source_target_pairs={{0,16},{16,32},{32,48},{48,64},{64,80},{80,96},{96,112},{112,128},... | collective-permute-start | bytes 688136 | tf_op jit(solution)/shard_map/ppermute | solution.py:190
  118.0 11.9 %collective-permute-start.17 = (bf16[448,128]{1,0:T(8,128)(2,1)S(1)}, bf16[448,128]{1,0:T(8,128)(2,1)S(1)}, u32[]{:S(2)}, u32[]{:S(2)}) collective-permute-start(bf16[448,128]{1,0:T(8,128)(2,1)S(1)} %slice.17), channel_id=1, source_target_pairs={{0,240},{16,0},{32,16},{48,32},{64,48},{80,64},{96,80},{112,96},{1... | collective-permute-start | bytes 344072 | tf_op jit(solution)/shard_map/ppermute | solution.py:190
  127.1 7.9 %collective-permute-start.9 = (bf16[448,128]{1,0:T(8,128)(2,1)S(1)}, bf16[448,128]{1,0:T(8,128)(2,1)S(1)}, u32[]{:S(2)}, u32[]{:S(2)}) collective-permute-start(bf16[448,128]{1,0:T(8,128)(2,1)S(1)} %slice.16), channel_id=1, source_target_pairs={{0,16},{16,32},{32,48},{48,64},{64,80},{80,96},{96,112},{112,128},... | collective-permute-start | bytes 344072 | tf_op jit(solution)/shard_map/ppermute | solution.py:190
  136.0 4.0 %collective-permute-start.18 = (f32[656,224]{1,0:T(8,128)S(1)}, f32[656,224]{1,0:T(8,128)S(1)}, u32[]{:S(2)}, u32[]{:S(2)}) collective-permute-start(f32[656,224]{1,0:T(8,128)S(1)} %get-tuple-element.6), channel_id=1, source_target_pairs={{0,8},{8,0},{1,9},{9,1},{2,10},{10,2},{3,11},{11,3},{4,12},{12,4},... | collective-permute-start | bytes 1763336 | tf_op jit(solution)/shard_map/ppermute | solution.py:186
  141.8 36.3 %collective-permute-start.20 = (bf16[128,12800]{1,0:T(8,128)(2,1)}, bf16[128,12800]{1,0:T(8,128)(2,1)S(1)}, u32[]{:S(2)}, u32[]{:S(2)}) collective-permute-start(bf16[128,12800]{1,0:T(8,128)(2,1)} %shard_map.81.own_ref), channel_id=1, source_target_pairs={{0,8},{8,0},{1,9},{9,1},{2,10},{10,2},{3,11},{11,3},{4,12},{12,4},... | collective-permute-start | bytes 9830408 | tf_op jit(solution)/shard_map/ppermute | solution.py:186
  144.2 34.0 %copy-start = (bf16[128,12800]{1,0:T(8,128)(2,1)S(1)}, bf16[128,12800]{1,0:T(8,128)(2,1)}, u32[]{:S(2)}) copy-start(bf16[128,12800]{1,0:T(8,128)(2,1)} %shard_map.81.own_ref) | copy-start | bytes 9830404
  (8 other events, 51.4 us)
Sparse Core Ops, SparseCore 0:
  54.4 78.6 all-gather.1

commit v6 on v5

--- a/solution.py
+++ b/solution.py
@@ -268,7 +268,7 @@
     sent, kept = jnp.where(core == 0, high, low), jnp.where(core == 0, low, high)
     attended, a = merge(kept, swap(sent, "core"))
 
-    weight = behind(weight, a)
+    weight = behind(weight, state)
     sources = lax.all_to_all(jnp.broadcast_to(a[None], (NY * NX, ROWS, WIDE)), "tp", 0, 0)
     projected = project(here, (weight, swap(weight, "core")), sources)
     return (attended, projected)

time: 192 us -> 204 us (1.062)
  the two profiles are of different devices: /device:TPU:6 before, /device:TPU:1 now
where the time goes in v6:
time: 204 us; the launch traced here: 203 us
  starting transfers between devices  98.3 us (48%)
  blocking collectives  32.8 us (16%)
  waiting for transfers between devices  31.5 us (15%)
  Pallas kernels  19.1 us (9%)
  between operations  14.4 us (7%)
  local copies, waits for them, and re-layouts  5.36 us (3%)
    ppermute x16, starting transfers between devices, ring(): return lax.ppermute(value, 'z', [(i, (i + steps) % NZ) for i in range(NZ)])  66.1 us
    all_to_all x1, blocking collectives, body(): lax.all_to_all(jnp.broadcast_to(a[None], (NY * NX, ROWS, WIDE)), 'tp', 0, 0)  32.8 us
    ppermute x5, starting transfers between devices, swap(): return lax.ppermute(value, axis, [(0, 1), (1, 0)])  28.8 us
    ppermute x16, waiting for transfers between devices, ring(): return lax.ppermute(value, 'z', [(i, (i + steps) % NZ) for i in range(NZ)])  23 us
    pallas_call x9, Pallas kernels, attend(): pl.pallas_call(functools.partial(attend_kernel, visits, state is None), o...  9.23 us
    ppermute x5, waiting for transfers between devices, swap(): return lax.ppermute(value, axis, [(0, 1), (1, 0)])  8.47 us
    pallas_call x1, Pallas kernels, project(): pl.pallas_call(project_kernel, out_shape=jax.ShapeDtypeStruct((ROWS, WIDE...  5.5 us
    unnamed x19, local copies, waits for them, and re-layouts  4.31 us
  transfers between devices with their start and end apart: 23, of which 13 were waited for; matrix products, arithmetic and copies ran while one was open for 2% of the time, Pallas kernels for 6%

profile of v6, /device:TPU:1, one launch (start us, length us, event | category | flops | bytes accessed | tf_op | source)
XLA Modules:
  0.0 203.0 jit_solution(10069598310156931666)
XLA Ops:
  7.2 8.8 %collective-permute-start = (bf16[224,640]{1,0:T(8,128)(2,1)}, bf16[224,640]{1,0:T(8,128)(2,1)S(1)}, u32[]{:S(2)}, u32[]{:S(2)}) collective-permute-start(bf16[224,640]{1,0:T(8,128)(2,1)} %param.5), channel_id=1, source_target_pairs={{0,8},{8,0},{1,9},{9,1},{2,10},{10,2},{3,11},{11,3},{4,12},{12,4},... | collective-permute-start | bytes 860168 | tf_op jit(solution)/shard_map/ppermute | solution.py:186
  17.7 1.9 collective-permute-start.1
  21.2 3.4 %all-to-all-start = ((bf16[8,2,3200]{2,1,0:T(2,128)(2,1)}), bf16[8,2,3200]{2,1,0:T(2,128)(2,1)S(1)}, u32[]{:S(2)}, u32[]{:S(2)}) async-start(bf16[8,2,3200]{2,1,0:T(2,128)(2,1)} %shard_map.78), calls=%async_computation | async-start | bytes 204800 | tf_op jit(solution)/shard_map/all_to_all | solution.py:232
  27.1 2.5 %shard_map.68.refs_2_.refs_1_ = f32[656,448]{1,0:T(8,128)S(1)} custom-call(s32[3]{0:T(128)S(1)} %pad_add_fusion.here_ref, s32[16]{0:T(128)S(1)} %copy-done.5, bf16[448,640]{1,0:T(8,128)(2,1)S(1)} %maximum_select_fusion.q_ref, bf16[896,128]{1,0:T(8,128)(2,1)S(1)} %constant_dynamic-update-slice_fusion.2.refs_0_), custom_call_target="tpu_custom_call" | custom-call | flops 4110417920 | bytes 18808832 | tf_op jit(solution)/shard_map/pallas_call | solution.py:101
  31.4 4.2 %collective-permute-start.19 = (bf16[8,2,3200]{2,1,0:T(2,128)(2,1)}, bf16[8,2,3200]{2,1,0:T(2,128)(2,1)S(1)}, u32[]{:S(2)}, u32[]{:S(2)}) collective-permute-start(bf16[8,2,3200]{2,1,0:T(2,128)(2,1)} %shard_map.79.mine_ref), channel_id=1, source_target_pairs={{0,256},{256,0},{1,257},{257,1},{2,258},{258,2},{3,259},{259,3},{4... | collective-permute-start | bytes 307208 | tf_op jit(solution)/shard_map/ppermute | solution.py:186
  35.5 3.1 %collective-permute-done.19.other_ref = bf16[8,2,3200]{2,1,0:T(2,128)(2,1)S(1)} collective-permute-done((bf16[8,2,3200]{2,1,0:T(2,128)(2,1)}, bf16[8,2,3200]{2,1,0:T(2,128)(2,1)S(1)}, u32[]{:S(2)}, u32[]{:S(2)}) %collective-permute-start.19) | collective-permute-done | bytes 102432 | tf_op jit(solution)/shard_map/ppermute | solution.py:186
  41.0 8.6 %collective-permute-start.10 = (bf16[896,128]{1,0:T(8,128)(2,1)S(1)}, bf16[896,128]{1,0:T(8,128)(2,1)S(1)}, u32[]{:S(2)}, u32[]{:S(2)}) collective-permute-start(bf16[896,128]{1,0:T(8,128)(2,1)S(1)} %constant_dynamic-update-slice_fusion.2.refs_0_), channel_id=1, source_target_pairs={{0,240},{16,0},{32,16},{48,32},{64,48},{80,64},{96,80},{112,96},{1... | collective-permute-start | bytes 688136 | tf_op jit(solution)/shard_map/ppermute | solution.py:190
  49.6 1.9 collective-permute-start.2
  52.5 5.0 %collective-permute-start.11 = (bf16[896,128]{1,0:T(8,128)(2,1)S(1)}, bf16[896,128]{1,0:T(8,128)(2,1)S(1)}, u32[]{:S(2)}, u32[]{:S(2)}) collective-permute-start(bf16[896,128]{1,0:T(8,128)(2,1)S(1)} %collective-permute-done.10.refs_1_), channel_id=1, source_target_pairs={{0,240},{16,0},{32,16},{48,32},{64,48},{80,64},{96,80},{112,96},{1... | collective-permute-start | bytes 688136 | tf_op jit(solution)/shard_map/ppermute | solution.py:190
  62.0 6.6 %collective-permute-start.12 = (bf16[896,128]{1,0:T(8,128)(2,1)S(1)}, bf16[896,128]{1,0:T(8,128)(2,1)S(1)}, u32[]{:S(2)}, u32[]{:S(2)}) collective-permute-start(bf16[896,128]{1,0:T(8,128)(2,1)S(1)} %collective-permute-done.11.refs_1_), channel_id=1, source_target_pairs={{0,240},{16,0},{32,16},{48,32},{64,48},{80,64},{96,80},{112,96},{1... | collective-permute-start | bytes 688136 | tf_op jit(solution)/shard_map/ppermute | solution.py:190
  74.0 6.7 %collective-permute-start.13 = (bf16[896,128]{1,0:T(8,128)(2,1)S(1)}, bf16[896,128]{1,0:T(8,128)(2,1)S(1)}, u32[]{:S(2)}, u32[]{:S(2)}) collective-permute-start(bf16[896,128]{1,0:T(8,128)(2,1)S(1)} %collective-permute-done.12.refs_1_), channel_id=1, source_target_pairs={{0,240},{16,0},{32,16},{48,32},{64,48},{80,64},{96,80},{112,96},{1... | collective-permute-start | bytes 688136 | tf_op jit(solution)/shard_map/ppermute | solution.py:190
  80.7 1.9 collective-permute-start.5
  83.7 2.5 %collective-permute-done.13.refs_1_ = bf16[896,128]{1,0:T(8,128)(2,1)S(1)} collective-permute-done((bf16[896,128]{1,0:T(8,128)(2,1)S(1)}, bf16[896,128]{1,0:T(8,128)(2,1)S(1)}, u32[]{:S(2)}, u32[]{:S(2)}) %collective-permute-start.13) | collective-permute-done | bytes 229408 | tf_op jit(solution)/shard_map/ppermute | solution.py:190
  86.2 5.8 %collective-permute-start.14 = (bf16[896,128]{1,0:T(8,128)(2,1)S(1)}, bf16[896,128]{1,0:T(8,128)(2,1)S(1)}, u32[]{:S(2)}, u32[]{:S(2)}) collective-permute-start(bf16[896,128]{1,0:T(8,128)(2,1)S(1)} %collective-permute-done.13.refs_1_), channel_id=1, source_target_pairs={{0,240},{16,0},{32,16},{48,32},{64,48},{80,64},{96,80},{112,96},{1... | collective-permute-start | bytes 688136 | tf_op jit(solution)/shard_map/ppermute | solution.py:190
  94.7 4.4 %collective-permute-done.14.refs_1_ = bf16[896,128]{1,0:T(8,128)(2,1)S(1)} collective-permute-done((bf16[896,128]{1,0:T(8,128)(2,1)S(1)}, bf16[896,128]{1,0:T(8,128)(2,1)S(1)}, u32[]{:S(2)}, u32[]{:S(2)}) %collective-permute-start.14) | collective-permute-done | bytes 229408 | tf_op jit(solution)/shard_map/ppermute | solution.py:190
  99.1 5.3 %collective-permute-start.15 = (bf16[896,128]{1,0:T(8,128)(2,1)S(1)}, bf16[896,128]{1,0:T(8,128)(2,1)S(1)}, u32[]{:S(2)}, u32[]{:S(2)}) collective-permute-start(bf16[896,128]{1,0:T(8,128)(2,1)S(1)} %collective-permute-done.14.refs_1_), channel_id=1, source_target_pairs={{0,240},{16,0},{32,16},{48,32},{64,48},{80,64},{96,80},{112,96},{1... | collective-permute-start | bytes 688136 | tf_op jit(solution)/shard_map/ppermute | solution.py:190
  107.2 4.8 %collective-permute-done.15.refs_1_ = bf16[896,128]{1,0:T(8,128)(2,1)S(1)} collective-permute-done((bf16[896,128]{1,0:T(8,128)(2,1)S(1)}, bf16[896,128]{1,0:T(8,128)(2,1)S(1)}, u32[]{:S(2)}, u32[]{:S(2)}) %collective-permute-start.15) | collective-permute-done | bytes 229408 | tf_op jit(solution)/shard_map/ppermute | solution.py:190
  112.0 5.4 %collective-permute-start.16 = (bf16[896,128]{1,0:T(8,128)(2,1)S(1)}, bf16[896,128]{1,0:T(8,128)(2,1)S(1)}, u32[]{:S(2)}, u32[]{:S(2)}) collective-permute-start(bf16[896,128]{1,0:T(8,128)(2,1)S(1)} %collective-permute-done.15.refs_1_), channel_id=1, source_target_pairs={{0,240},{16,0},{32,16},{48,32},{64,48},{80,64},{96,80},{112,96},{1... | collective-permute-start | bytes 688136 | tf_op jit(solution)/shard_map/ppermute | solution.py:190
  122.1 7.4 %collective-permute-start.17 = (bf16[448,128]{1,0:T(8,128)(2,1)S(1)}, bf16[448,128]{1,0:T(8,128)(2,1)S(1)}, u32[]{:S(2)}, u32[]{:S(2)}) collective-permute-start(bf16[448,128]{1,0:T(8,128)(2,1)S(1)} %slice.17), channel_id=1, source_target_pairs={{0,240},{16,0},{32,16},{48,32},{64,48},{80,64},{96,80},{112,96},{1... | collective-permute-start | bytes 344072 | tf_op jit(solution)/shard_map/ppermute | solution.py:190
  132.3 4.0 %collective-permute-done.9.refs_0_ = bf16[448,128]{1,0:T(8,128)(2,1)S(1)} collective-permute-done((bf16[448,128]{1,0:T(8,128)(2,1)S(1)}, bf16[448,128]{1,0:T(8,128)(2,1)S(1)}, u32[]{:S(2)}, u32[]{:S(2)}) %collective-permute-start.9) | collective-permute-done | bytes 114720 | tf_op jit(solution)/shard_map/ppermute | solution.py:190
  138.2 12.0 %collective-permute-start.20 = (bf16[128,12800]{1,0:T(8,128)(2,1)}, bf16[128,12800]{1,0:T(8,128)(2,1)S(1)}, u32[]{:S(2)}, u32[]{:S(2)}) collective-permute-start(bf16[128,12800]{1,0:T(8,128)(2,1)} %shard_map.81.own_ref), channel_id=1, source_target_pairs={{0,8},{8,0},{1,9},{9,1},{2,10},{10,2},{3,11},{11,3},{4,12},{12,4},... | collective-permute-start | bytes 9830408 | tf_op jit(solution)/shard_map/ppermute | solution.py:186
  152.4 4.2 %collective-permute-done.18.other_ref = f32[656,224]{1,0:T(8,128)S(1)} collective-permute-done((f32[656,224]{1,0:T(8,128)S(1)}, f32[656,224]{1,0:T(8,128)S(1)}, u32[]{:S(2)}, u32[]{:S(2)}) %collective-permute-start.18) | collective-permute-done | bytes 587808 | tf_op jit(solution)/shard_map/ppermute | solution.py:186
  157.8 32.8 %all_to_all.10.a_ref = bf16[8,224,640]{2,1,0:T(8,128)(2,1)S(1)} all-to-all(bf16[8,224,640]{2,1,0:T(8,128)(2,1)S(1)} %broadcast_in_dim.2), channel_id=1, replica_groups=mesh['xh'=2,'z'=16,'core'=2,'tp'=8] {'tp'}, dimensions={0} | all-to-all | bytes 4587520 | tf_op jit(solution)/shard_map/all_to_all | solution.py:272
  190.7 5.5 %shard_map.82 = f32[224,640]{1,0:T(8,128)} custom-call(s32[3]{0:T(128)S(1)} %pad_add_fusion.here_ref, bf16[128,12800]{1,0:T(8,128)(2,1)S(1)} %copy-done, bf16[128,12800]{1,0:T(8,128)(2,1)S(1)} %collective-permute-done.20.other_ref, bf16[8,224,640]{2,1,0:T(8,128)(2,1)S(1)} %all_to_all.10.a_ref), custom_call_target="tpu_custom_call" | custom-call | flops 2055208960 | bytes 6553600 | tf_op jit(solution)/shard_map/pallas_call | solution.py:171
  (66 shorter events, 39.8 us)
Async XLA Ops:
  7.2 18.7 %collective-permute-start = (bf16[224,640]{1,0:T(8,128)(2,1)}, bf16[224,640]{1,0:T(8,128)(2,1)S(1)}, u32[]{:S(2)}, u32[]{:S(2)}) collective-permute-start(bf16[224,640]{1,0:T(8,128)(2,1)} %param.5), channel_id=1, source_target_pairs={{0,8},{8,0},{1,9},{9,1},{2,10},{10,2},{3,11},{11,3},{4,12},{12,4},... | collective-permute-start | bytes 860168 | tf_op jit(solution)/shard_map/ppermute | solution.py:186
  17.7 8.2 %collective-permute-start.1 = (bf16[448,128]{1,0:T(8,128)(2,1)S(1)}, bf16[448,128]{1,0:T(8,128)(2,1)S(1)}, u32[]{:S(2)}, u32[]{:S(2)}) collective-permute-start(bf16[448,128]{1,0:T(8,128)(2,1)S(1)} %get-tuple-element.8.after_ref), channel_id=1, source_target_pairs={{0,256},{256,0},{1,257},{257,1},{2,258},{258,2},{3,259},{259,3},{4... | collective-permute-start | bytes 344072 | tf_op jit(solution)/shard_map/ppermute | solution.py:186
  21.2 9.6 %all-to-all-start = ((bf16[8,2,3200]{2,1,0:T(2,128)(2,1)}), bf16[8,2,3200]{2,1,0:T(2,128)(2,1)S(1)}, u32[]{:S(2)}, u32[]{:S(2)}) async-start(bf16[8,2,3200]{2,1,0:T(2,128)(2,1)} %shard_map.78), calls=%async_computation | async-start | bytes 204800 | tf_op jit(solution)/shard_map/all_to_all | solution.py:232
  24.5 113.7 %all-gather.2.cloned.1.call-start = ((), (), s32[]{:S(2)}) async-start(), calls=%async_computation.2 | async-start | bytes 3481600 | tf_op jit(solution)/shard_map/all_gather | solution.py:243
  31.4 7.2 %collective-permute-start.19 = (bf16[8,2,3200]{2,1,0:T(2,128)(2,1)}, bf16[8,2,3200]{2,1,0:T(2,128)(2,1)S(1)}, u32[]{:S(2)}, u32[]{:S(2)}) collective-permute-start(bf16[8,2,3200]{2,1,0:T(2,128)(2,1)} %shard_map.79.mine_ref), channel_id=1, source_target_pairs={{0,256},{256,0},{1,257},{257,1},{2,258},{258,2},{3,259},{259,3},{4... | collective-permute-start | bytes 307208 | tf_op jit(solution)/shard_map/ppermute | solution.py:186
  41.0 11.5 %collective-permute-start.10 = (bf16[896,128]{1,0:T(8,128)(2,1)S(1)}, bf16[896,128]{1,0:T(8,128)(2,1)S(1)}, u32[]{:S(2)}, u32[]{:S(2)}) collective-permute-start(bf16[896,128]{1,0:T(8,128)(2,1)S(1)} %constant_dynamic-update-slice_fusion.2.refs_0_), channel_id=1, source_target_pairs={{0,240},{16,0},{32,16},{48,32},{64,48},{80,64},{96,80},{112,96},{1... | collective-permute-start | bytes 688136 | tf_op jit(solution)/shard_map/ppermute | solution.py:190
  49.6 8.0 %collective-permute-start.2 = (bf16[896,128]{1,0:T(8,128)(2,1)S(1)}, bf16[896,128]{1,0:T(8,128)(2,1)S(1)}, u32[]{:S(2)}, u32[]{:S(2)}) collective-permute-start(bf16[896,128]{1,0:T(8,128)(2,1)S(1)} %constant_dynamic-update-slice_fusion.2.refs_0_), channel_id=1, source_target_pairs={{0,16},{16,32},{32,48},{48,64},{64,80},{80,96},{96,112},{112,128},... | collective-permute-start | bytes 688136 | tf_op jit(solution)/shard_map/ppermute | solution.py:190
  52.5 9.5 %collective-permute-start.11 = (bf16[896,128]{1,0:T(8,128)(2,1)S(1)}, bf16[896,128]{1,0:T(8,128)(2,1)S(1)}, u32[]{:S(2)}, u32[]{:S(2)}) collective-permute-start(bf16[896,128]{1,0:T(8,128)(2,1)S(1)} %collective-permute-done.10.refs_1_), channel_id=1, source_target_pairs={{0,240},{16,0},{32,16},{48,32},{64,48},{80,64},{96,80},{112,96},{1... | collective-permute-start | bytes 688136 | tf_op jit(solution)/shard_map/ppermute | solution.py:190
  57.5 12.2 %collective-permute-start.3 = (bf16[896,128]{1,0:T(8,128)(2,1)S(1)}, bf16[896,128]{1,0:T(8,128)(2,1)S(1)}, u32[]{:S(2)}, u32[]{:S(2)}) collective-permute-start(bf16[896,128]{1,0:T(8,128)(2,1)S(1)} %collective-permute-done.2.refs_0_), channel_id=1, source_target_pairs={{0,16},{16,32},{32,48},{48,64},{64,80},{80,96},{96,112},{112,128},... | collective-permute-start | bytes 688136 | tf_op jit(solution)/shard_map/ppermute | solution.py:190
  62.0 12.0 %collective-permute-start.12 = (bf16[896,128]{1,0:T(8,128)(2,1)S(1)}, bf16[896,128]{1,0:T(8,128)(2,1)S(1)}, u32[]{:S(2)}, u32[]{:S(2)}) collective-permute-start(bf16[896,128]{1,0:T(8,128)(2,1)S(1)} %collective-permute-done.11.refs_1_), channel_id=1, source_target_pairs={{0,240},{16,0},{32,16},{48,32},{64,48},{80,64},{96,80},{112,96},{1... | collective-permute-start | bytes 688136 | tf_op jit(solution)/shard_map/ppermute | solution.py:190
  69.7 11.0 %collective-permute-start.4 = (bf16[896,128]{1,0:T(8,128)(2,1)S(1)}, bf16[896,128]{1,0:T(8,128)(2,1)S(1)}, u32[]{:S(2)}, u32[]{:S(2)}) collective-permute-start(bf16[896,128]{1,0:T(8,128)(2,1)S(1)} %collective-permute-done.3.refs_0_), channel_id=1, source_target_pairs={{0,16},{16,32},{32,48},{48,64},{64,80},{80,96},{96,112},{112,128},... | collective-permute-start | bytes 688136 | tf_op jit(solution)/shard_map/ppermute | solution.py:190
  74.0 12.2 %collective-permute-start.13 = (bf16[896,128]{1,0:T(8,128)(2,1)S(1)}, bf16[896,128]{1,0:T(8,128)(2,1)S(1)}, u32[]{:S(2)}, u32[]{:S(2)}) collective-permute-start(bf16[896,128]{1,0:T(8,128)(2,1)S(1)} %collective-permute-done.12.refs_1_), channel_id=1, source_target_pairs={{0,240},{16,0},{32,16},{48,32},{64,48},{80,64},{96,80},{112,96},{1... | collective-permute-start | bytes 688136 | tf_op jit(solution)/shard_map/ppermute | solution.py:190
  80.7 11.2 %collective-permute-start.5 = (bf16[896,128]{1,0:T(8,128)(2,1)S(1)}, bf16[896,128]{1,0:T(8,128)(2,1)S(1)}, u32[]{:S(2)}, u32[]{:S(2)}) collective-permute-start(bf16[896,128]{1,0:T(8,128)(2,1)S(1)} %collective-permute-done.4.refs_0_), channel_id=1, source_target_pairs={{0,16},{16,32},{32,48},{48,64},{64,80},{80,96},{96,112},{112,128},... | collective-permute-start | bytes 688136 | tf_op jit(solution)/shard_map/ppermute | solution.py:190
  86.2 12.9 %collective-permute-start.14 = (bf16[896,128]{1,0:T(8,128)(2,1)S(1)}, bf16[896,128]{1,0:T(8,128)(2,1)S(1)}, u32[]{:S(2)}, u32[]{:S(2)}) collective-permute-start(bf16[896,128]{1,0:T(8,128)(2,1)S(1)} %collective-permute-done.13.refs_1_), channel_id=1, source_target_pairs={{0,240},{16,0},{32,16},{48,32},{64,48},{80,64},{96,80},{112,96},{1... | collective-permute-start | bytes 688136 | tf_op jit(solution)/shard_map/ppermute | solution.py:190
  92.0 12.5 %collective-permute-start.6 = (bf16[896,128]{1,0:T(8,128)(2,1)S(1)}, bf16[896,128]{1,0:T(8,128)(2,1)S(1)}, u32[]{:S(2)}, u32[]{:S(2)}) collective-permute-start(bf16[896,128]{1,0:T(8,128)(2,1)S(1)} %collective-permute-done.5.refs_0_), channel_id=1, source_target_pairs={{0,16},{16,32},{32,48},{48,64},{64,80},{80,96},{96,112},{112,128},... | collective-permute-start | bytes 688136 | tf_op jit(solution)/shard_map/ppermute | solution.py:190
  99.1 12.9 %collective-permute-start.15 = (bf16[896,128]{1,0:T(8,128)(2,1)S(1)}, bf16[896,128]{1,0:T(8,128)(2,1)S(1)}, u32[]{:S(2)}, u32[]{:S(2)}) collective-permute-start(bf16[896,128]{1,0:T(8,128)(2,1)S(1)} %collective-permute-done.14.refs_1_), channel_id=1, source_target_pairs={{0,240},{16,0},{32,16},{48,32},{64,48},{80,64},{96,80},{112,96},{1... | collective-permute-start | bytes 688136 | tf_op jit(solution)/shard_map/ppermute | solution.py:190
  104.5 13.8 %collective-permute-start.7 = (bf16[896,128]{1,0:T(8,128)(2,1)S(1)}, bf16[896,128]{1,0:T(8,128)(2,1)S(1)}, u32[]{:S(2)}, u32[]{:S(2)}) collective-permute-start(bf16[896,128]{1,0:T(8,128)(2,1)S(1)} %collective-permute-done.6.refs_0_), channel_id=1, source_target_pairs={{0,16},{16,32},{32,48},{48,64},{64,80},{80,96},{96,112},{112,128},... | collective-permute-start | bytes 688136 | tf_op jit(solution)/shard_map/ppermute | solution.py:190
  112.0 10.1 %collective-permute-start.16 = (bf16[896,128]{1,0:T(8,128)(2,1)S(1)}, bf16[896,128]{1,0:T(8,128)(2,1)S(1)}, u32[]{:S(2)}, u32[]{:S(2)}) collective-permute-start(bf16[896,128]{1,0:T(8,128)(2,1)S(1)} %collective-permute-done.15.refs_1_), channel_id=1, source_target_pairs={{0,240},{16,0},{32,16},{48,32},{64,48},{80,64},{96,80},{112,96},{1... | collective-permute-start | bytes 688136 | tf_op jit(solution)/shard_map/ppermute | solution.py:190
  118.3 11.3 %collective-permute-start.8 = (bf16[896,128]{1,0:T(8,128)(2,1)S(1)}, bf16[896,128]{1,0:T(8,128)(2,1)S(1)}, u32[]{:S(2)}, u32[]{:S(2)}) collective-permute-start(bf16[896,128]{1,0:T(8,128)(2,1)S(1)} %collective-permute-done.7.refs_0_), channel_id=1, source_target_pairs={{0,16},{16,32},{32,48},{48,64},{64,80},{80,96},{96,112},{112,128},... | collective-permute-start | bytes 688136 | tf_op jit(solution)/shard_map/ppermute | solution.py:190
  122.1 10.2 %collective-permute-start.17 = (bf16[448,128]{1,0:T(8,128)(2,1)S(1)}, bf16[448,128]{1,0:T(8,128)(2,1)S(1)}, u32[]{:S(2)}, u32[]{:S(2)}) collective-permute-start(bf16[448,128]{1,0:T(8,128)(2,1)S(1)} %slice.17), channel_id=1, source_target_pairs={{0,240},{16,0},{32,16},{48,32},{64,48},{80,64},{96,80},{112,96},{1... | collective-permute-start | bytes 344072 | tf_op jit(solution)/shard_map/ppermute | solution.py:190
  129.6 6.7 %collective-permute-start.9 = (bf16[448,128]{1,0:T(8,128)(2,1)S(1)}, bf16[448,128]{1,0:T(8,128)(2,1)S(1)}, u32[]{:S(2)}, u32[]{:S(2)}) collective-permute-start(bf16[448,128]{1,0:T(8,128)(2,1)S(1)} %slice.16), channel_id=1, source_target_pairs={{0,16},{16,32},{32,48},{48,64},{64,80},{80,96},{96,112},{112,128},... | collective-permute-start | bytes 344072 | tf_op jit(solution)/shard_map/ppermute | solution.py:190
  138.2 52.5 %collective-permute-start.20 = (bf16[128,12800]{1,0:T(8,128)(2,1)}, bf16[128,12800]{1,0:T(8,128)(2,1)S(1)}, u32[]{:S(2)}, u32[]{:S(2)}) collective-permute-start(bf16[128,12800]{1,0:T(8,128)(2,1)} %shard_map.81.own_ref), channel_id=1, source_target_pairs={{0,8},{8,0},{1,9},{9,1},{2,10},{10,2},{3,11},{11,3},{4,12},{12,4},... | collective-permute-start | bytes 9830408 | tf_op jit(solution)/shard_map/ppermute | solution.py:186
  150.4 6.2 %collective-permute-start.18 = (f32[656,224]{1,0:T(8,128)S(1)}, f32[656,224]{1,0:T(8,128)S(1)}, u32[]{:S(2)}, u32[]{:S(2)}) collective-permute-start(f32[656,224]{1,0:T(8,128)S(1)} %get-tuple-element.6), channel_id=1, source_target_pairs={{0,8},{8,0},{1,9},{9,1},{2,10},{10,2},{3,11},{11,3},{4,12},{12,4},... | collective-permute-start | bytes 1763336 | tf_op jit(solution)/shard_map/ppermute | solution.py:186
  157.8 32.8 %copy-start = (bf16[128,12800]{1,0:T(8,128)(2,1)S(1)}, bf16[128,12800]{1,0:T(8,128)(2,1)}, u32[]{:S(2)}) copy-start(bf16[128,12800]{1,0:T(8,128)(2,1)} %shard_map.81.own_ref) | copy-start | bytes 9830404
  (8 other events, 65.4 us)
Sparse Core Ops, SparseCore 0:
  41.1 78.5 all-gather.1
